TPU v7x, 512 devices: a whole 4x4x16 slice. The times are simulated.
512 devices in a mesh: view: 64 (over x_lo, z, core), strip: 8 (over y, x_hi).
Axes of the slice: x: 4 (x_hi: 2, x_lo: 2; x = x_hi * 2 + x_lo), y: 4, z: 16, core: 2. Of those that a mesh axis runs over, the one named last changes fastest.
Arguments:
- slab: bfloat16 [64, 2, 128, 1024], P('view', None, None, 'strip'), may hold values from -6 to 6
- psi_start: float32 [64, 2, 128, 1024], P('view', None, None, 'strip'), may hold values from -6 to 6
- dual: float32 [64, 2, 128, 1024], P('view', None, None, 'strip'), may hold values from -3 to 3
- amplitudes: float32 [64, 32, 128, 128], P('view', 'strip'), may hold values from 0.2 to 3
- offsets: int32 [64, 32], P('view', 'strip'), may hold values from 0 to 127
- angles: int32 [64], replicated, may hold values from 0 to 32
- probe: float32 [2, 128, 128], replicated, may hold values from -6 to 6
Outputs:
- psi_out: float32 [64, 2, 128, 1024], P('view', None, None, 'strip')
- slab_out: bfloat16 [64, 2, 128, 1024], P('view', None, None, 'strip')
Inputs may be any that keep to these rules, and one draw needn't show every extreme that they name: offsets lie inside the strip of their position.
All inputs are finite; a program needn't handle non-finite values.
Results may differ from a plain program's by a relative error of at most 0.0047.
Values may be sent and summed in bfloat16 or wider, within the bound.
No kernel may reach another device: no remote copies, remote signals or barrier semaphores. Data moves between devices by JAX's collectives and lax.ppermute only.
A program may use at most 64 MiB of HBM per device.

v0:
```python
import math

import jax
import jax.numpy as jnp
from jax import lax
from jax.sharding import PartitionSpec as P

HALO = 16
ITERS = 2


coupling = 0.5
descent = 0.5
highest = lax.Precision.HIGHEST


def with_halo(shard, sides, width):
    for axis, dim in sides:
        size, length = (lax.axis_size(axis), shard.shape[dim])
        up = [(i, (i + 1) % size) for i in range(size - 1)]
        down = [(j, i) for i, j in up]
        last = lax.slice_in_dim(shard, length - width, length, axis=dim)
        initial = lax.slice_in_dim(shard, 0, width, axis=dim)
        before = lax.ppermute(last, axis, up)
        after = lax.ppermute(initial, axis, down)
        shard = jnp.concatenate([before, shard, after], axis=dim)
    return shard


def from_behind(shard, axis, by):
    length = lax.axis_size(axis)
    pairs = [(i, i + by) for i in range(length) if 0 <= i + by < length]
    return lax.ppermute(shard, axis, pairs)


def dft_tables(length):
    counter = jnp.arange(length, dtype=jnp.int32)
    phase = counter[:, None] * counter[None, :] % length
    angle_table = phase.astype(jnp.float32) * (2.0 * math.pi / length)
    norm_factor = 1.0 / math.sqrt(length)
    return (jnp.cos(angle_table) * norm_factor, jnp.sin(angle_table) * norm_factor)


def transform(real_in, imag_in, cosine, sine, forward):
    left_real = jnp.einsum(
        "ij,pjk->pik", cosine, real_in, precision=highest
    ) + forward * jnp.einsum("ij,pjk->pik", sine, imag_in, precision=highest)
    left_imag = jnp.einsum(
        "ij,pjk->pik", cosine, imag_in, precision=highest
    ) - forward * jnp.einsum("ij,pjk->pik", sine, real_in, precision=highest)
    out_real = jnp.einsum(
        "pij,jk->pik", left_real, cosine, precision=highest
    ) + forward * jnp.einsum("pij,jk->pik", left_imag, sine, precision=highest)
    out_imag = jnp.einsum(
        "pij,jk->pik", left_imag, cosine, precision=highest
    ) - forward * jnp.einsum("pij,jk->pik", left_real, sine, precision=highest)
    return (out_real, out_imag)


def shear_shift(tilt, depth, count):
    return tilt * (2 * depth - count + 1) // count


def per_device(slab, psi_start, dual, amplitudes, offsets, angles, probe):
    slices = lax.axis_size("view")
    own_place = lax.axis_index("view")
    width = slab.shape[3]
    rows = slab.shape[2]
    patch = probe.shape[1]
    root_scale = 1.0 / math.sqrt(slices)
    own_tilt = lax.dynamic_index_in_dim(angles, own_place, 0, keepdims=False) - HALO
    empty = jnp.zeros((2, rows, width), jnp.float32)
    slab_all = lax.all_gather(slab, "view", axis=0, tiled=True)
    slab_wide = with_halo(slab_all, (("strip", 3),), HALO)

    def one_slice(position, carry):
        layer = lax.dynamic_index_in_dim(slab_wide, position, 0, keepdims=False)
        offset = HALO + shear_shift(own_tilt, 0 + position, slices)
        return carry + lax.dynamic_slice_in_dim(layer, offset, width, 2).astype(jnp.float32)

    projected = lax.fori_loop(0, slab_wide.shape[0], one_slice, empty)
    projected = projected * root_scale
    object_now = psi_start[0]
    own_dual = dual[0]
    cosine, sine = dft_tables(patch)
    probe_real = probe[0]
    probe_imag = probe[1]
    starts = offsets[0]
    measured = amplitudes[0]
    columns = jnp.arange(2 * width, dtype=jnp.int32)
    placement = (
        columns[None, None, :]
        == starts[:, None, None] + jnp.arange(patch, dtype=jnp.int32)[None, :, None]
    ).astype(jnp.float32)
    step_size = 1.0 / starts.shape[0]
    for sweep in range(ITERS):
        neighbour = from_behind(object_now, "strip", -1)
        extended = jnp.concatenate([object_now, neighbour], axis=2)
        patches = jax.vmap(lambda begin: lax.dynamic_slice_in_dim(extended, begin, patch, 2))(
            starts
        )
        patch_real = patches[:, 0]
        patch_imag = patches[:, 1]
        exit_real = probe_real * patch_real - probe_imag * patch_imag
        exit_imag = probe_real * patch_imag + probe_imag * patch_real
        far_real, far_imag = transform(exit_real, exit_imag, cosine, sine, 1.0)
        factor = measured / jnp.sqrt(far_real * far_real + far_imag * far_imag + 1.0)
        back_real, back_imag = transform(far_real * factor, far_imag * factor, cosine, sine, -1.0)
        delta_real = back_real - exit_real
        delta_imag = back_imag - exit_imag
        grad_real = probe_real * delta_real + probe_imag * delta_imag
        grad_imag = probe_real * delta_imag - probe_imag * delta_real
        gradient = jnp.stack([grad_real, grad_imag], axis=1)
        spread = jnp.einsum("pkhi,pic->khc", gradient, placement, precision=highest)
        spill = from_behind(spread[:, :, width:], "strip", 1)
        object_now = (
            object_now
            + step_size * (spread[:, :, :width] + spill)
            + coupling * (projected - own_dual - object_now)
        )
    residual = (projected - object_now - own_dual).astype(jnp.bfloat16)[None]
    residual_all = lax.all_gather(residual, "view", axis=0, tiled=True)
    residual_wide = with_halo(residual_all, (("strip", 3),), HALO)

    def one_view(position, carry):
        layer = lax.dynamic_index_in_dim(residual_wide, position, 0, keepdims=False)
        tilt = lax.dynamic_index_in_dim(angles, 0 + position, 0, keepdims=False) - HALO
        offset = HALO - shear_shift(tilt, own_place, slices)
        return carry + lax.dynamic_slice_in_dim(layer, offset, width, 2).astype(jnp.float32)

    backward = lax.fori_loop(0, residual_wide.shape[0], one_view, empty)
    slab_new = (slab[0].astype(jnp.float32) - descent * (backward * root_scale)).astype(
        jnp.bfloat16
    )[None]
    return (object_now[None], slab_new)


def solution(mesh):
    return jax.shard_map(
        per_device,
        mesh=mesh,
        in_specs=(
            P("view", None, None, "strip"),
            P("view", None, None, "strip"),
            P("view", None, None, "strip"),
            P("view", "strip", None, None),
            P("view", "strip"),
            P(),
            P(),
        ),
        out_specs=(P("view", None, None, "strip"), P("view", None, None, "strip")),
        check_vma=False,
    )
```

profile of v0, /device:TPU:25, one launch (start us, length us, event | category | flops | bytes accessed | tf_op | source)
XLA Modules:
  0.0 618.8 jit_solution(3948516667276718579)
XLA Ops:
  8.0 4.8 collective-permute-start
  12.8 1.2 dynamic_slice.33
  18.1 1.1 gather_fusion
  29.7 13.3 %fusion.11 = f32[4,128,128]{2,1,0:T(8,128)S(1)} fusion(f32[4,128,128]{2,1,0:T(8,128)S(1)} %get-tuple-element.407, f32[4,128,128]{2,1,0:T(8,128)S(1)} %fusion.83, f32[4,128,128]{1,2,0:T(8,128)S(1)} %fusion.17), kind=kOutput, calls=%fused_computation.28 | convolution fusion | flops 101105664 | bytes 1048576 | tf_op jit(solution)/shard_map/pij,jk->pik/dot_general | solution.py:56
  43.0 96.3 %all-gather.4.cloned.1.call-done = bf16[64,2,128,128]{3,2,1,0:T(8,128)(2,1)} async-done(((bf16[1,2,128,128]{3,2,1,0:T(8,128)(2,1)}), bf16[64,2,128,128]{3,2,1,0:T(8,128)(2,1)}) %all-gather.4.cloned.1.call-update) | async-done | bytes 4194320 | tf_op jit(solution)/shard_map/all_gather | solution.py:73
  139.3 7.7 %fusion.277 = (bf16[64,2,128,16]{3,2,1,0:T(8,128)(2,1)}, bf16[64,2,128,16]{3,2,1,0:T(8,128)(2,1)}) fusion(bf16[64,2,128,128]{3,2,1,0:T(8,128)(2,1)} %all-gather.4.cloned.1.call-done), kind=kLoop, calls=%fused_computation.322 | loop fusion | bytes 2097152 | tf_op jit(solution)/shard_map/slice | solution.py:22
  147.0 3.5 copy.67
  150.5 4.6 collective-permute-start.3
  155.1 3.5 copy.66
  158.6 2.3 collective-permute-start.2
  162.8 1.9 collective-permute-start.1
  164.8 2.4 collective-permute-done.3
  167.1 3.1 copy.69
  170.2 8.6 %collective-permute-done.2 = bf16[64,2,128,16]{2,3,1,0:T(8,128)(2,1)} collective-permute-done((bf16[64,2,128,16]{2,3,1,0:T(8,128)(2,1)S(1)}, bf16[64,2,128,16]{2,3,1,0:T(8,128)(2,1)}, u32[]{:S(2)}, u32[]{:S(2)}) %collective-permute-start.2) | collective-permute-done | bytes 524320 | tf_op jit(solution)/shard_map/ppermute | solution.py:24
  178.8 4.5 copy.68
  183.3 10.7 %pad_maximum_fusion = bf16[64,2,128,160]{3,2,1,0:T(8,128)(2,1)} fusion(bf16[64,2,128,16]{3,2,1,0:T(8,128)(2,1)} %copy.69, bf16[64,2,128,128]{3,2,1,0:T(8,128)(2,1)} %all-gather.4.cloned.1.call-done, bf16[64,2,128,16]{3,2,1,0:T(8,128)(2,1)} %copy.68), kind=kLoop, calls=%fused_computation.4 | loop fusion | flops 15728640 | bytes 10485760 | tf_op jit(solution)/shard_map/concatenate | solution.py:26
  194.0 68.8 %while.36 = (s32[]{:T(128)}, f32[2,128,128]{2,1,0:T(8,128)S(1)}, s32[]{:T(128)}, bf16[64,2,128,160]{3,2,1,0:T(8,128)(2,1)}, s32[]{:T(128)}, /*index=5*/s32[]{:T(...) while((s32[]{:T(128)}, f32[2,128,128]{2,1,0:T(8,128)S(1)}, ...), condition=%wide.region_1.2_spmd.clone, body=%wide.region_0.1_spmd.clone.sunk | while | flops 98331 | bytes 328103 | solution.py:81
  262.8 4.3 collective-permute-start.4
  267.1 2.9 collective-permute-done.4
  270.2 1.1 gather_fusion.1
  284.7 1.9 collective-permute-start.5
  286.7 6.2 collective-permute-done.5
  293.6 124.3 %all-gather.6.cloned.1.call-done = bf16[128,128,128]{2,1,0:T(8,128)(2,1)} async-done(((bf16[2,128,128]{2,1,0:T(8,128)(2,1)}), bf16[128,128,128]{2,1,0:T(8,128)(2,1)}) %all-gather.6.cloned.1.call-update) | async-done | bytes 4194320 | tf_op jit(solution)/shard_map/all_gather | solution.py:122
  417.9 7.7 %fusion.276 = (bf16[64,2,128,16]{3,2,1,0:T(8,128)(2,1)}, bf16[64,2,128,16]{3,2,1,0:T(8,128)(2,1)}) fusion(bf16[64,2,128,128]{3,2,1,0:T(8,128)(2,1)} %bitcast.221), kind=kLoop, calls=%fused_computation.321 | loop fusion | bytes 2097152 | tf_op jit(solution)/shard_map/slice | solution.py:22
  425.6 3.5 copy.132
  429.1 4.5 collective-permute-start.7
  433.6 3.5 copy.131
  437.1 2.3 collective-permute-start.6
  439.4 6.3 %collective-permute-done.7 = bf16[64,2,128,16]{2,3,1,0:T(8,128)(2,1)S(1)} collective-permute-done((bf16[64,2,128,16]{2,3,1,0:T(8,128)(2,1)S(1)}, bf16[64,2,128,16]{2,3,1,0:T(8,128)(2,1)S(1)}, u32[]{:S(2)}, u32[]{:S(2)}) %collective-permute-start.7) | collective-permute-done | bytes 524320 | tf_op jit(solution)/shard_map/ppermute | solution.py:25
  445.7 3.1 copy.92
  448.8 8.3 %collective-permute-done.6 = bf16[64,2,128,16]{2,3,1,0:T(8,128)(2,1)S(1)} collective-permute-done((bf16[64,2,128,16]{2,3,1,0:T(8,128)(2,1)S(1)}, bf16[64,2,128,16]{2,3,1,0:T(8,128)(2,1)S(1)}, u32[]{:S(2)}, u32[]{:S(2)}) %collective-permute-start.6) | collective-permute-done | bytes 524320 | tf_op jit(solution)/shard_map/ppermute | solution.py:24
  457.1 3.0 copy.91
  460.2 10.7 %pad_maximum_fusion.1 = bf16[64,2,128,160]{3,2,1,0:T(8,128)(2,1)} fusion(bf16[64,2,128,16]{3,2,1,0:T(8,128)(2,1)} %copy.92, bf16[64,2,128,128]{3,2,1,0:T(8,128)(2,1)} %bitcast.222, bf16[64,2,128,16]{3,2,1,0:T(8,128)(2,1)} %copy.91), kind=kLoop, calls=%fused_computation.5 | loop fusion | flops 15728640 | bytes 10485760 | tf_op jit(solution)/shard_map/concatenate | solution.py:26
  470.9 140.0 %while.37 = (s32[]{:T(128)}, f32[2,128,128]{2,1,0:T(8,128)S(1)}, s32[64]{0:T(128)S(1)}, s32[]{:T(128)}, bf16[64,2,128,160]{3,2,1,0:T(8,128)(2,1)}, /*index=5*/s3...) while((s32[]{:T(128)}, f32[2,128,128]{2,1,0:T(8,128)S(1)}, ...), condition=%wide.region_3.4_spmd.clone, body=%wide.region_2.3_spmd.clone.sunk | while | flops 98330 | bytes 328103 | solution.py:131
  472.0 1.0 convert_add_fusion.5
  474.2 1.0 convert_add_fusion.5
  476.4 1.0 convert_add_fusion.5
  478.6 1.0 convert_add_fusion.5
  480.8 1.0 convert_add_fusion.5
  483.0 1.0 convert_add_fusion.5
  485.1 1.0 convert_add_fusion.5
  487.3 1.0 convert_add_fusion.5
  489.5 1.0 convert_add_fusion.5
  491.7 1.0 convert_add_fusion.5
  493.9 1.0 convert_add_fusion.5
  496.1 1.0 convert_add_fusion.5
  498.3 1.0 convert_add_fusion.5
  500.5 1.0 convert_add_fusion.5
  502.7 1.0 convert_add_fusion.5
  504.8 1.0 convert_add_fusion.5
  507.0 1.0 convert_add_fusion.5
  509.2 1.0 convert_add_fusion.5
  511.4 1.0 convert_add_fusion.5
  513.6 1.0 convert_add_fusion.5
  515.8 1.0 convert_add_fusion.5
  518.0 1.0 convert_add_fusion.5
  520.2 1.0 convert_add_fusion.5
  522.4 1.0 convert_add_fusion.5
  524.5 1.0 convert_add_fusion.5
  526.7 1.0 convert_add_fusion.5
  546.4 1.0 convert_add_fusion.5
  548.6 1.0 convert_add_fusion.5
  588.0 1.0 convert_add_fusion.5
  590.2 1.0 convert_add_fusion.5
  (233 shorter events, 166.4 us)
Async XLA Ops:
  7.2 18.6 %copy-start = (f32[1,4,128,128]{3,2,1,0:T(8,128)S(1)}, f32[1,4,128,128]{3,2,1,0:T(8,128)}, u32[]{:S(2)}) copy-start(f32[1,4,128,128]{3,2,1,0:T(8,128)} %param.14) | copy-start | bytes 786436
  7.2 132.1 %all-gather.4.cloned.1.call-start = ((), (), s32[]{:S(2)}) async-start(), calls=%async_computation | async-start | bytes 4259840 | tf_op jit(solution)/shard_map/all_gather | solution.py:73
  7.9 410.0 %all-gather.6.cloned.1.call-start = ((), (), s32[]{:S(2)}) async-start(), calls=%async_computation.1 | async-start | bytes 4259840 | tf_op jit(solution)/shard_map/all_gather | solution.py:122
  8.0 9.0 %collective-permute-start = (f32[2,128,128]{2,1,0:T(8,128)}, f32[2,128,128]{2,1,0:T(8,128)S(1)}, u32[]{:S(2)}, u32[]{:S(2)}) collective-permute-start(f32[2,128,128]{2,1,0:T(8,128)} %bitcast.223), channel_id=1, source_target_pairs={{1,0},{2,1},{3,2},{4,3},{5,4},{6,5},{7,6},{9,8},{10,9},{11,10},{12... | collective-permute-start | bytes 393224 | tf_op jit(solution)/shard_map/ppermute | solution.py:33
  150.5 16.6 %collective-permute-start.3 = (bf16[64,2,128,16]{2,3,1,0:T(8,128)(2,1)S(1)}, bf16[64,2,128,16]{2,3,1,0:T(8,128)(2,1)S(1)}, u32[]{:S(2)}, u32[]{:S(2)}) collective-permute-start(bf16[64,2,128,16]{2,3,1,0:T(8,128)(2,1)S(1)} %copy.67), channel_id=1, source_target_pairs={{1,0},{2,1},{3,2},{4,3},{5,4},{6,5},{7,6},{9,8},{10,9},{11,10},{12... | collective-permute-start | bytes 1572872 | tf_op jit(solution)/shard_map/ppermute | solution.py:25
  158.6 20.2 %collective-permute-start.2 = (bf16[64,2,128,16]{2,3,1,0:T(8,128)(2,1)S(1)}, bf16[64,2,128,16]{2,3,1,0:T(8,128)(2,1)}, u32[]{:S(2)}, u32[]{:S(2)}) collective-permute-start(bf16[64,2,128,16]{2,3,1,0:T(8,128)(2,1)S(1)} %copy.66), channel_id=1, source_target_pairs={{0,1},{1,2},{2,3},{3,4},{4,5},{5,6},{6,7},{8,9},{9,10},{10,11},{11... | collective-permute-start | bytes 1572872 | tf_op jit(solution)/shard_map/ppermute | solution.py:24
  162.8 99.9 %collective-permute-start.1 = (f32[2,128,128]{2,1,0:T(8,128)S(1)}, f32[2,128,128]{2,1,0:T(8,128)S(1)}, u32[]{:S(2)}, u32[]{:S(2)}) collective-permute-start(f32[2,128,128]{2,1,0:T(8,128)S(1)} %slice.65), channel_id=1, source_target_pairs={{0,1},{1,2},{2,3},{3,4},{4,5},{5,6},{6,7},{8,9},{9,10},{10,11},{11... | collective-permute-start | bytes 393224 | tf_op jit(solution)/shard_map/ppermute | solution.py:33
  183.3 79.5 %copy-start.1 = (f32[1,2,128,128]{3,2,1,0:T(8,128)S(1)}, f32[1,2,128,128]{3,2,1,0:T(8,128)}, u32[]{:S(2)}) copy-start(f32[1,2,128,128]{3,2,1,0:T(8,128)} %param.12) | copy-start | bytes 393220
  183.3 79.5 %copy-start.2 = (f32[1,2,128,128]{3,2,1,0:T(8,128)S(1)}, f32[1,2,128,128]{3,2,1,0:T(8,128)}, u32[]{:S(2)}) copy-start(f32[1,2,128,128]{3,2,1,0:T(8,128)} %param.13) | copy-start | bytes 393220
  262.8 7.2 %collective-permute-start.4 = (f32[2,128,128]{2,1,0:T(8,128)S(1)}, f32[2,128,128]{2,1,0:T(8,128)S(1)}, u32[]{:S(2)}, u32[]{:S(2)}) collective-permute-start(f32[2,128,128]{2,1,0:T(8,128)S(1)} %fusion.44), channel_id=1, source_target_pairs={{1,0},{2,1},{3,2},{4,3},{5,4},{6,5},{7,6},{9,8},{10,9},{11,10},{12... | collective-permute-start | bytes 393224 | tf_op jit(solution)/shard_map/ppermute | solution.py:33
  284.7 8.1 %collective-permute-start.5 = (f32[2,128,128]{2,1,0:T(8,128)S(1)}, f32[2,128,128]{2,1,0:T(8,128)S(1)}, u32[]{:S(2)}, u32[]{:S(2)}) collective-permute-start(f32[2,128,128]{2,1,0:T(8,128)S(1)} %slice.71), channel_id=1, source_target_pairs={{0,1},{1,2},{2,3},{3,4},{4,5},{5,6},{6,7},{8,9},{9,10},{10,11},{11... | collective-permute-start | bytes 393224 | tf_op jit(solution)/shard_map/ppermute | solution.py:33
  429.1 16.6 %collective-permute-start.7 = (bf16[64,2,128,16]{2,3,1,0:T(8,128)(2,1)S(1)}, bf16[64,2,128,16]{2,3,1,0:T(8,128)(2,1)S(1)}, u32[]{:S(2)}, u32[]{:S(2)}) collective-permute-start(bf16[64,2,128,16]{2,3,1,0:T(8,128)(2,1)S(1)} %copy.132), channel_id=1, source_target_pairs={{1,0},{2,1},{3,2},{4,3},{5,4},{6,5},{7,6},{9,8},{10,9},{11,10},{12... | collective-permute-start | bytes 1572872 | tf_op jit(solution)/shard_map/ppermute | solution.py:25
  437.1 20.0 %collective-permute-start.6 = (bf16[64,2,128,16]{2,3,1,0:T(8,128)(2,1)S(1)}, bf16[64,2,128,16]{2,3,1,0:T(8,128)(2,1)S(1)}, u32[]{:S(2)}, u32[]{:S(2)}) collective-permute-start(bf16[64,2,128,16]{2,3,1,0:T(8,128)(2,1)S(1)} %copy.131), channel_id=1, source_target_pairs={{0,1},{1,2},{2,3},{3,4},{4,5},{5,6},{6,7},{8,9},{9,10},{10,11},{11... | collective-permute-start | bytes 1572872 | tf_op jit(solution)/shard_map/ppermute | solution.py:24
  460.2 10.7 %copy-start.4 = (s32[64]{0:T(128)S(1)}, s32[64]{0:T(128)}, u32[]{:S(2)}) copy-start(s32[64]{0:T(128)} %param.16) | copy-start | bytes 772
  460.2 150.7 %copy-start.3 = (bf16[1,2,128,128]{3,2,1,0:T(8,128)(2,1)S(1)}, bf16[1,2,128,128]{3,2,1,0:T(8,128)(2,1)}, u32[]{:S(2)}) copy-start(bf16[1,2,128,128]{3,2,1,0:T(8,128)(2,1)} %param.11) | copy-start | bytes 196612
Sparse Core Ops, SparseCore 0:
  10.2 129.0 all-gather.3
  293.7 124.1 all-gather.5
where the time goes:
time: 631 us; the launch traced here: 619 us
  waiting for transfers between devices  256 us (41%)
  other arithmetic  155 us (25%)
  local copies, waits for them, and re-layouts  84.8 us (13%)
  loops' own time  43.1 us (7%)
  matrix products  37.4 us (6%)
  starting transfers between devices  26.7 us (4%)
  between operations  15.6 us (2%)
    all_gather x1, waiting for transfers between devices, per_device(): residual_all = lax.all_gather(residual, 'view', axis=0, tiled=True)  124 us
    all_gather x1, waiting for transfers between devices, per_device(): slab_all = lax.all_gather(slab, 'view', axis=0, tiled=True)  96.3 us
    add x64, other arithmetic, one_view(): carry + lax.dynamic_slice_in_dim(layer, offset, width, 2).astype(jnp.floa...  65.1 us
    add x64, other arithmetic, one_slice(): carry + lax.dynamic_slice_in_dim(layer, offset, width, 2).astype(jnp.floa...  65 us
    another operation x1, loops' own time, per_device(): backward = lax.fori_loop(0, residual_wide.shape[0], one_view, empty)  39.4 us
    dynamic_slice x64, local copies, waits for them, and re-layouts, one_view(): lax.dynamic_index_in_dim(angles, 0 + position, 0, keepdims=False) - HALO  35.6 us
    concatenate x2, other arithmetic, with_halo(): shard = jnp.concatenate([before, shard, after], axis=dim)  21.4 us
    slice x3, local copies, waits for them, and re-layouts, with_halo(): last = lax.slice_in_dim(shard, length - width, length, axis=dim)  18.9 us
  transfers between devices with their start and end apart: 10, of which 8 were waited for; matrix products, arithmetic and copies ran while one was open for 20% of the time, Pallas kernels for 0%

commit v1 on v0

v1 whole, which is shorter than its diff:
```python
import math

import jax
import jax.numpy as jnp
import numpy as np
from jax import lax
from jax.experimental import pallas as pl
from jax.experimental.pallas import tpu as pltpu
from jax.sharding import PartitionSpec as P

HALO = 16
ITERS = 2
TAPS = 2 * HALO + 1
coupling = 0.5
descent = 0.5
bf16 = jnp.bfloat16
f32 = jnp.float32


def dft_blocks(length):
    counter = np.arange(length)
    phase = (counter[:, None] * counter[None, :]) % length
    angle = phase.astype(np.float64) * (2.0 * math.pi / length)
    cosine = np.cos(angle) / math.sqrt(length)
    sine = np.sin(angle) / math.sqrt(length)
    ahead = np.block([[cosine, sine], [-sine, cosine]])
    behind = np.block([[cosine, -sine], [sine, cosine]])
    both = np.stack([ahead, behind]).astype(np.float32)
    high = both.astype(jnp.bfloat16)
    low = (both - high.astype(np.float32)).astype(jnp.bfloat16)
    return jnp.asarray(np.stack([high, low], axis=1))


def split(value):
    high = value.astype(bf16)
    low = (value - high.astype(f32)).astype(bf16)
    return high, low


def dot(a, b):
    return jnp.dot(a, b, preferred_element_type=f32)


def table_left(table, value):
    high, low = split(value)
    return dot(table[0], high) + dot(table[0], low) + dot(table[1], high)


def table_right(value, table):
    high, low = split(value)
    return dot(high, table[0]) + dot(low, table[0]) + dot(high, table[1])


def gradient_kernel(starts, own, following, measured, probe, tables, spread):
    side = own.shape[1]
    count = measured.shape[0]
    ahead = (tables[0, 0], tables[0, 1])
    behind = (tables[1, 0], tables[1, 1])
    wide_real = jnp.concatenate([own[0], following[0]], axis=1)
    wide_imag = jnp.concatenate([own[1], following[1]], axis=1)
    probe_real = probe[0]
    probe_imag = probe[1]
    exits = []
    for p in range(count):
        by = lax.rem(2 * side - starts[p], 2 * side)
        patch_real = pltpu.roll(wide_real, by, 1)[:, :side]
        patch_imag = pltpu.roll(wide_imag, by, 1)[:, :side]
        exit_real = probe_real * patch_real - probe_imag * patch_imag
        exit_imag = probe_real * patch_imag + probe_imag * patch_real
        exits.append(jnp.concatenate([exit_real, exit_imag], axis=0))
    exitw = jnp.concatenate(exits, axis=1)
    left = table_left(ahead, exitw)

    def to_rows(value):
        return jnp.concatenate(
            [
                jnp.concatenate(
                    [
                        value[:side, p * side : (p + 1) * side],
                        value[side:, p * side : (p + 1) * side],
                    ],
                    axis=1,
                )
                for p in range(count)
            ],
            axis=0,
        )

    def to_columns(value):
        return jnp.concatenate(
            [
                jnp.concatenate(
                    [
                        value[p * side : (p + 1) * side, :side],
                        value[p * side : (p + 1) * side, side:],
                    ],
                    axis=0,
                )
                for p in range(count)
            ],
            axis=1,
        )

    far = table_right(to_rows(left), behind)
    far_real = far[:, :side]
    far_imag = far[:, side:]
    level = jnp.concatenate([measured[p] for p in range(count)], axis=0)
    factor = level * lax.rsqrt(far_real * far_real + far_imag * far_imag + 1.0)
    fixed = jnp.concatenate([far_real * factor, far_imag * factor], axis=1)
    back = table_left(behind, to_columns(table_right(fixed, ahead)))
    delta = back - exitw
    total_real = jnp.zeros((side, 2 * side), f32)
    total_imag = jnp.zeros((side, 2 * side), f32)
    nothing = jnp.zeros((side, side), f32)
    for p in range(count):
        delta_real = delta[:side, p * side : (p + 1) * side]
        delta_imag = delta[side:, p * side : (p + 1) * side]
        grad_real = probe_real * delta_real + probe_imag * delta_imag
        grad_imag = probe_real * delta_imag - probe_imag * delta_real
        total_real += pltpu.roll(jnp.concatenate([grad_real, nothing], axis=1), starts[p], 1)
        total_imag += pltpu.roll(jnp.concatenate([grad_imag, nothing], axis=1), starts[p], 1)
    spread[0, 0] = total_real[:, :side]
    spread[0, 1] = total_imag[:, :side]
    spread[1, 0] = total_real[:, side:]
    spread[1, 1] = total_imag[:, side:]


def gradient(starts, own, following, measured, probe, tables):
    vmem = pl.BlockSpec(memory_space=pltpu.VMEM)
    return pl.pallas_call(
        gradient_kernel,
        out_shape=jax.ShapeDtypeStruct((2,) + own.shape, f32),
        in_specs=[pl.BlockSpec(memory_space=pltpu.SMEM)] + [vmem] * 5,
        out_specs=vmem,
        compiler_params=pltpu.CompilerParams(vmem_limit_bytes=32 * 1024 * 1024),
    )(starts, own, following, measured, probe, tables)


def shear_kernel(scale, lines, source, choice, out, plain, taps, result):
    channels = choice.shape[0]
    side = source.shape[1]
    plain[...] = source[...].astype(f32)
    for r in range(lines):
        near = plain[pl.ds(r, channels, stride=2 * lines), :]
        edge = plain[pl.ds(lines + r, channels, stride=2 * lines), :]
        wide = jnp.concatenate([near, edge], axis=1)
        for d in range(TAPS):
            moved = pltpu.roll(wide, (2 * side + HALO - d) % (2 * side), 1)[:, :side]
            taps[d * channels : (d + 1) * channels, r * side : (r + 1) * side] = moved.astype(bf16)
    summed = dot(choice[...], taps[...]) * scale
    for r in range(lines):
        result[pl.ds(r, channels, stride=lines), :] = summed[:, r * side : (r + 1) * side]
    out[...] = result[...].astype(bf16)


def shear_sum(source, choice, scale):
    channels = choice.shape[0]
    side = source.shape[1]
    lines = source.shape[0] // (2 * channels)
    vmem = pl.BlockSpec(memory_space=pltpu.VMEM)
    return pl.pallas_call(
        lambda *refs: shear_kernel(scale, lines, *refs),
        out_shape=jax.ShapeDtypeStruct((lines * channels, side), bf16),
        in_specs=[vmem] * 2,
        out_specs=vmem,
        scratch_shapes=[
            pltpu.VMEM((2 * lines * channels, side), f32),
            pltpu.VMEM((TAPS * channels, lines * side), bf16),
            pltpu.VMEM((lines * channels, side), f32),
        ],
        compiler_params=pltpu.CompilerParams(vmem_limit_bytes=32 * 1024 * 1024),
    )(source, choice)


def strip_move(value, by):
    length = lax.axis_size("strip")
    pairs = [(i, i + by) for i in range(length) if 0 <= i + by < length]
    return lax.ppermute(value, "strip", pairs)


def with_edges(value, before, after):
    lane = lax.broadcasted_iota(jnp.int32, value.shape, value.ndim - 1)
    return jnp.where(lane < value.shape[-1] // 2, after, before)


def exchange(own, edge, groups):
    side = own.shape[-1]
    lines = own.size // (groups * side)
    parcel = jnp.concatenate(
        [own.reshape(groups, lines, side), edge.reshape(groups, lines, side)], axis=1
    )
    got = lax.all_to_all(parcel, "view", 0, 0, tiled=True)
    return got.reshape(groups * 2 * lines, side)


def give_back(value, groups):
    side = value.shape[-1]
    parcel = value.reshape(groups, value.shape[0] // groups, side)
    return lax.all_to_all(parcel, "view", 0, 0, tiled=True)


def per_device(slab, psi_start, dual, amplitudes, offsets, angles, probe):
    slices = lax.axis_size("view")
    own_slab = slab[0]
    shape = own_slab.shape
    psi = psi_start[0]
    own_dual = dual[0]
    measured = amplitudes[0]
    starts = offsets[0]
    root_scale = 1.0 / math.sqrt(slices)
    tables = dft_blocks(probe.shape[1])
    step_size = 1.0 / starts.shape[0]

    depth = jnp.arange(slices, dtype=jnp.int32)
    tilt = angles - HALO
    shift = (tilt[:, None] * (2 * depth[None, :] - slices + 1)) // slices
    tap = jnp.arange(TAPS, dtype=jnp.int32) - HALO
    choice_project = (
        (shift[:, None, :] == tap[None, :, None]).astype(bf16).reshape(slices, TAPS * slices)
    )
    choice_back = (
        (-shift.T[:, None, :] == tap[None, :, None]).astype(bf16).reshape(slices, TAPS * slices)
    )

    slab_edge = with_edges(own_slab, strip_move(own_slab, 1), strip_move(own_slab, -1))
    following = strip_move(psi, -1)
    lined = exchange(own_slab, slab_edge, slices)
    spread = gradient(starts, psi, following, measured, probe, tables)
    spill = strip_move(spread[1], 1)
    sums = shear_sum(lined, choice_project, root_scale)
    projected = give_back(sums, slices).reshape(shape).astype(f32)
    pull = projected - own_dual
    psi = psi + step_size * (spread[0] + spill) + coupling * (pull - psi)

    following = strip_move(psi, -1)
    spread = gradient(starts, psi, following, measured, probe, tables)
    part = psi + step_size * spread[0] + coupling * (pull - psi)
    rest = (pull - part).astype(bf16)
    outer = (spread[1] * step_size).astype(bf16)
    up = strip_move(jnp.stack([rest, outer]), 1)
    up_two = strip_move(outer, 2)
    down = strip_move(rest, -1)
    incoming = up[1].astype(f32)
    psi = part + incoming
    residual = (pull - psi).astype(bf16)
    residual_edge = with_edges(
        residual,
        (up[0].astype(f32) - up_two.astype(f32)).astype(bf16),
        (down.astype(f32) - outer.astype(f32)).astype(bf16),
    )
    last = lax.axis_index("strip") == lax.axis_size("strip") - 1
    first = lax.axis_index("strip") == 0
    lane = lax.broadcasted_iota(jnp.int32, shape, 2)
    outside = (last & (lane < shape[2] // 2)) | (first & (lane >= shape[2] // 2))
    residual_edge = jnp.where(outside, jnp.zeros_like(residual_edge), residual_edge)
    lined = exchange(residual, residual_edge, slices)
    sums = shear_sum(lined, choice_back, descent * root_scale)
    backward = give_back(sums, slices).reshape(shape).astype(f32)
    slab_new = (own_slab.astype(f32) - backward).astype(bf16)
    return (psi[None], slab_new[None])


def solution(mesh):
    return jax.shard_map(
        per_device,
        mesh=mesh,
        in_specs=(
            P("view", None, None, "strip"),
            P("view", None, None, "strip"),
            P("view", None, None, "strip"),
            P("view", "strip", None, None),
            P("view", "strip"),
            P(),
            P(),
        ),
        out_specs=(P("view", None, None, "strip"), P("view", None, None, "strip")),
        check_vma=False,
    )
```

time: 631 us -> 143 us (0.23); the launches traced: 619 us -> 143 us
  waiting for transfers between devices: 256 us -> 37 us
  other arithmetic: 155 us -> 3.25 us
  local copies, waits for them, and re-layouts: 84.8 us -> 1.22 us
  blocking collectives: 0 us -> 44 us
  loops' own time: 43.1 us -> 0 us
  matrix products: 37.4 us -> 0 us
  starting transfers between devices: 26.7 us -> 47.5 us
  between operations: 15.6 us -> 0.96 us
  Pallas kernels: 0 us -> 8.68 us
    all_gather x2 -> x0, waiting for transfers between devices: 221 us -> none  [the longest x1 124 us: per_device(): residual_all = lax.all_gather(residual, 'view', axis=0, tiled=True)]
    add x132 -> x2, other arithmetic: 131 us -> 0.71 us  [the longest x1 0.66 us: per_device(): shift = tilt[:, None] * (2 * depth[None, :] - slices + 1) // slices]
    all_to_all x0 -> x2, blocking collectives: none -> 44 us  [the longest x1 25.7 us: exchange(): got = lax.all_to_all(parcel, 'view', 0, 0, tiled=True)]
    another operation x2 -> x0, loops' own time: 43.1 us -> none  [the longest x1 39.4 us: per_device(): backward = lax.fori_loop(0, residual_wide.shape[0], one_view, empty)]
    dot_general x34 -> x0, matrix products: 37.4 us -> none  [the longest x4 15.5 us: transform(): jnp.einsum('pij,jk->pik', left_real, sine, precision=highest)]
    dynamic_slice x65 -> x0, local copies, waits for them, and re-layouts: 36.8 us -> none  [the longest x64 35.6 us: one_view(): lax.dynamic_index_in_dim(angles, 0 + position, 0, keepdims=False) - HALO]
    slice x8 -> x0, local copies, waits for them, and re-layouts: 23.3 us -> none  [the longest x3 18.9 us: with_halo(): last = lax.slice_in_dim(shard, length - width, length, axis=dim)]
    concatenate x5 -> x2, other arithmetic: 23 us -> 0.8 us  [exchange(): jnp.concatenate([own.reshape(groups, lines, side), edge.reshape(groups, l...]
  transfers between devices with their start and end apart: 10 -> 10, of which waited for: 8 -> 6; matrix products, arithmetic and copies ran while one was open for 20% -> 2% of each run, Pallas kernels for 0% -> 2%
where the time goes in v1:
time: 143 us
  starting transfers between devices  47.5 us (33%)
  blocking collectives  44 us (31%)
  waiting for transfers between devices  37 us (26%)
  Pallas kernels  8.68 us (6%)
  other arithmetic  3.25 us (2%)
    ppermute x8, starting transfers between devices, strip_move(): return lax.ppermute(value, 'strip', pairs)  25.9 us
    all_to_all x1, blocking collectives, exchange(): got = lax.all_to_all(parcel, 'view', 0, 0, tiled=True)  25.7 us
    all_to_all x1, blocking collectives, give_back(): return lax.all_to_all(parcel, 'view', 0, 0, tiled=True)  18.3 us
    all_to_all x1, starting transfers between devices, exchange(): got = lax.all_to_all(parcel, 'view', 0, 0, tiled=True)  17.2 us
    ppermute x8, waiting for transfers between devices, strip_move(): return lax.ppermute(value, 'strip', pairs)  17 us
    all_to_all x1, waiting for transfers between devices, exchange(): got = lax.all_to_all(parcel, 'view', 0, 0, tiled=True)  14.4 us
    all_to_all x1, waiting for transfers between devices, give_back(): return lax.all_to_all(parcel, 'view', 0, 0, tiled=True)  5.62 us
    pallas_call x2, Pallas kernels, gradient(): pl.pallas_call(gradient_kernel, out_shape=jax.ShapeDtypeStruct((2,) + own...  5.06 us
  transfers between devices with their start and end apart: 10, of which 6 were waited for; matrix products, arithmetic and copies ran while one was open for 2% of the time, Pallas kernels for 2%

profile of v1, /device:TPU:25, one launch (start us, length us, event | category | flops | bytes accessed | tf_op | source)
XLA Modules:
  0.0 142.7 jit_solution(11331356595239203853)
XLA Ops:
  0.6 4.8 %collective-permute-start.2 = (bf16[2,128,128]{2,1,0:T(8,128)(2,1)}, bf16[2,128,128]{2,1,0:T(8,128)(2,1)S(1)}, u32[]{:S(2)}, u32[]{:S(2)}) collective-permute-start(bf16[2,128,128]{2,1,0:T(8,128)(2,1)} %bitcast.106), channel_id=1, source_target_pairs={{1,0},{2,1},{3,2},{4,3},{5,4},{6,5},{7,6},{9,8},{10,9},{11,10},{12... | collective-permute-start | bytes 196616 | tf_op jit(solution)/shard_map/ppermute | solution.py:178
  5.5 2.0 %collective-permute-start.3 = (bf16[2,128,128]{2,1,0:T(8,128)(2,1)}, bf16[2,128,128]{2,1,0:T(8,128)(2,1)S(1)}, u32[]{:S(2)}, u32[]{:S(2)}) collective-permute-start(bf16[2,128,128]{2,1,0:T(8,128)(2,1)} %bitcast.107), channel_id=1, source_target_pairs={{0,1},{1,2},{2,3},{3,4},{4,5},{5,6},{6,7},{8,9},{9,10},{10,11},{11... | collective-permute-start | bytes 196616 | tf_op jit(solution)/shard_map/ppermute | solution.py:178
  7.4 5.7 %collective-permute-start = (f32[2,128,128]{2,1,0:T(8,128)}, f32[2,128,128]{2,1,0:T(8,128)S(1)}, u32[]{:S(2)}, u32[]{:S(2)}) collective-permute-start(f32[2,128,128]{2,1,0:T(8,128)} %bitcast.97), channel_id=1, source_target_pairs={{1,0},{2,1},{3,2},{4,3},{5,4},{6,5},{7,6},{9,8},{10,9},{11,10},{12... | collective-permute-start | bytes 393224 | tf_op jit(solution)/shard_map/ppermute | solution.py:178
  13.2 0.7 multiply_add_fusion
  13.8 0.1 fusion.15
  14.0 0.1 eq.46
  14.1 0.3 eq.47
  14.3 0.1 eq.54
  14.4 0.0 copy-start.6
  14.4 0.3 eq.55
  14.7 0.0 copy-start
  14.7 0.0 copy-start.1
  14.7 0.0 copy-start.2
  14.8 0.0 copy-start.3
  14.8 0.0 copy-start.4
  14.8 0.1 eq.48
  14.8 0.1 eq.49
  14.9 0.0 collective-permute-done.2
  14.9 0.0 collective-permute-done.3
  15.0 0.3 copy-done.6
  15.3 0.7 pad_maximum_fusion
  16.0 17.2 %all-to-all-start = ((bf16[64,8,128]{2,1,0:T(8,128)(2,1)}), bf16[64,8,128]{2,1,0:T(8,128)(2,1)S(1)}, u32[]{:S(2)}, u32[]{:S(2)}) async-start(bf16[64,8,128]{2,1,0:T(8,128)(2,1)} %pad_maximum_fusion), calls=%async_computation | async-start | bytes 262144 | tf_op jit(solution)/shard_map/all_to_all | solution.py:192
  33.2 0.1 compare_convert_fusion
  33.3 0.0 copy-start.5
  33.3 0.0 collective-permute-done.following
  33.3 0.0 copy-done
  33.3 0.0 copy-done.1
  33.3 0.0 copy-done.2
  33.4 0.0 copy-done.3
  33.4 0.0 copy-done.4
  33.4 2.5 %shard_map.95 = f32[2,2,128,128]{3,2,1,0:T(8,128)S(1)} custom-call(s32[4]{0:T(128)S(1)} %bitcast.100, f32[2,128,128]{2,1,0:T(8,128)S(1)} %bitcast.98, f32[2,128,128]{2,1,0:T(8,128)S(1)} %collective-permute-done.following, f32[4,128,128]{2,1,0:T(8,128)S(1)} %bitcast.93, f32[2,128,128]{2,1,0:T(8,128)S(1)} %copy-done.3, bf16[2,2,256,256]{3,2,1,0:T(8,128)(2,1)S(1)} %copy-done), custom_call_target="tpu_custom_call" | custom-call | tf_op jit(solution)/shard_map/pallas_call | solution.py:130
  35.9 14.4 %all-to-all-done = bf16[64,8,128]{2,1,0:T(8,128)(2,1)S(1)} async-done(((bf16[64,8,128]{2,1,0:T(8,128)(2,1)}), bf16[64,8,128]{2,1,0:T(8,128)(2,1)S(1)}, u32[]{:S(2)}, u32[]{:S(2)}) %all-to-all-start) | async-done | bytes 131104 | tf_op jit(solution)/shard_map/all_to_all | solution.py:192
  50.3 2.1 %shard_map.96 = bf16[256,128]{1,0:T(8,128)(2,1)} custom-call(bf16[512,128]{1,0:T(8,128)(2,1)S(1)} %bitcast.95, bf16[64,2112]{1,0:T(8,128)(2,1)S(1)} %get-tuple-element.5.refs_1_), custom_call_target="tpu_custom_call" | custom-call | tf_op jit(solution)/shard_map/pallas_call | solution.py:161
  52.4 4.4 %all-to-all-start.1 = ((bf16[64,4,128]{2,1,0:T(4,128)(2,1)}), bf16[64,4,128]{2,1,0:T(4,128)(2,1)S(1)}, u32[]{:S(2)}, u32[]{:S(2)}) async-start(bf16[64,4,128]{2,1,0:T(4,128)(2,1)} %bitcast.9), calls=%async_computation.1 | async-start | bytes 131072 | tf_op jit(solution)/shard_map/all_to_all | solution.py:199
  56.9 2.6 %collective-permute-start.1 = (f32[2,128,128]{2,1,0:T(8,128)S(1)}, f32[2,128,128]{2,1,0:T(8,128)S(1)}, u32[]{:S(2)}, u32[]{:S(2)}) collective-permute-start(f32[2,128,128]{2,1,0:T(8,128)S(1)} %slice_bitcast_fusion), channel_id=1, source_target_pairs={{0,1},{1,2},{2,3},{3,4},{4,5},{5,6},{6,7},{8,9},{9,10},{10,11},{11... | collective-permute-start | bytes 393224 | tf_op jit(solution)/shard_map/ppermute | solution.py:178
  59.5 6.5 %collective-permute-done.1 = f32[2,128,128]{2,1,0:T(8,128)S(1)} collective-permute-done((f32[2,128,128]{2,1,0:T(8,128)S(1)}, f32[2,128,128]{2,1,0:T(8,128)S(1)}, u32[]{:S(2)}, u32[]{:S(2)}) %collective-permute-start.1) | collective-permute-done | bytes 131104 | tf_op jit(solution)/shard_map/ppermute | solution.py:178
  66.0 5.6 %all-to-all-done.1 = bf16[64,4,128]{2,1,0:T(4,128)(2,1)S(1)} async-done(((bf16[64,4,128]{2,1,0:T(4,128)(2,1)}), bf16[64,4,128]{2,1,0:T(4,128)(2,1)S(1)}, u32[]{:S(2)}, u32[]{:S(2)}) %all-to-all-start.1) | async-done | bytes 65568 | tf_op jit(solution)/shard_map/all_to_all | solution.py:199
  71.6 0.0 copy-done.5
  71.7 2.7 %collective-permute-start.4 = (f32[2,128,128]{2,1,0:T(8,128)S(1)}, f32[2,128,128]{2,1,0:T(8,128)S(1)}, u32[]{:S(2)}, u32[]{:S(2)}) collective-permute-start(f32[2,128,128]{2,1,0:T(8,128)S(1)} %fusion.7.own), channel_id=1, source_target_pairs={{1,0},{2,1},{3,2},{4,3},{5,4},{6,5},{7,6},{9,8},{10,9},{11,10},{12... | collective-permute-start | bytes 393224 | tf_op jit(solution)/shard_map/ppermute | solution.py:178
  74.4 5.3 %collective-permute-done.4.following = f32[2,128,128]{2,1,0:T(8,128)S(1)} collective-permute-done((f32[2,128,128]{2,1,0:T(8,128)S(1)}, f32[2,128,128]{2,1,0:T(8,128)S(1)}, u32[]{:S(2)}, u32[]{:S(2)}) %collective-permute-start.4) | collective-permute-done | bytes 131104 | tf_op jit(solution)/shard_map/ppermute | solution.py:178
  79.7 2.5 %shard_map.97 = f32[2,2,128,128]{3,2,1,0:T(8,128)S(1)} custom-call(s32[4]{0:T(128)S(1)} %bitcast.101, f32[2,128,128]{2,1,0:T(8,128)S(1)} %fusion.7.own, f32[2,128,128]{2,1,0:T(8,128)S(1)} %collective-permute-done.4.following, f32[4,128,128]{2,1,0:T(8,128)S(1)} %bitcast.94, f32[2,128,128]{2,1,0:T(8,128)S(1)} %copy-done.3, bf16[2,2,256,256]{3,2,1,0:T(8,128)(2,1)S(1)} %copy-done), custom_call_target="tpu_custom_call" | custom-call | tf_op jit(solution)/shard_map/pallas_call | solution.py:130
  82.3 0.1 subtract_convert_fusion.2
  82.4 3.6 %collective-permute-start.6 = (bf16[2,128,128]{2,1,0:T(8,128)(2,1)S(1)}, bf16[2,128,128]{2,1,0:T(8,128)(2,1)S(1)}, u32[]{:S(2)}, u32[]{:S(2)}) collective-permute-start(bf16[2,128,128]{2,1,0:T(8,128)(2,1)S(1)} %subtract_convert_fusion.2), channel_id=1, source_target_pairs={{1,0},{2,1},{3,2},{4,3},{5,4},{6,5},{7,6},{9,8},{10,9},{11,10},{12... | collective-permute-start | bytes 196616 | tf_op jit(solution)/shard_map/ppermute | solution.py:178
  86.0 3.1 %collective-permute-start.5 = (bf16[2,2,128,128]{3,2,1,0:T(8,128)(2,1)S(1)}, bf16[2,2,128,128]{3,2,1,0:T(8,128)(2,1)S(1)}, u32[]{:S(2)}, u32[]{:S(2)}) collective-permute-start(bf16[2,2,128,128]{3,2,1,0:T(8,128)(2,1)S(1)} %pad_maximum_fusion.1), channel_id=1, source_target_pairs={{0,1},{1,2},{2,3},{3,4},{4,5},{5,6},{6,7},{8,9},{9,10},{10,11},{11... | collective-permute-start | bytes 393224 | tf_op jit(solution)/shard_map/ppermute | solution.py:178
  89.2 1.3 collective-permute-start.7
  90.5 3.7 %collective-permute-done.5 = bf16[2,2,128,128]{3,2,1,0:T(8,128)(2,1)S(1)} collective-permute-done((bf16[2,2,128,128]{3,2,1,0:T(8,128)(2,1)S(1)}, bf16[2,2,128,128]{3,2,1,0:T(8,128)(2,1)S(1)}, u32[]{:S(2)}, u32[]{:S(2)}) %collective-permute-start.5) | collective-permute-done | bytes 131104 | tf_op jit(solution)/shard_map/ppermute | solution.py:178
  94.2 0.7 subtract_convert_fusion.1
  94.9 0.0 collective-permute-done.6
  94.9 1.5 %collective-permute-done.7 = bf16[2,128,128]{2,1,0:T(8,128)(2,1)S(1)} collective-permute-done((bf16[2,128,128]{2,1,0:T(8,128)(2,1)S(1)}, bf16[2,128,128]{2,1,0:T(8,128)(2,1)S(1)}, u32[]{:S(2)}, u32[]{:S(2)}) %collective-permute-start.7) | collective-permute-done | bytes 65568 | tf_op jit(solution)/shard_map/ppermute | solution.py:178
  96.4 0.1 pad_maximum_fusion.2
  96.5 25.7 %all_to_all.20 = bf16[64,8,128]{2,1,0:T(8,128)(2,1)S(1)} all-to-all(bf16[64,8,128]{2,1,0:T(8,128)(2,1)S(1)} %pad_maximum_fusion.2), channel_id=1, replica_groups=mesh['view'=64,'strip'=8] {'view'}, dimensions={0} | all-to-all | bytes 262144 | tf_op jit(solution)/shard_map/all_to_all | solution.py:192
  122.2 1.5 %shard_map.98 = bf16[256,128]{1,0:T(8,128)(2,1)S(1)} custom-call(bf16[512,128]{1,0:T(8,128)(2,1)S(1)} %bitcast.96, bf16[64,2112]{1,0:T(8,128)(2,1)S(1)} %get-tuple-element.4.refs_1_), custom_call_target="tpu_custom_call" | custom-call | tf_op jit(solution)/shard_map/pallas_call | solution.py:161
  123.7 18.3 %all_to_all.21 = bf16[64,4,128]{2,1,0:T(4,128)(2,1)S(1)} all-to-all(bf16[64,4,128]{2,1,0:T(4,128)(2,1)S(1)} %bitcast.99), channel_id=1, replica_groups=mesh['view'=64,'strip'=8] {'view'}, dimensions={0} | all-to-all | bytes 131072 | tf_op jit(solution)/shard_map/all_to_all | solution.py:199
  142.0 0.6 fusion.8
  (10 shorter events, 0.2 us)
Async XLA Ops:
  0.6 14.3 %collective-permute-start.2 = (bf16[2,128,128]{2,1,0:T(8,128)(2,1)}, bf16[2,128,128]{2,1,0:T(8,128)(2,1)S(1)}, u32[]{:S(2)}, u32[]{:S(2)}) collective-permute-start(bf16[2,128,128]{2,1,0:T(8,128)(2,1)} %bitcast.106), channel_id=1, source_target_pairs={{1,0},{2,1},{3,2},{4,3},{5,4},{6,5},{7,6},{9,8},{10,9},{11,10},{12... | collective-permute-start | bytes 196616 | tf_op jit(solution)/shard_map/ppermute | solution.py:178
  5.5 9.5 %collective-permute-start.3 = (bf16[2,128,128]{2,1,0:T(8,128)(2,1)}, bf16[2,128,128]{2,1,0:T(8,128)(2,1)S(1)}, u32[]{:S(2)}, u32[]{:S(2)}) collective-permute-start(bf16[2,128,128]{2,1,0:T(8,128)(2,1)} %bitcast.107), channel_id=1, source_target_pairs={{0,1},{1,2},{2,3},{3,4},{4,5},{5,6},{6,7},{8,9},{9,10},{10,11},{11... | collective-permute-start | bytes 196616 | tf_op jit(solution)/shard_map/ppermute | solution.py:178
  7.4 25.9 %collective-permute-start = (f32[2,128,128]{2,1,0:T(8,128)}, f32[2,128,128]{2,1,0:T(8,128)S(1)}, u32[]{:S(2)}, u32[]{:S(2)}) collective-permute-start(f32[2,128,128]{2,1,0:T(8,128)} %bitcast.97), channel_id=1, source_target_pairs={{1,0},{2,1},{3,2},{4,3},{5,4},{6,5},{7,6},{9,8},{10,9},{11,10},{12... | collective-permute-start | bytes 393224 | tf_op jit(solution)/shard_map/ppermute | solution.py:178
  14.4 0.8 copy-start.6
  14.7 18.6 %copy-start = (bf16[2,2,256,256]{3,2,1,0:T(8,128)(2,1)S(1)}, bf16[2,2,256,256]{3,2,1,0:T(8,128)(2,1)}, u32[]{:S(2)}) copy-start(bf16[2,2,256,256]{3,2,1,0:T(8,128)(2,1)} %constant.45.clone.tables) | copy-start | bytes 1572868
  14.7 18.6 %copy-start.1 = (f32[1,4,128,128]{3,2,1,0:T(8,128)S(1)}, f32[1,4,128,128]{3,2,1,0:T(8,128)}, u32[]{:S(2)}) copy-start(f32[1,4,128,128]{3,2,1,0:T(8,128)} %param.11) | copy-start | bytes 786436
  14.7 18.6 %copy-start.2 = (f32[1,2,128,128]{3,2,1,0:T(8,128)S(1)}, f32[1,2,128,128]{3,2,1,0:T(8,128)}, u32[]{:S(2)}) copy-start(f32[1,2,128,128]{3,2,1,0:T(8,128)} %param.9) | copy-start | bytes 393220
  14.8 18.6 %copy-start.3 = (f32[2,128,128]{2,1,0:T(8,128)S(1)}, f32[2,128,128]{2,1,0:T(8,128)}, u32[]{:S(2)}) copy-start(f32[2,128,128]{2,1,0:T(8,128)} %probe.3) | copy-start | bytes 393220
  14.8 18.6 %copy-start.4 = (s32[1,4]{1,0:T(1,128)S(1)}, s32[1,4]{1,0:T(1,128)}, u32[]{:S(2)}) copy-start(s32[1,4]{1,0:T(1,128)} %param.12) | copy-start | bytes 52
  16.0 34.3 %all-to-all-start = ((bf16[64,8,128]{2,1,0:T(8,128)(2,1)}), bf16[64,8,128]{2,1,0:T(8,128)(2,1)S(1)}, u32[]{:S(2)}, u32[]{:S(2)}) async-start(bf16[64,8,128]{2,1,0:T(8,128)(2,1)} %pad_maximum_fusion), calls=%async_computation | async-start | bytes 262144 | tf_op jit(solution)/shard_map/all_to_all | solution.py:192
  33.3 38.3 %copy-start.5 = (f32[1,2,128,128]{3,2,1,0:T(8,128)S(1)}, f32[1,2,128,128]{3,2,1,0:T(8,128)}, u32[]{:S(2)}) copy-start(f32[1,2,128,128]{3,2,1,0:T(8,128)} %param.10) | copy-start | bytes 393220
  52.4 19.2 %all-to-all-start.1 = ((bf16[64,4,128]{2,1,0:T(4,128)(2,1)}), bf16[64,4,128]{2,1,0:T(4,128)(2,1)S(1)}, u32[]{:S(2)}, u32[]{:S(2)}) async-start(bf16[64,4,128]{2,1,0:T(4,128)(2,1)} %bitcast.9), calls=%async_computation.1 | async-start | bytes 131072 | tf_op jit(solution)/shard_map/all_to_all | solution.py:199
  56.9 9.1 %collective-permute-start.1 = (f32[2,128,128]{2,1,0:T(8,128)S(1)}, f32[2,128,128]{2,1,0:T(8,128)S(1)}, u32[]{:S(2)}, u32[]{:S(2)}) collective-permute-start(f32[2,128,128]{2,1,0:T(8,128)S(1)} %slice_bitcast_fusion), channel_id=1, source_target_pairs={{0,1},{1,2},{2,3},{3,4},{4,5},{5,6},{6,7},{8,9},{9,10},{10,11},{11... | collective-permute-start | bytes 393224 | tf_op jit(solution)/shard_map/ppermute | solution.py:178
  71.7 8.1 %collective-permute-start.4 = (f32[2,128,128]{2,1,0:T(8,128)S(1)}, f32[2,128,128]{2,1,0:T(8,128)S(1)}, u32[]{:S(2)}, u32[]{:S(2)}) collective-permute-start(f32[2,128,128]{2,1,0:T(8,128)S(1)} %fusion.7.own), channel_id=1, source_target_pairs={{1,0},{2,1},{3,2},{4,3},{5,4},{6,5},{7,6},{9,8},{10,9},{11,10},{12... | collective-permute-start | bytes 393224 | tf_op jit(solution)/shard_map/ppermute | solution.py:178
  82.4 12.6 %collective-permute-start.6 = (bf16[2,128,128]{2,1,0:T(8,128)(2,1)S(1)}, bf16[2,128,128]{2,1,0:T(8,128)(2,1)S(1)}, u32[]{:S(2)}, u32[]{:S(2)}) collective-permute-start(bf16[2,128,128]{2,1,0:T(8,128)(2,1)S(1)} %subtract_convert_fusion.2), channel_id=1, source_target_pairs={{1,0},{2,1},{3,2},{4,3},{5,4},{6,5},{7,6},{9,8},{10,9},{11,10},{12... | collective-permute-start | bytes 196616 | tf_op jit(solution)/shard_map/ppermute | solution.py:178
  86.0 8.2 %collective-permute-start.5 = (bf16[2,2,128,128]{3,2,1,0:T(8,128)(2,1)S(1)}, bf16[2,2,128,128]{3,2,1,0:T(8,128)(2,1)S(1)}, u32[]{:S(2)}, u32[]{:S(2)}) collective-permute-start(bf16[2,2,128,128]{3,2,1,0:T(8,128)(2,1)S(1)} %pad_maximum_fusion.1), channel_id=1, source_target_pairs={{0,1},{1,2},{2,3},{3,4},{4,5},{5,6},{6,7},{8,9},{9,10},{10,11},{11... | collective-permute-start | bytes 393224 | tf_op jit(solution)/shard_map/ppermute | solution.py:178
  89.2 7.2 %collective-permute-start.7 = (bf16[2,128,128]{2,1,0:T(8,128)(2,1)S(1)}, bf16[2,128,128]{2,1,0:T(8,128)(2,1)S(1)}, u32[]{:S(2)}, u32[]{:S(2)}) collective-permute-start(bf16[2,128,128]{2,1,0:T(8,128)(2,1)S(1)} %fusion.24), channel_id=1, source_target_pairs={{0,2},{1,3},{2,4},{3,5},{4,6},{5,7},{8,10},{9,11},{10,12},{11,13},... | collective-permute-start | bytes 196616 | tf_op jit(solution)/shard_map/ppermute | solution.py:178

commit v2 on v1

--- a/solution.py
+++ b/solution.py
@@ -136,37 +136,46 @@
     )(starts, own, following, measured, probe, tables)
 
 
-def shear_kernel(scale, lines, source, choice, out, plain, taps, result):
+def shear_kernel(scale, lines, into, source, choice, out, plain, taps, result):
     channels = choice.shape[0]
     side = source.shape[1]
+    pieces = source.shape[0] // (lines * channels)
+    span = into * side
     plain[...] = source[...].astype(f32)
     for r in range(lines):
-        near = plain[pl.ds(r, channels, stride=2 * lines), :]
-        edge = plain[pl.ds(lines + r, channels, stride=2 * lines), :]
+        near = plain[pl.ds(r, channels, stride=pieces * lines), :]
+        if pieces == 1:
+            edge = jnp.zeros_like(near)
+        else:
+            edge = plain[pl.ds(lines + r, channels, stride=pieces * lines), :]
         wide = jnp.concatenate([near, edge], axis=1)
         for d in range(TAPS):
-            moved = pltpu.roll(wide, (2 * side + HALO - d) % (2 * side), 1)[:, :side]
-            taps[d * channels : (d + 1) * channels, r * side : (r + 1) * side] = moved.astype(bf16)
+            moved = pltpu.roll(wide, (2 * side + HALO - d) % (2 * side), 1)[:, :span]
+            taps[d * channels : (d + 1) * channels, r * span : (r + 1) * span] = moved.astype(bf16)
     summed = dot(choice[...], taps[...]) * scale
     for r in range(lines):
-        result[pl.ds(r, channels, stride=lines), :] = summed[:, r * side : (r + 1) * side]
+        for j in range(into):
+            begin = r * span + j * side
+            result[pl.ds(j * lines + r, channels, stride=into * lines), :] = summed[
+                :, begin : begin + side
+            ]
     out[...] = result[...].astype(bf16)
 
 
-def shear_sum(source, choice, scale):
+def shear_sum(source, choice, scale, lines, into):
     channels = choice.shape[0]
     side = source.shape[1]
-    lines = source.shape[0] // (2 * channels)
+    pieces = source.shape[0] // (lines * channels)
     vmem = pl.BlockSpec(memory_space=pltpu.VMEM)
     return pl.pallas_call(
-        lambda *refs: shear_kernel(scale, lines, *refs),
-        out_shape=jax.ShapeDtypeStruct((lines * channels, side), bf16),
+        lambda *refs: shear_kernel(scale, lines, into, *refs),
+        out_shape=jax.ShapeDtypeStruct((into * lines * channels, side), bf16),
         in_specs=[vmem] * 2,
         out_specs=vmem,
         scratch_shapes=[
-            pltpu.VMEM((2 * lines * channels, side), f32),
-            pltpu.VMEM((TAPS * channels, lines * side), bf16),
-            pltpu.VMEM((lines * channels, side), f32),
+            pltpu.VMEM((pieces * lines * channels, side), f32),
+            pltpu.VMEM((TAPS * channels, into * lines * side), bf16),
+            pltpu.VMEM((into * lines * channels, side), f32),
         ],
         compiler_params=pltpu.CompilerParams(vmem_limit_bytes=32 * 1024 * 1024),
     )(source, choice)
@@ -183,14 +192,12 @@
     return jnp.where(lane < value.shape[-1] // 2, after, before)
 
 
-def exchange(own, edge, groups):
-    side = own.shape[-1]
-    lines = own.size // (groups * side)
-    parcel = jnp.concatenate(
-        [own.reshape(groups, lines, side), edge.reshape(groups, lines, side)], axis=1
-    )
+def exchange(parts, groups):
+    side = parts[0].shape[-1]
+    lines = parts[0].size // (groups * side)
+    parcel = jnp.concatenate([part.reshape(groups, lines, side) for part in parts], axis=1)
     got = lax.all_to_all(parcel, "view", 0, 0, tiled=True)
-    return got.reshape(groups * 2 * lines, side)
+    return got.reshape(groups * len(parts) * lines, side)
 
 
 def give_back(value, groups):
@@ -222,17 +229,31 @@
         (-shift.T[:, None, :] == tap[None, :, None]).astype(bf16).reshape(slices, TAPS * slices)
     )
 
-    slab_edge = with_edges(own_slab, strip_move(own_slab, 1), strip_move(own_slab, -1))
+    lines = shape[0] * shape[1] // slices
+    last = lax.axis_index("strip") == lax.axis_size("strip") - 1
+    first = lax.axis_index("strip") == 0
     following = strip_move(psi, -1)
-    lined = exchange(own_slab, slab_edge, slices)
+    lined = exchange([own_slab], slices)
     spread = gradient(starts, psi, following, measured, probe, tables)
+    sums = shear_sum(lined, choice_project, root_scale, lines, 2)
+    sums, spread = lax.optimization_barrier((sums, spread))
     spill = strip_move(spread[1], 1)
-    sums = shear_sum(lined, choice_project, root_scale)
-    projected = give_back(sums, slices).reshape(shape).astype(f32)
+    sums = give_back(sums, slices)
+    projected = sums[:, :lines].reshape(shape).astype(f32)
+    beyond = sums[:, lines:].reshape(shape)
     pull = projected - own_dual
     psi = psi + step_size * (spread[0] + spill) + coupling * (pull - psi)
 
-    following = strip_move(psi, -1)
+    beyond_up = strip_move(beyond, 1)
+    beyond_two = strip_move(beyond, -2)
+    down = strip_move(jnp.stack([psi.astype(bf16), beyond]), -1)
+    gain = with_edges(beyond, down[1], beyond_up).astype(f32)
+    pull = pull + gain
+    psi = psi + coupling * gain
+    following = down[0].astype(f32) + coupling * with_edges(
+        beyond, beyond_two, beyond
+    ).astype(f32)
+    following = jnp.where(last, 0.0, following)
     spread = gradient(starts, psi, following, measured, probe, tables)
     part = psi + step_size * spread[0] + coupling * (pull - psi)
     rest = (pull - part).astype(bf16)
@@ -248,13 +269,11 @@
         (up[0].astype(f32) - up_two.astype(f32)).astype(bf16),
         (down.astype(f32) - outer.astype(f32)).astype(bf16),
     )
-    last = lax.axis_index("strip") == lax.axis_size("strip") - 1
-    first = lax.axis_index("strip") == 0
     lane = lax.broadcasted_iota(jnp.int32, shape, 2)
     outside = (last & (lane < shape[2] // 2)) | (first & (lane >= shape[2] // 2))
     residual_edge = jnp.where(outside, jnp.zeros_like(residual_edge), residual_edge)
-    lined = exchange(residual, residual_edge, slices)
-    sums = shear_sum(lined, choice_back, descent * root_scale)
+    lined = exchange([residual, residual_edge], slices)
+    sums = shear_sum(lined, choice_back, descent * root_scale, lines, 1)
     backward = give_back(sums, slices).reshape(shape).astype(f32)
     slab_new = (own_slab.astype(f32) - backward).astype(bf16)
     return (psi[None], slab_new[None])

time: 143 us -> 138 us (0.965)
  waiting for transfers between devices: 37 us -> 29 us
  starting transfers between devices: 47.5 us -> 52.6 us
    all_to_all x1, waiting for transfers between devices: 14.4 us -> 3.52 us  [exchange(): got = lax.all_to_all(parcel, 'view', 0, 0, tiled=True)]
    all_to_all x1, waiting for transfers between devices: 5.62 us -> 15.2 us  [give_back(): return lax.all_to_all(parcel, 'view', 0, 0, tiled=True)]
    ppermute x8, waiting for transfers between devices: 17 us -> 10.3 us  [strip_move(): return lax.ppermute(value, 'strip', pairs)]
    all_to_all x1, starting transfers between devices: 4.44 us -> 10.8 us  [give_back(): return lax.all_to_all(parcel, 'view', 0, 0, tiled=True)]
  transfers between devices with their start and end apart: 10 -> 10, of which waited for: 6 -> 5; matrix products, arithmetic and copies ran while one was open for 2% -> 2% of each run, Pallas kernels for 2% -> 2%
where the time goes in v2:
time: 138 us
  starting transfers between devices  52.6 us (38%)
  blocking collectives  43.4 us (31%)
  waiting for transfers between devices  29 us (21%)
  Pallas kernels  8.36 us (6%)
  other arithmetic  2.6 us (2%)
    all_to_all x1, blocking collectives, exchange(): got = lax.all_to_all(parcel, 'view', 0, 0, tiled=True)  25.1 us
    ppermute x8, starting transfers between devices, strip_move(): return lax.ppermute(value, 'strip', pairs)  24.5 us
    all_to_all x1, blocking collectives, give_back(): return lax.all_to_all(parcel, 'view', 0, 0, tiled=True)  18.3 us
    all_to_all x1, starting transfers between devices, exchange(): got = lax.all_to_all(parcel, 'view', 0, 0, tiled=True)  17.3 us
    all_to_all x1, waiting for transfers between devices, give_back(): return lax.all_to_all(parcel, 'view', 0, 0, tiled=True)  15.2 us
    all_to_all x1, starting transfers between devices, give_back(): return lax.all_to_all(parcel, 'view', 0, 0, tiled=True)  10.8 us
    ppermute x8, waiting for transfers between devices, strip_move(): return lax.ppermute(value, 'strip', pairs)  10.3 us
    pallas_call x2, Pallas kernels, gradient(): pl.pallas_call(gradient_kernel, out_shape=jax.ShapeDtypeStruct((2,) + own...  5.07 us
  transfers between devices with their start and end apart: 10, of which 5 were waited for; matrix products, arithmetic and copies ran while one was open for 2% of the time, Pallas kernels for 2%

profile of v2, /device:TPU:25, one launch (start us, length us, event | category | flops | bytes accessed | tf_op | source)
XLA Modules:
  0.0 137.9 jit_solution(9585969982830635568)
XLA Ops:
  0.6 17.3 %all-to-all-start = ((bf16[64,4,128]{2,1,0:T(4,128)(2,1)}), bf16[64,4,128]{2,1,0:T(4,128)(2,1)S(1)}, u32[]{:S(2)}, u32[]{:S(2)}) async-start(bf16[64,4,128]{2,1,0:T(4,128)(2,1)} %bitcast.104), calls=%async_computation | async-start | bytes 131072 | tf_op jit(solution)/shard_map/all_to_all | solution.py:199
  17.9 4.5 %collective-permute-start = (f32[2,128,128]{2,1,0:T(8,128)}, f32[2,128,128]{2,1,0:T(8,128)S(1)}, u32[]{:S(2)}, u32[]{:S(2)}) collective-permute-start(f32[2,128,128]{2,1,0:T(8,128)} %bitcast.92), channel_id=1, source_target_pairs={{1,0},{2,1},{3,2},{4,3},{5,4},{6,5},{7,6},{9,8},{10,9},{11,10},{12... | collective-permute-start | bytes 393224 | tf_op jit(solution)/shard_map/ppermute | solution.py:187
  22.5 0.7 multiply_add_fusion
  23.1 0.1 fusion.17
  23.2 0.1 eq.46
  23.3 0.3 eq.47
  23.6 0.1 eq.54
  23.7 0.3 eq.55
  24.0 0.0 copy-start
  24.0 0.0 copy-start.1
  24.0 0.0 copy-start.2
  24.0 0.0 copy-start.3
  24.0 0.0 copy-start.4
  24.0 0.1 eq.48
  24.1 0.1 eq.49
  24.2 0.1 compare_convert_fusion
  24.3 2.1 %collective-permute-done.following = f32[2,128,128]{2,1,0:T(8,128)S(1)} collective-permute-done((f32[2,128,128]{2,1,0:T(8,128)}, f32[2,128,128]{2,1,0:T(8,128)S(1)}, u32[]{:S(2)}, u32[]{:S(2)}) %collective-permute-start) | collective-permute-done | bytes 131104 | tf_op jit(solution)/shard_map/ppermute | solution.py:187
  26.4 0.0 copy-done
  26.4 0.0 copy-done.1
  26.4 0.0 copy-done.2
  26.4 0.0 copy-done.3
  26.4 0.0 copy-done.4
  26.4 0.0 copy-start.5
  26.4 2.5 %shard_map.96 = f32[2,2,128,128]{3,2,1,0:T(8,128)S(1)} custom-call(s32[4]{0:T(128)S(1)} %bitcast.96, f32[2,128,128]{2,1,0:T(8,128)S(1)} %bitcast.93, f32[2,128,128]{2,1,0:T(8,128)S(1)} %collective-permute-done.following, f32[4,128,128]{2,1,0:T(8,128)S(1)} %bitcast.89, f32[2,128,128]{2,1,0:T(8,128)S(1)} %copy-done.3, bf16[2,2,256,256]{3,2,1,0:T(8,128)(2,1)S(1)} %copy-done), custom_call_target="tpu_custom_call" | custom-call | tf_op jit(solution)/shard_map/pallas_call | solution.py:130
  29.0 3.5 %all-to-all-done = bf16[64,4,128]{2,1,0:T(4,128)(2,1)S(1)} async-done(((bf16[64,4,128]{2,1,0:T(4,128)(2,1)}), bf16[64,4,128]{2,1,0:T(4,128)(2,1)S(1)}, u32[]{:S(2)}, u32[]{:S(2)}) %all-to-all-start) | async-done | bytes 65568 | tf_op jit(solution)/shard_map/all_to_all | solution.py:199
  32.5 1.8 %shard_map.95 = bf16[512,128]{1,0:T(8,128)(2,1)} custom-call(bf16[256,128]{1,0:T(8,128)(2,1)S(1)} %bitcast.94, bf16[64,2112]{1,0:T(8,128)(2,1)S(1)} %get-tuple-element.17.refs_1_), custom_call_target="tpu_custom_call" | custom-call | tf_op jit(solution)/shard_map/pallas_call | solution.py:170
  34.3 10.8 %all-to-all-start.1 = ((bf16[64,8,128]{2,1,0:T(8,128)(2,1)}), bf16[64,8,128]{2,1,0:T(8,128)(2,1)S(1)}, u32[]{:S(2)}, u32[]{:S(2)}) async-start(bf16[64,8,128]{2,1,0:T(8,128)(2,1)} %bitcast.7), calls=%async_computation.1 | async-start | bytes 262144 | tf_op jit(solution)/shard_map/all_to_all | solution.py:206
  45.2 1.9 %collective-permute-start.1 = (f32[2,128,128]{2,1,0:T(8,128)S(1)}, f32[2,128,128]{2,1,0:T(8,128)S(1)}, u32[]{:S(2)}, u32[]{:S(2)}) collective-permute-start(f32[2,128,128]{2,1,0:T(8,128)S(1)} %slice_bitcast_fusion), channel_id=1, source_target_pairs={{0,1},{1,2},{2,3},{3,4},{4,5},{5,6},{6,7},{8,9},{9,10},{10,11},{11... | collective-permute-start | bytes 393224 | tf_op jit(solution)/shard_map/ppermute | solution.py:187
  47.1 15.2 %all-to-all-done.1 = bf16[64,8,128]{2,1,0:T(8,128)(2,1)S(1)} async-done(((bf16[64,8,128]{2,1,0:T(8,128)(2,1)}), bf16[64,8,128]{2,1,0:T(8,128)(2,1)S(1)}, u32[]{:S(2)}, u32[]{:S(2)}) %all-to-all-start.1) | async-done | bytes 131104 | tf_op jit(solution)/shard_map/all_to_all | solution.py:206
  62.3 0.0 collective-permute-done.1
  62.3 0.0 copy-done.5
  62.4 5.4 %collective-permute-start.3 = (bf16[2,2,128,128]{3,2,1,0:T(8,128)(2,1)S(1)}, bf16[2,2,128,128]{3,2,1,0:T(8,128)(2,1)S(1)}, u32[]{:S(2)}, u32[]{:S(2)}) collective-permute-start(bf16[2,2,128,128]{3,2,1,0:T(8,128)(2,1)S(1)} %pad_maximum_fusion), channel_id=1, source_target_pairs={{1,0},{2,1},{3,2},{4,3},{5,4},{6,5},{7,6},{9,8},{10,9},{11,10},{12... | collective-permute-start | bytes 393224 | tf_op jit(solution)/shard_map/ppermute | solution.py:187
  67.9 1.9 %collective-permute-start.2 = (bf16[2,128,128]{2,1,0:T(8,128)(2,1)S(1)}, bf16[2,128,128]{2,1,0:T(8,128)(2,1)S(1)}, u32[]{:S(2)}, u32[]{:S(2)}) collective-permute-start(bf16[2,128,128]{2,1,0:T(8,128)(2,1)S(1)} %bitcast.101), channel_id=1, source_target_pairs={{0,1},{1,2},{2,3},{3,4},{4,5},{5,6},{6,7},{8,9},{9,10},{10,11},{11... | collective-permute-start | bytes 196616 | tf_op jit(solution)/shard_map/ppermute | solution.py:187
  69.8 2.2 %collective-permute-start.4 = (bf16[2,128,128]{2,1,0:T(8,128)(2,1)S(1)}, bf16[2,128,128]{2,1,0:T(8,128)(2,1)S(1)}, u32[]{:S(2)}, u32[]{:S(2)}) collective-permute-start(bf16[2,128,128]{2,1,0:T(8,128)(2,1)S(1)} %bitcast.102), channel_id=1, source_target_pairs={{2,0},{3,1},{4,2},{5,3},{6,4},{7,5},{10,8},{11,9},{12,10},{13,11},... | collective-permute-start | bytes 196616 | tf_op jit(solution)/shard_map/ppermute | solution.py:187
  72.0 3.3 %collective-permute-done.2 = bf16[2,128,128]{2,1,0:T(8,128)(2,1)S(1)} collective-permute-done((bf16[2,128,128]{2,1,0:T(8,128)(2,1)S(1)}, bf16[2,128,128]{2,1,0:T(8,128)(2,1)S(1)}, u32[]{:S(2)}, u32[]{:S(2)}) %collective-permute-start.2) | collective-permute-done | bytes 65568 | tf_op jit(solution)/shard_map/ppermute | solution.py:187
  75.3 0.0 collective-permute-done.4
  75.3 0.0 collective-permute-done.3
  75.3 0.1 fusion.7
  75.4 2.5 %shard_map.97 = f32[2,2,128,128]{3,2,1,0:T(8,128)S(1)} custom-call(s32[4]{0:T(128)S(1)} %bitcast.97, f32[2,128,128]{2,1,0:T(8,128)S(1)} %get-tuple-element.13.own, f32[2,128,128]{2,1,0:T(8,128)S(1)} %get-tuple-element.12.following, f32[4,128,128]{2,1,0:T(8,128)S(1)} %bitcast.90, f32[2,128,128]{2,1,0:T(8,128)S(1)} %copy-done.3, ...), custom_call_target="tpu_custom_call" | custom-call | tf_op jit(solution)/shard_map/pallas_call | solution.py:130
  77.9 0.1 subtract_convert_fusion.2
  78.0 5.3 %collective-permute-start.6 = (bf16[2,128,128]{2,1,0:T(8,128)(2,1)S(1)}, bf16[2,128,128]{2,1,0:T(8,128)(2,1)S(1)}, u32[]{:S(2)}, u32[]{:S(2)}) collective-permute-start(bf16[2,128,128]{2,1,0:T(8,128)(2,1)S(1)} %get-tuple-element.6), channel_id=1, source_target_pairs={{1,0},{2,1},{3,2},{4,3},{5,4},{6,5},{7,6},{9,8},{10,9},{11,10},{12... | collective-permute-start | bytes 196616 | tf_op jit(solution)/shard_map/ppermute | solution.py:187
  83.3 0.0 copy-start.6
  83.3 1.9 %collective-permute-start.5 = (bf16[2,2,128,128]{3,2,1,0:T(8,128)(2,1)S(1)}, bf16[2,2,128,128]{3,2,1,0:T(8,128)(2,1)S(1)}, u32[]{:S(2)}, u32[]{:S(2)}) collective-permute-start(bf16[2,2,128,128]{3,2,1,0:T(8,128)(2,1)S(1)} %pad_maximum_fusion.1), channel_id=1, source_target_pairs={{0,1},{1,2},{2,3},{3,4},{4,5},{5,6},{6,7},{8,9},{9,10},{10,11},{11... | collective-permute-start | bytes 393224 | tf_op jit(solution)/shard_map/ppermute | solution.py:187
  85.3 1.3 collective-permute-start.7
  86.6 5.0 %collective-permute-done.5 = bf16[2,2,128,128]{3,2,1,0:T(8,128)(2,1)S(1)} collective-permute-done((bf16[2,2,128,128]{3,2,1,0:T(8,128)(2,1)S(1)}, bf16[2,2,128,128]{3,2,1,0:T(8,128)(2,1)S(1)}, u32[]{:S(2)}, u32[]{:S(2)}) %collective-permute-start.5) | collective-permute-done | bytes 131104 | tf_op jit(solution)/shard_map/ppermute | solution.py:187
  91.6 0.7 subtract_convert_fusion.1
  92.3 0.0 collective-permute-done.6
  92.3 0.0 collective-permute-done.7
  92.3 0.1 pad_maximum_fusion.2
  92.4 25.1 %all_to_all.20 = bf16[64,8,128]{2,1,0:T(8,128)(2,1)S(1)} all-to-all(bf16[64,8,128]{2,1,0:T(8,128)(2,1)S(1)} %pad_maximum_fusion.2), channel_id=1, replica_groups=mesh['view'=64,'strip'=8] {'view'}, dimensions={0} | all-to-all | bytes 262144 | tf_op jit(solution)/shard_map/all_to_all | solution.py:199
  117.5 1.5 %shard_map.98 = bf16[256,128]{1,0:T(8,128)(2,1)S(1)} custom-call(bf16[512,128]{1,0:T(8,128)(2,1)S(1)} %bitcast.91, bf16[64,2112]{1,0:T(8,128)(2,1)S(1)} %get-tuple-element.16.refs_1_), custom_call_target="tpu_custom_call" | custom-call | tf_op jit(solution)/shard_map/pallas_call | solution.py:170
  119.0 18.3 %all_to_all.21 = bf16[64,4,128]{2,1,0:T(4,128)(2,1)S(1)} all-to-all(bf16[64,4,128]{2,1,0:T(4,128)(2,1)S(1)} %bitcast.95), channel_id=1, replica_groups=mesh['view'=64,'strip'=8] {'view'}, dimensions={0} | all-to-all | bytes 131072 | tf_op jit(solution)/shard_map/all_to_all | solution.py:206
  137.3 0.0 copy-done.6
  137.3 0.7 fusion.5
  (11 shorter events, 0.2 us)
Async XLA Ops:
  0.6 31.9 %all-to-all-start = ((bf16[64,4,128]{2,1,0:T(4,128)(2,1)}), bf16[64,4,128]{2,1,0:T(4,128)(2,1)S(1)}, u32[]{:S(2)}, u32[]{:S(2)}) async-start(bf16[64,4,128]{2,1,0:T(4,128)(2,1)} %bitcast.104), calls=%async_computation | async-start | bytes 131072 | tf_op jit(solution)/shard_map/all_to_all | solution.py:199
  17.9 8.5 %collective-permute-start = (f32[2,128,128]{2,1,0:T(8,128)}, f32[2,128,128]{2,1,0:T(8,128)S(1)}, u32[]{:S(2)}, u32[]{:S(2)}) collective-permute-start(f32[2,128,128]{2,1,0:T(8,128)} %bitcast.92), channel_id=1, source_target_pairs={{1,0},{2,1},{3,2},{4,3},{5,4},{6,5},{7,6},{9,8},{10,9},{11,10},{12... | collective-permute-start | bytes 393224 | tf_op jit(solution)/shard_map/ppermute | solution.py:187
  24.0 2.4 %copy-start = (bf16[2,2,256,256]{3,2,1,0:T(8,128)(2,1)S(1)}, bf16[2,2,256,256]{3,2,1,0:T(8,128)(2,1)}, u32[]{:S(2)}) copy-start(bf16[2,2,256,256]{3,2,1,0:T(8,128)(2,1)} %constant.47.clone.tables) | copy-start | bytes 1572868
  24.0 2.4 %copy-start.1 = (f32[1,4,128,128]{3,2,1,0:T(8,128)S(1)}, f32[1,4,128,128]{3,2,1,0:T(8,128)}, u32[]{:S(2)}) copy-start(f32[1,4,128,128]{3,2,1,0:T(8,128)} %param.11) | copy-start | bytes 786436
  24.0 2.4 %copy-start.2 = (f32[1,2,128,128]{3,2,1,0:T(8,128)S(1)}, f32[1,2,128,128]{3,2,1,0:T(8,128)}, u32[]{:S(2)}) copy-start(f32[1,2,128,128]{3,2,1,0:T(8,128)} %param.9) | copy-start | bytes 393220
  24.0 2.4 %copy-start.3 = (f32[2,128,128]{2,1,0:T(8,128)S(1)}, f32[2,128,128]{2,1,0:T(8,128)}, u32[]{:S(2)}) copy-start(f32[2,128,128]{2,1,0:T(8,128)} %probe.3) | copy-start | bytes 393220
  24.0 2.4 %copy-start.4 = (s32[1,4]{1,0:T(1,128)S(1)}, s32[1,4]{1,0:T(1,128)}, u32[]{:S(2)}) copy-start(s32[1,4]{1,0:T(1,128)} %param.12) | copy-start | bytes 52
  26.4 35.9 %copy-start.5 = (f32[1,2,128,128]{3,2,1,0:T(8,128)S(1)}, f32[1,2,128,128]{3,2,1,0:T(8,128)}, u32[]{:S(2)}) copy-start(f32[1,2,128,128]{3,2,1,0:T(8,128)} %param.10) | copy-start | bytes 393220
  34.3 28.0 %all-to-all-start.1 = ((bf16[64,8,128]{2,1,0:T(8,128)(2,1)}), bf16[64,8,128]{2,1,0:T(8,128)(2,1)S(1)}, u32[]{:S(2)}, u32[]{:S(2)}) async-start(bf16[64,8,128]{2,1,0:T(8,128)(2,1)} %bitcast.7), calls=%async_computation.1 | async-start | bytes 262144 | tf_op jit(solution)/shard_map/all_to_all | solution.py:206
  45.2 17.2 %collective-permute-start.1 = (f32[2,128,128]{2,1,0:T(8,128)S(1)}, f32[2,128,128]{2,1,0:T(8,128)S(1)}, u32[]{:S(2)}, u32[]{:S(2)}) collective-permute-start(f32[2,128,128]{2,1,0:T(8,128)S(1)} %slice_bitcast_fusion), channel_id=1, source_target_pairs={{0,1},{1,2},{2,3},{3,4},{4,5},{5,6},{6,7},{8,9},{9,10},{10,11},{11... | collective-permute-start | bytes 393224 | tf_op jit(solution)/shard_map/ppermute | solution.py:187
  62.4 12.9 %collective-permute-start.3 = (bf16[2,2,128,128]{3,2,1,0:T(8,128)(2,1)S(1)}, bf16[2,2,128,128]{3,2,1,0:T(8,128)(2,1)S(1)}, u32[]{:S(2)}, u32[]{:S(2)}) collective-permute-start(bf16[2,2,128,128]{3,2,1,0:T(8,128)(2,1)S(1)} %pad_maximum_fusion), channel_id=1, source_target_pairs={{1,0},{2,1},{3,2},{4,3},{5,4},{6,5},{7,6},{9,8},{10,9},{11,10},{12... | collective-permute-start | bytes 393224 | tf_op jit(solution)/shard_map/ppermute | solution.py:187
  67.9 7.4 %collective-permute-start.2 = (bf16[2,128,128]{2,1,0:T(8,128)(2,1)S(1)}, bf16[2,128,128]{2,1,0:T(8,128)(2,1)S(1)}, u32[]{:S(2)}, u32[]{:S(2)}) collective-permute-start(bf16[2,128,128]{2,1,0:T(8,128)(2,1)S(1)} %bitcast.101), channel_id=1, source_target_pairs={{0,1},{1,2},{2,3},{3,4},{4,5},{5,6},{6,7},{8,9},{9,10},{10,11},{11... | collective-permute-start | bytes 196616 | tf_op jit(solution)/shard_map/ppermute | solution.py:187
  69.8 5.5 %collective-permute-start.4 = (bf16[2,128,128]{2,1,0:T(8,128)(2,1)S(1)}, bf16[2,128,128]{2,1,0:T(8,128)(2,1)S(1)}, u32[]{:S(2)}, u32[]{:S(2)}) collective-permute-start(bf16[2,128,128]{2,1,0:T(8,128)(2,1)S(1)} %bitcast.102), channel_id=1, source_target_pairs={{2,0},{3,1},{4,2},{5,3},{6,4},{7,5},{10,8},{11,9},{12,10},{13,11},... | collective-permute-start | bytes 196616 | tf_op jit(solution)/shard_map/ppermute | solution.py:187
  78.0 14.3 %collective-permute-start.6 = (bf16[2,128,128]{2,1,0:T(8,128)(2,1)S(1)}, bf16[2,128,128]{2,1,0:T(8,128)(2,1)S(1)}, u32[]{:S(2)}, u32[]{:S(2)}) collective-permute-start(bf16[2,128,128]{2,1,0:T(8,128)(2,1)S(1)} %get-tuple-element.6), channel_id=1, source_target_pairs={{1,0},{2,1},{3,2},{4,3},{5,4},{6,5},{7,6},{9,8},{10,9},{11,10},{12... | collective-permute-start | bytes 196616 | tf_op jit(solution)/shard_map/ppermute | solution.py:187
  83.3 54.0 %copy-start.6 = (bf16[1,2,128,128]{3,2,1,0:T(8,128)(2,1)S(1)}, bf16[1,2,128,128]{3,2,1,0:T(8,128)(2,1)}, u32[]{:S(2)}) copy-start(bf16[1,2,128,128]{3,2,1,0:T(8,128)(2,1)} %param.8) | copy-start | bytes 196612
  83.3 8.2 %collective-permute-start.5 = (bf16[2,2,128,128]{3,2,1,0:T(8,128)(2,1)S(1)}, bf16[2,2,128,128]{3,2,1,0:T(8,128)(2,1)S(1)}, u32[]{:S(2)}, u32[]{:S(2)}) collective-permute-start(bf16[2,2,128,128]{3,2,1,0:T(8,128)(2,1)S(1)} %pad_maximum_fusion.1), channel_id=1, source_target_pairs={{0,1},{1,2},{2,3},{3,4},{4,5},{5,6},{6,7},{8,9},{9,10},{10,11},{11... | collective-permute-start | bytes 393224 | tf_op jit(solution)/shard_map/ppermute | solution.py:187
  85.3 7.0 %collective-permute-start.7 = (bf16[2,128,128]{2,1,0:T(8,128)(2,1)S(1)}, bf16[2,128,128]{2,1,0:T(8,128)(2,1)S(1)}, u32[]{:S(2)}, u32[]{:S(2)}) collective-permute-start(bf16[2,128,128]{2,1,0:T(8,128)(2,1)S(1)} %fusion.28), channel_id=1, source_target_pairs={{0,2},{1,3},{2,4},{3,5},{4,6},{5,7},{8,10},{9,11},{10,12},{11,13},... | collective-permute-start | bytes 196616 | tf_op jit(solution)/shard_map/ppermute | solution.py:187

commit v3 on v2

--- a/solution.py
+++ b/solution.py
@@ -234,26 +234,24 @@
     first = lax.axis_index("strip") == 0
     following = strip_move(psi, -1)
     lined = exchange([own_slab], slices)
+    sums = shear_sum(lined, choice_project, root_scale, lines, 2)
+    sums, following = lax.optimization_barrier((sums, following))
+    sums = give_back(sums, slices)
     spread = gradient(starts, psi, following, measured, probe, tables)
-    sums = shear_sum(lined, choice_project, root_scale, lines, 2)
-    sums, spread = lax.optimization_barrier((sums, spread))
-    spill = strip_move(spread[1], 1)
-    sums = give_back(sums, slices)
     projected = sums[:, :lines].reshape(shape).astype(f32)
     beyond = sums[:, lines:].reshape(shape)
     pull = projected - own_dual
-    psi = psi + step_size * (spread[0] + spill) + coupling * (pull - psi)
-
-    beyond_up = strip_move(beyond, 1)
+    psi = psi + step_size * spread[0] + coupling * (pull - psi)
+    outer = step_size * spread[1]
+
     beyond_two = strip_move(beyond, -2)
+    up = strip_move(jnp.stack([outer.astype(bf16), beyond]), 1)
     down = strip_move(jnp.stack([psi.astype(bf16), beyond]), -1)
-    gain = with_edges(beyond, down[1], beyond_up).astype(f32)
+    gain = with_edges(beyond, down[1], up[1]).astype(f32)
     pull = pull + gain
-    psi = psi + coupling * gain
-    following = down[0].astype(f32) + coupling * with_edges(
-        beyond, beyond_two, beyond
-    ).astype(f32)
-    following = jnp.where(last, 0.0, following)
+    psi = psi + up[0].astype(f32) + coupling * gain
+    gain = with_edges(beyond, beyond_two, beyond).astype(f32)
+    following = jnp.where(last, 0.0, down[0].astype(f32) + outer + coupling * gain)
     spread = gradient(starts, psi, following, measured, probe, tables)
     part = psi + step_size * spread[0] + coupling * (pull - psi)
     rest = (pull - part).astype(bf16)

time: 138 us -> 133 us (0.964)
  blocking collectives: 43.4 us -> 23.3 us
  waiting for transfers between devices: 29 us -> 42 us
    all_to_all x1 -> x0, blocking collectives: 18.3 us -> none  [give_back(): return lax.all_to_all(parcel, 'view', 0, 0, tiled=True)]
    all_to_all x1 -> x2, waiting for transfers between devices: 15.2 us -> 28.6 us  [give_back(): return lax.all_to_all(parcel, 'view', 0, 0, tiled=True)]
    ppermute x8 -> x7, waiting for transfers between devices: 10.3 us -> 5.22 us  [strip_move(): return lax.ppermute(value, 'strip', pairs)]
    all_to_all x1, waiting for transfers between devices: 3.52 us -> 8.19 us  [exchange(): got = lax.all_to_all(parcel, 'view', 0, 0, tiled=True)]
    all_to_all x1, blocking collectives: 25.1 us -> 23.3 us  [exchange(): got = lax.all_to_all(parcel, 'view', 0, 0, tiled=True)]
    ppermute x8 -> x7, starting transfers between devices: 24.5 us -> 24.3 us  [strip_move(): return lax.ppermute(value, 'strip', pairs)]
    all_to_all x1 -> x2, starting transfers between devices: 10.8 us -> 10.9 us  [give_back(): return lax.all_to_all(parcel, 'view', 0, 0, tiled=True)]
  transfers between devices with their start and end apart: 10 -> 10, of which waited for: 5 -> 6; matrix products, arithmetic and copies ran while one was open for 2% -> 2% of each run, Pallas kernels for 2% -> 3%
where the time goes in v3:
time: 133 us; the launch traced here: 132 us
  starting transfers between devices  52.5 us (39%)
  waiting for transfers between devices  42 us (32%)
  blocking collectives  23.3 us (18%)
  Pallas kernels  8.99 us (7%)
  other arithmetic  2.97 us (2%)
    all_to_all x2, waiting for transfers between devices, give_back(): return lax.all_to_all(parcel, 'view', 0, 0, tiled=True)  28.6 us
    ppermute x7, starting transfers between devices, strip_move(): return lax.ppermute(value, 'strip', pairs)  24.3 us
    all_to_all x1, blocking collectives, exchange(): got = lax.all_to_all(parcel, 'view', 0, 0, tiled=True)  23.3 us
    all_to_all x1, starting transfers between devices, exchange(): got = lax.all_to_all(parcel, 'view', 0, 0, tiled=True)  17.3 us
    all_to_all x2, starting transfers between devices, give_back(): return lax.all_to_all(parcel, 'view', 0, 0, tiled=True)  10.9 us
    all_to_all x1, waiting for transfers between devices, exchange(): got = lax.all_to_all(parcel, 'view', 0, 0, tiled=True)  8.19 us
    ppermute x7, waiting for transfers between devices, strip_move(): return lax.ppermute(value, 'strip', pairs)  5.22 us
    pallas_call x2, Pallas kernels, gradient(): pl.pallas_call(gradient_kernel, out_shape=jax.ShapeDtypeStruct((2,) + own...  5.07 us
  transfers between devices with their start and end apart: 10, of which 6 were waited for; matrix products, arithmetic and copies ran while one was open for 2% of the time, Pallas kernels for 3%

profile of v3, /device:TPU:25, one launch (start us, length us, event | category | flops | bytes accessed | tf_op | source)
XLA Modules:
  0.0 131.6 jit_solution(6018280048160217680)
XLA Ops:
  0.6 17.3 %all-to-all-start = ((bf16[64,4,128]{2,1,0:T(4,128)(2,1)}), bf16[64,4,128]{2,1,0:T(4,128)(2,1)S(1)}, u32[]{:S(2)}, u32[]{:S(2)}) async-start(bf16[64,4,128]{2,1,0:T(4,128)(2,1)} %bitcast.100), calls=%async_computation | async-start | bytes 131072 | tf_op jit(solution)/shard_map/all_to_all | solution.py:199
  17.9 4.5 %collective-permute-start = (f32[2,128,128]{2,1,0:T(8,128)}, f32[2,128,128]{2,1,0:T(8,128)S(1)}, u32[]{:S(2)}, u32[]{:S(2)}) collective-permute-start(f32[2,128,128]{2,1,0:T(8,128)} %bitcast.79), channel_id=1, source_target_pairs={{1,0},{2,1},{3,2},{4,3},{5,4},{6,5},{7,6},{9,8},{10,9},{11,10},{12... | collective-permute-start | bytes 393224 | tf_op jit(solution)/shard_map/ppermute | solution.py:187
  22.5 0.7 multiply_add_fusion.2
  23.1 0.1 fusion.17
  23.2 0.1 eq.46
  23.3 0.3 eq.47
  23.6 0.1 eq.54
  23.7 0.3 eq.55
  24.0 0.0 copy-start
  24.0 0.0 copy-start.1
  24.0 0.0 copy-start.2
  24.0 0.0 copy-start.3
  24.0 0.0 copy-start.4
  24.0 0.1 eq.48
  24.1 0.1 eq.49
  24.2 0.1 compare_convert_fusion
  24.3 0.0 copy-start.5
  24.3 8.2 %all-to-all-done = bf16[64,4,128]{2,1,0:T(4,128)(2,1)S(1)} async-done(((bf16[64,4,128]{2,1,0:T(4,128)(2,1)}), bf16[64,4,128]{2,1,0:T(4,128)(2,1)S(1)}, u32[]{:S(2)}, u32[]{:S(2)}) %all-to-all-start) | async-done | bytes 65568 | tf_op jit(solution)/shard_map/all_to_all | solution.py:199
  32.5 1.8 %shard_map.95 = bf16[512,128]{1,0:T(8,128)(2,1)} custom-call(bf16[256,128]{1,0:T(8,128)(2,1)S(1)} %bitcast.85, bf16[64,2112]{1,0:T(8,128)(2,1)S(1)} %get-tuple-element.23.refs_1_), custom_call_target="tpu_custom_call" | custom-call | tf_op jit(solution)/shard_map/pallas_call | solution.py:170
  34.3 0.0 collective-permute-done.following
  34.3 6.5 %all-to-all-start.1 = ((bf16[64,8,128]{2,1,0:T(8,128)(2,1)}), bf16[64,8,128]{2,1,0:T(8,128)(2,1)S(1)}, u32[]{:S(2)}, u32[]{:S(2)}) async-start(bf16[64,8,128]{2,1,0:T(8,128)(2,1)} %bitcast.5), calls=%async_computation.1 | async-start | bytes 262144 | tf_op jit(solution)/shard_map/all_to_all | solution.py:206
  40.7 0.0 copy-done
  40.8 0.0 copy-done.1
  40.8 0.0 copy-done.2
  40.8 0.0 copy-done.3
  40.8 0.0 copy-done.4
  40.8 2.5 %shard_map.96 = f32[2,2,128,128]{3,2,1,0:T(8,128)S(1)} custom-call(s32[4]{0:T(128)S(1)} %bitcast.86, f32[2,128,128]{2,1,0:T(8,128)S(1)} %bitcast.80, f32[2,128,128]{2,1,0:T(8,128)S(1)} %collective-permute-done.following, f32[4,128,128]{2,1,0:T(8,128)S(1)} %bitcast.82, f32[2,128,128]{2,1,0:T(8,128)S(1)} %copy-done.3, bf16[2,2,256,256]{3,2,1,0:T(8,128)(2,1)S(1)} %copy-done.1), custom_call_target="tpu_custom_call" | custom-call | tf_op jit(solution)/shard_map/pallas_call | solution.py:130
  43.3 14.5 %all-to-all-done.1 = bf16[64,8,128]{2,1,0:T(8,128)(2,1)S(1)} async-done(((bf16[64,8,128]{2,1,0:T(8,128)(2,1)}), bf16[64,8,128]{2,1,0:T(8,128)(2,1)S(1)}, u32[]{:S(2)}, u32[]{:S(2)}) %all-to-all-start.1) | async-done | bytes 131104 | tf_op jit(solution)/shard_map/all_to_all | solution.py:206
  57.9 0.0 copy-done.5
  57.9 0.1 fusion.14
  58.0 2.5 %collective-permute-start.1 = (bf16[2,2,128,128]{3,2,1,0:T(8,128)(2,1)S(1)}, bf16[2,2,128,128]{3,2,1,0:T(8,128)(2,1)S(1)}, u32[]{:S(2)}, u32[]{:S(2)}) collective-permute-start(bf16[2,2,128,128]{3,2,1,0:T(8,128)(2,1)S(1)} %get-tuple-element.20), channel_id=1, source_target_pairs={{0,1},{1,2},{2,3},{3,4},{4,5},{5,6},{6,7},{8,9},{9,10},{10,11},{11... | collective-permute-start | bytes 393224 | tf_op jit(solution)/shard_map/ppermute | solution.py:187
  60.5 5.2 %collective-permute-start.2 = (bf16[2,2,128,128]{3,2,1,0:T(8,128)(2,1)S(1)}, bf16[2,2,128,128]{3,2,1,0:T(8,128)(2,1)S(1)}, u32[]{:S(2)}, u32[]{:S(2)}) collective-permute-start(bf16[2,2,128,128]{3,2,1,0:T(8,128)(2,1)S(1)} %get-tuple-element.21), channel_id=1, source_target_pairs={{1,0},{2,1},{3,2},{4,3},{5,4},{6,5},{7,6},{9,8},{10,9},{11,10},{12... | collective-permute-start | bytes 393224 | tf_op jit(solution)/shard_map/ppermute | solution.py:187
  65.7 2.4 %collective-permute-start.3 = (bf16[2,128,128]{2,1,0:T(8,128)(2,1)S(1)}, bf16[2,128,128]{2,1,0:T(8,128)(2,1)S(1)}, u32[]{:S(2)}, u32[]{:S(2)}) collective-permute-start(bf16[2,128,128]{2,1,0:T(8,128)(2,1)S(1)} %bitcast.93), channel_id=1, source_target_pairs={{2,0},{3,1},{4,2},{5,3},{6,4},{7,5},{10,8},{11,9},{12,10},{13,11},... | collective-permute-start | bytes 196616 | tf_op jit(solution)/shard_map/ppermute | solution.py:187
  68.1 1.3 collective-permute-done.3
  69.4 0.0 collective-permute-done.1
  69.4 0.0 collective-permute-done.2
  69.4 0.1 fusion.9
  69.5 2.5 %shard_map.97 = f32[2,2,128,128]{3,2,1,0:T(8,128)S(1)} custom-call(s32[4]{0:T(128)S(1)} %bitcast.87, f32[2,128,128]{2,1,0:T(8,128)S(1)} %get-tuple-element.11.own, f32[2,128,128]{2,1,0:T(8,128)S(1)} %get-tuple-element.10.following, f32[4,128,128]{2,1,0:T(8,128)S(1)} %bitcast.83, f32[2,128,128]{2,1,0:T(8,128)S(1)} %copy-done.3, ...), custom_call_target="tpu_custom_call" | custom-call | tf_op jit(solution)/shard_map/pallas_call | solution.py:130
  72.1 0.1 subtract_convert_fusion.2
  72.2 4.9 %collective-permute-start.4 = (bf16[2,2,128,128]{3,2,1,0:T(8,128)(2,1)S(1)}, bf16[2,2,128,128]{3,2,1,0:T(8,128)(2,1)S(1)}, u32[]{:S(2)}, u32[]{:S(2)}) collective-permute-start(bf16[2,2,128,128]{3,2,1,0:T(8,128)(2,1)S(1)} %pad_maximum_fusion.2), channel_id=1, source_target_pairs={{0,1},{1,2},{2,3},{3,4},{4,5},{5,6},{6,7},{8,9},{9,10},{10,11},{11... | collective-permute-start | bytes 393224 | tf_op jit(solution)/shard_map/ppermute | solution.py:187
  77.1 0.1 fusion.8
  77.2 3.5 %collective-permute-start.5 = (bf16[2,128,128]{2,1,0:T(8,128)(2,1)S(1)}, bf16[2,128,128]{2,1,0:T(8,128)(2,1)S(1)}, u32[]{:S(2)}, u32[]{:S(2)}) collective-permute-start(bf16[2,128,128]{2,1,0:T(8,128)(2,1)S(1)} %fusion.8), channel_id=1, source_target_pairs={{1,0},{2,1},{3,2},{4,3},{5,4},{6,5},{7,6},{9,8},{10,9},{11,10},{12... | collective-permute-start | bytes 196616 | tf_op jit(solution)/shard_map/ppermute | solution.py:187
  80.7 1.3 collective-permute-start.6
  82.1 0.0 collective-permute-done.4
  82.1 1.6 %collective-permute-done.5 = bf16[2,128,128]{2,1,0:T(8,128)(2,1)S(1)} collective-permute-done((bf16[2,128,128]{2,1,0:T(8,128)(2,1)S(1)}, bf16[2,128,128]{2,1,0:T(8,128)(2,1)S(1)}, u32[]{:S(2)}, u32[]{:S(2)}) %collective-permute-start.5) | collective-permute-done | bytes 65568 | tf_op jit(solution)/shard_map/ppermute | solution.py:187
  83.7 2.3 %collective-permute-done.6 = bf16[2,128,128]{2,1,0:T(8,128)(2,1)S(1)} collective-permute-done((bf16[2,128,128]{2,1,0:T(8,128)(2,1)S(1)}, bf16[2,128,128]{2,1,0:T(8,128)(2,1)S(1)}, u32[]{:S(2)}, u32[]{:S(2)}) %collective-permute-start.6) | collective-permute-done | bytes 65568 | tf_op jit(solution)/shard_map/ppermute | solution.py:187
  86.1 0.0 copy-start.6
  86.1 0.2 subtract_convert_fusion.1
  86.3 0.1 pad_maximum_fusion.3
  86.4 23.3 %all_to_all.20 = bf16[64,8,128]{2,1,0:T(8,128)(2,1)S(1)} all-to-all(bf16[64,8,128]{2,1,0:T(8,128)(2,1)S(1)} %pad_maximum_fusion.3), channel_id=1, replica_groups=mesh['view'=64,'strip'=8] {'view'}, dimensions={0} | all-to-all | bytes 262144 | tf_op jit(solution)/shard_map/all_to_all | solution.py:199
  109.7 2.1 %shard_map.98 = bf16[256,128]{1,0:T(8,128)(2,1)} custom-call(bf16[512,128]{1,0:T(8,128)(2,1)S(1)} %bitcast.84, bf16[64,2112]{1,0:T(8,128)(2,1)S(1)} %get-tuple-element.22.refs_1_), custom_call_target="tpu_custom_call" | custom-call | tf_op jit(solution)/shard_map/pallas_call | solution.py:170
  111.8 4.4 %all-to-all-start.3 = ((bf16[64,4,128]{2,1,0:T(4,128)(2,1)}), bf16[64,4,128]{2,1,0:T(4,128)(2,1)S(1)}, u32[]{:S(2)}, u32[]{:S(2)}) async-start(bf16[64,4,128]{2,1,0:T(4,128)(2,1)} %bitcast.29), calls=%async_computation.3 | async-start | bytes 131072 | tf_op jit(solution)/shard_map/all_to_all | solution.py:206
  116.3 0.7 fusion.26
  116.9 14.0 %all-to-all-done.3 = bf16[64,4,128]{2,1,0:T(4,128)(2,1)S(1)} async-done(((bf16[64,4,128]{2,1,0:T(4,128)(2,1)}), bf16[64,4,128]{2,1,0:T(4,128)(2,1)S(1)}, u32[]{:S(2)}, u32[]{:S(2)}) %all-to-all-start.3) | async-done | bytes 65568 | tf_op jit(solution)/shard_map/all_to_all | solution.py:206
  131.0 0.0 copy-done.6
  131.0 0.7 fusion.4
  (10 shorter events, 0.2 us)
Async XLA Ops:
  0.6 31.9 %all-to-all-start = ((bf16[64,4,128]{2,1,0:T(4,128)(2,1)}), bf16[64,4,128]{2,1,0:T(4,128)(2,1)S(1)}, u32[]{:S(2)}, u32[]{:S(2)}) async-start(bf16[64,4,128]{2,1,0:T(4,128)(2,1)} %bitcast.100), calls=%async_computation | async-start | bytes 131072 | tf_op jit(solution)/shard_map/all_to_all | solution.py:199
  17.9 16.4 %collective-permute-start = (f32[2,128,128]{2,1,0:T(8,128)}, f32[2,128,128]{2,1,0:T(8,128)S(1)}, u32[]{:S(2)}, u32[]{:S(2)}) collective-permute-start(f32[2,128,128]{2,1,0:T(8,128)} %bitcast.79), channel_id=1, source_target_pairs={{1,0},{2,1},{3,2},{4,3},{5,4},{6,5},{7,6},{9,8},{10,9},{11,10},{12... | collective-permute-start | bytes 393224 | tf_op jit(solution)/shard_map/ppermute | solution.py:187
  24.0 16.8 %copy-start = (f32[1,2,128,128]{3,2,1,0:T(8,128)S(1)}, f32[1,2,128,128]{3,2,1,0:T(8,128)}, u32[]{:S(2)}) copy-start(f32[1,2,128,128]{3,2,1,0:T(8,128)} %param.9) | copy-start | bytes 393220
  24.0 16.8 %copy-start.1 = (bf16[2,2,256,256]{3,2,1,0:T(8,128)(2,1)S(1)}, bf16[2,2,256,256]{3,2,1,0:T(8,128)(2,1)}, u32[]{:S(2)}) copy-start(bf16[2,2,256,256]{3,2,1,0:T(8,128)(2,1)} %constant.47.clone.tables) | copy-start | bytes 1572868
  24.0 16.8 %copy-start.2 = (f32[1,4,128,128]{3,2,1,0:T(8,128)S(1)}, f32[1,4,128,128]{3,2,1,0:T(8,128)}, u32[]{:S(2)}) copy-start(f32[1,4,128,128]{3,2,1,0:T(8,128)} %param.11) | copy-start | bytes 786436
  24.0 16.8 %copy-start.3 = (f32[2,128,128]{2,1,0:T(8,128)S(1)}, f32[2,128,128]{2,1,0:T(8,128)}, u32[]{:S(2)}) copy-start(f32[2,128,128]{2,1,0:T(8,128)} %probe.3) | copy-start | bytes 393220
  24.0 16.8 %copy-start.4 = (s32[1,4]{1,0:T(1,128)S(1)}, s32[1,4]{1,0:T(1,128)}, u32[]{:S(2)}) copy-start(s32[1,4]{1,0:T(1,128)} %param.12) | copy-start | bytes 52
  24.3 33.6 %copy-start.5 = (f32[1,2,128,128]{3,2,1,0:T(8,128)S(1)}, f32[1,2,128,128]{3,2,1,0:T(8,128)}, u32[]{:S(2)}) copy-start(f32[1,2,128,128]{3,2,1,0:T(8,128)} %param.10) | copy-start | bytes 393220
  34.3 23.6 %all-to-all-start.1 = ((bf16[64,8,128]{2,1,0:T(8,128)(2,1)}), bf16[64,8,128]{2,1,0:T(8,128)(2,1)S(1)}, u32[]{:S(2)}, u32[]{:S(2)}) async-start(bf16[64,8,128]{2,1,0:T(8,128)(2,1)} %bitcast.5), calls=%async_computation.1 | async-start | bytes 262144 | tf_op jit(solution)/shard_map/all_to_all | solution.py:206
  58.0 11.4 %collective-permute-start.1 = (bf16[2,2,128,128]{3,2,1,0:T(8,128)(2,1)S(1)}, bf16[2,2,128,128]{3,2,1,0:T(8,128)(2,1)S(1)}, u32[]{:S(2)}, u32[]{:S(2)}) collective-permute-start(bf16[2,2,128,128]{3,2,1,0:T(8,128)(2,1)S(1)} %get-tuple-element.20), channel_id=1, source_target_pairs={{0,1},{1,2},{2,3},{3,4},{4,5},{5,6},{6,7},{8,9},{9,10},{10,11},{11... | collective-permute-start | bytes 393224 | tf_op jit(solution)/shard_map/ppermute | solution.py:187
  60.5 8.9 %collective-permute-start.2 = (bf16[2,2,128,128]{3,2,1,0:T(8,128)(2,1)S(1)}, bf16[2,2,128,128]{3,2,1,0:T(8,128)(2,1)S(1)}, u32[]{:S(2)}, u32[]{:S(2)}) collective-permute-start(bf16[2,2,128,128]{3,2,1,0:T(8,128)(2,1)S(1)} %get-tuple-element.21), channel_id=1, source_target_pairs={{1,0},{2,1},{3,2},{4,3},{5,4},{6,5},{7,6},{9,8},{10,9},{11,10},{12... | collective-permute-start | bytes 393224 | tf_op jit(solution)/shard_map/ppermute | solution.py:187
  65.7 3.7 %collective-permute-start.3 = (bf16[2,128,128]{2,1,0:T(8,128)(2,1)S(1)}, bf16[2,128,128]{2,1,0:T(8,128)(2,1)S(1)}, u32[]{:S(2)}, u32[]{:S(2)}) collective-permute-start(bf16[2,128,128]{2,1,0:T(8,128)(2,1)S(1)} %bitcast.93), channel_id=1, source_target_pairs={{2,0},{3,1},{4,2},{5,3},{6,4},{7,5},{10,8},{11,9},{12,10},{13,11},... | collective-permute-start | bytes 196616 | tf_op jit(solution)/shard_map/ppermute | solution.py:187
  72.2 9.9 %collective-permute-start.4 = (bf16[2,2,128,128]{3,2,1,0:T(8,128)(2,1)S(1)}, bf16[2,2,128,128]{3,2,1,0:T(8,128)(2,1)S(1)}, u32[]{:S(2)}, u32[]{:S(2)}) collective-permute-start(bf16[2,2,128,128]{3,2,1,0:T(8,128)(2,1)S(1)} %pad_maximum_fusion.2), channel_id=1, source_target_pairs={{0,1},{1,2},{2,3},{3,4},{4,5},{5,6},{6,7},{8,9},{9,10},{10,11},{11... | collective-permute-start | bytes 393224 | tf_op jit(solution)/shard_map/ppermute | solution.py:187
  77.2 6.5 %collective-permute-start.5 = (bf16[2,128,128]{2,1,0:T(8,128)(2,1)S(1)}, bf16[2,128,128]{2,1,0:T(8,128)(2,1)S(1)}, u32[]{:S(2)}, u32[]{:S(2)}) collective-permute-start(bf16[2,128,128]{2,1,0:T(8,128)(2,1)S(1)} %fusion.8), channel_id=1, source_target_pairs={{1,0},{2,1},{3,2},{4,3},{5,4},{6,5},{7,6},{9,8},{10,9},{11,10},{12... | collective-permute-start | bytes 196616 | tf_op jit(solution)/shard_map/ppermute | solution.py:187
  80.7 5.3 %collective-permute-start.6 = (bf16[2,128,128]{2,1,0:T(8,128)(2,1)S(1)}, bf16[2,128,128]{2,1,0:T(8,128)(2,1)S(1)}, u32[]{:S(2)}, u32[]{:S(2)}) collective-permute-start(bf16[2,128,128]{2,1,0:T(8,128)(2,1)S(1)} %bitcast.95), channel_id=1, source_target_pairs={{0,2},{1,3},{2,4},{3,5},{4,6},{5,7},{8,10},{9,11},{10,12},{11,13},... | collective-permute-start | bytes 196616 | tf_op jit(solution)/shard_map/ppermute | solution.py:187
  86.1 44.9 %copy-start.6 = (bf16[1,2,128,128]{3,2,1,0:T(8,128)(2,1)S(1)}, bf16[1,2,128,128]{3,2,1,0:T(8,128)(2,1)}, u32[]{:S(2)}) copy-start(bf16[1,2,128,128]{3,2,1,0:T(8,128)(2,1)} %param.8) | copy-start | bytes 196612
  111.8 19.2 %all-to-all-start.3 = ((bf16[64,4,128]{2,1,0:T(4,128)(2,1)}), bf16[64,4,128]{2,1,0:T(4,128)(2,1)S(1)}, u32[]{:S(2)}, u32[]{:S(2)}) async-start(bf16[64,4,128]{2,1,0:T(4,128)(2,1)} %bitcast.29), calls=%async_computation.3 | async-start | bytes 131072 | tf_op jit(solution)/shard_map/all_to_all | solution.py:206

commit v4 on v1

--- a/solution.py
+++ b/solution.py
@@ -51,13 +51,11 @@
     return dot(high, table[0]) + dot(low, table[0]) + dot(high, table[1])
 
 
-def gradient_kernel(starts, own, following, measured, probe, tables, spread):
-    side = own.shape[1]
+def gradient_sums(starts, wide_real, wide_imag, measured, probe, tables):
+    side = measured.shape[1]
     count = measured.shape[0]
     ahead = (tables[0, 0], tables[0, 1])
     behind = (tables[1, 0], tables[1, 1])
-    wide_real = jnp.concatenate([own[0], following[0]], axis=1)
-    wide_imag = jnp.concatenate([own[1], following[1]], axis=1)
     probe_real = probe[0]
     probe_imag = probe[1]
     exits = []
@@ -119,16 +117,46 @@
         grad_imag = probe_real * delta_imag - probe_imag * delta_real
         total_real += pltpu.roll(jnp.concatenate([grad_real, nothing], axis=1), starts[p], 1)
         total_imag += pltpu.roll(jnp.concatenate([grad_imag, nothing], axis=1), starts[p], 1)
-    spread[0, 0] = total_real[:, :side]
-    spread[0, 1] = total_imag[:, :side]
-    spread[1, 0] = total_real[:, side:]
-    spread[1, 1] = total_imag[:, side:]
-
-
-def gradient(starts, own, following, measured, probe, tables):
+    return total_real, total_imag
+
+
+def pack_edges(source, lines):
+    side = source.shape[1]
+    count = source.shape[0] // lines
+    lane = lax.broadcasted_iota(jnp.int32, (count, side), 1)
+    packed = jnp.zeros((count, side), f32)
+    for r in range(lines):
+        part = source[pl.ds(r, count, stride=lines), :]
+        part = pltpu.roll(part, (HALO + 2 * HALO * r) % side, 1)
+        packed = jnp.where(lane // (2 * HALO) == r, part, packed)
+    return packed
+
+
+def open_edges(packed, r):
+    side = packed.shape[1]
+    lane = lax.broadcasted_iota(jnp.int32, packed.shape, 1)
+    part = pltpu.roll(packed, (2 * side - HALO - 2 * HALO * r) % side, 1)
+    return jnp.where((lane < HALO) | (lane >= side - HALO), part, 0.0)
+
+
+def first_kernel(starts, own, following, measured, probe, tables, spread):
+    side = own.shape[1]
+    wide_real = jnp.concatenate([own[0], following[0]], axis=1)
+    wide_imag = jnp.concatenate([own[1], following[1]], axis=1)
+    total_real, total_imag = gradient_sums(
+        starts, wide_real, wide_imag, measured, probe, tables
+    )
+    share = 1.0 / measured.shape[0]
+    spread[0, 0] = total_real[:, :side] * share
+    spread[0, 1] = total_imag[:, :side] * share
+    spread[1, 0] = total_real[:, side:] * share
+    spread[1, 1] = total_imag[:, side:] * share
+
+
+def first_gradient(starts, own, following, measured, probe, tables):
     vmem = pl.BlockSpec(memory_space=pltpu.VMEM)
     return pl.pallas_call(
-        gradient_kernel,
+        first_kernel,
         out_shape=jax.ShapeDtypeStruct((2,) + own.shape, f32),
         in_specs=[pl.BlockSpec(memory_space=pltpu.SMEM)] + [vmem] * 5,
         out_specs=vmem,
@@ -136,37 +164,208 @@
     )(starts, own, following, measured, probe, tables)
 
 
-def shear_kernel(scale, lines, source, choice, out, plain, taps, result):
+def between_kernel(
+    lines, odd, sums, spread, psi, dual, base, pull, send_pair, send_next, edges, plain, lined
+):
+    side = psi.shape[2]
+    rows = 2 * psi.shape[1]
+    groups = rows // lines
+    stride = lines + 2
+    plain[...] = sums[...].astype(f32)
+    for r in range(lines):
+        lined[pl.ds(r, groups, stride=lines), :] = plain[pl.ds(r, groups, stride=stride), :]
+    edge = plain[pl.ds(lines, groups, stride=stride), :].astype(bf16)
+    known = lined[...] - dual[...].reshape(rows, side)
+    before = psi[...].reshape(rows, side)
+    fresh = before + spread[0].reshape(rows, side) + coupling * (known - before)
+    pull[...] = known
+    base[...] = fresh
+    outer = spread[1].reshape(rows, side)
+    send_pair[:rows] = jnp.where(odd[0] > 0, fresh, outer).astype(bf16)
+    send_pair[rows:] = edge
+    send_next[:rows] = jnp.where(odd[0] > 0, outer, fresh).astype(bf16)
+    send_next[rows:] = edge
+    edges[...] = edge
+
+
+def between(odd, sums, spread, psi, dual, lines):
+    side = psi.shape[2]
+    rows = 2 * psi.shape[1]
+    groups = rows // lines
+    vmem = pl.BlockSpec(memory_space=pltpu.VMEM)
+    return pl.pallas_call(
+        lambda *refs: between_kernel(lines, *refs),
+        out_shape=[
+            jax.ShapeDtypeStruct((rows, side), f32),
+            jax.ShapeDtypeStruct((rows, side), f32),
+            jax.ShapeDtypeStruct((rows + groups, side), bf16),
+            jax.ShapeDtypeStruct((rows + groups, side), bf16),
+            jax.ShapeDtypeStruct((groups, side), bf16),
+        ],
+        in_specs=[pl.BlockSpec(memory_space=pltpu.SMEM)] + [vmem] * 4,
+        out_specs=[vmem] * 5,
+        scratch_shapes=[
+            pltpu.VMEM((groups * (lines + 2), side), f32),
+            pltpu.VMEM((rows, side), f32),
+        ],
+        compiler_params=pltpu.CompilerParams(vmem_limit_bytes=32 * 1024 * 1024),
+    )(odd, sums, spread, psi, dual)
+
+
+def second_kernel(
+    lines, starts, inside, base, pull, spread, pair, beside, edges, two, measured, probe, tables,
+    part, want, send, rim, near, far,
+):
+    side = base.shape[1]
+    rows = base.shape[0]
+    high = rows // 2
+    groups = rows // lines
+    lane = lax.broadcasted_iota(jnp.int32, (groups, side), 1)
+    early = lane < side // 2
+    odd = inside[1] > 0
+    up = jnp.where(odd, pair[...].astype(f32), beside[...].astype(f32))
+    down = jnp.where(odd, beside[...].astype(f32), pair[...].astype(f32))
+    here = edges[...].astype(f32)
+    farther = two[...].astype(f32)
+    for r in range(lines):
+        near[pl.ds(r, groups, stride=lines), :] = jnp.where(
+            early, open_edges(up[rows:], r), open_edges(down[rows:], r)
+        )
+        far[pl.ds(r, groups, stride=lines), :] = jnp.where(
+            early, open_edges(here, r), open_edges(farther, r)
+        )
+    gain = near[...]
+    drawn = pull[...] + gain
+    psi = base[...] + up[:rows] + coupling * gain
+    beyond = down[:rows] + spread[1].reshape(rows, side) + coupling * far[...]
+    beyond = jnp.where(inside[0] > 0, beyond, 0.0)
+    wide_real = jnp.concatenate([psi[:high], beyond[:high]], axis=1)
+    wide_imag = jnp.concatenate([psi[high:], beyond[high:]], axis=1)
+    total_real, total_imag = gradient_sums(
+        starts, wide_real, wide_imag, measured, probe, tables
+    )
+    total = jnp.concatenate([total_real, total_imag], axis=0) * (1.0 / measured.shape[0])
+    mine = psi + total[:, :side] + coupling * (drawn - psi)
+    rest = drawn - mine
+    part[...] = mine
+    want[...] = drawn
+    send[:rows] = total[:, side:].astype(bf16)
+    near[...] = rest
+    send[rows:] = pack_edges(near, lines).astype(bf16)
+    far[...] = total[:, side:]
+    rim[...] = pack_edges(far, lines).astype(bf16)
+
+
+def second_gradient(
+    starts, inside, base, pull, spread, pair, beside, edges, two, measured, probe, tables, lines
+):
+    rows, side = base.shape
+    groups = rows // lines
+    smem = pl.BlockSpec(memory_space=pltpu.SMEM)
+    vmem = pl.BlockSpec(memory_space=pltpu.VMEM)
+    return pl.pallas_call(
+        lambda *refs: second_kernel(lines, *refs),
+        out_shape=[
+            jax.ShapeDtypeStruct((rows, side), f32),
+            jax.ShapeDtypeStruct((rows, side), f32),
+            jax.ShapeDtypeStruct((rows + groups, side), bf16),
+            jax.ShapeDtypeStruct((groups, side), bf16),
+        ],
+        in_specs=[smem] * 2 + [vmem] * 10,
+        out_specs=[vmem] * 4,
+        scratch_shapes=[pltpu.VMEM((rows, side), f32), pltpu.VMEM((rows, side), f32)],
+        compiler_params=pltpu.CompilerParams(vmem_limit_bytes=32 * 1024 * 1024),
+    )(starts, inside, base, pull, spread, pair, beside, edges, two, measured, probe, tables)
+
+
+def close_kernel(lines, ends, part, want, pair, beside, two, rim, psi, parcel, plain, lined):
+    rows, side = part.shape
+    groups = rows // lines
+    stride = lines + 2
+    odd = ends[2] > 0
+    up = jnp.where(odd, pair[...].astype(f32), beside[...].astype(f32))
+    down = jnp.where(odd, beside[rows:].astype(f32), pair[rows:].astype(f32))
+    settled = part[...] + up[:rows]
+    psi[...] = settled
+    lined[...] = want[...] - settled
+    for r in range(lines):
+        plain[pl.ds(r, groups, stride=stride), :] = lined[pl.ds(r, groups, stride=lines), :]
+    lane = lax.broadcasted_iota(jnp.int32, (groups, side), 1)
+    left = jnp.where(ends[0] > 0, up[rows:] - two[...].astype(f32), 0.0)
+    right = jnp.where(ends[1] > 0, down - rim[...].astype(f32), 0.0)
+    packed = jnp.where(lane % (2 * HALO) < HALO, left, right)
+    plain[pl.ds(lines, groups, stride=stride), :] = packed
+    plain[pl.ds(lines + 1, groups, stride=stride), :] = jnp.zeros((groups, side), f32)
+    parcel[...] = plain[...].astype(bf16)
+
+
+def close(ends, part, want, pair, beside, two, rim, lines):
+    rows, side = part.shape
+    groups = rows // lines
+    smem = pl.BlockSpec(memory_space=pltpu.SMEM)
+    vmem = pl.BlockSpec(memory_space=pltpu.VMEM)
+    return pl.pallas_call(
+        lambda *refs: close_kernel(lines, *refs),
+        out_shape=[
+            jax.ShapeDtypeStruct((rows, side), f32),
+            jax.ShapeDtypeStruct((groups * (lines + 2), side), bf16),
+        ],
+        in_specs=[smem] + [vmem] * 6,
+        out_specs=[vmem] * 2,
+        scratch_shapes=[
+            pltpu.VMEM((groups * (lines + 2), side), f32),
+            pltpu.VMEM((rows, side), f32),
+        ],
+        compiler_params=pltpu.CompilerParams(vmem_limit_bytes=32 * 1024 * 1024),
+    )(ends, part, want, pair, beside, two, rim)
+
+
+def shear_kernel(scale, lines, wide_out, source, choice, out, plain, taps, result):
     channels = choice.shape[0]
     side = source.shape[1]
+    pieces = source.shape[0] // channels
+    span = 2 * side if wide_out else side
     plain[...] = source[...].astype(f32)
-    for r in range(lines):
-        near = plain[pl.ds(r, channels, stride=2 * lines), :]
-        edge = plain[pl.ds(lines + r, channels, stride=2 * lines), :]
+    if pieces > lines:
+        packed = plain[pl.ds(lines, channels, stride=pieces), :]
+    for r in range(lines):
+        near = plain[pl.ds(r, channels, stride=pieces), :]
+        edge = open_edges(packed, r) if pieces > lines else jnp.zeros_like(near)
         wide = jnp.concatenate([near, edge], axis=1)
         for d in range(TAPS):
-            moved = pltpu.roll(wide, (2 * side + HALO - d) % (2 * side), 1)[:, :side]
-            taps[d * channels : (d + 1) * channels, r * side : (r + 1) * side] = moved.astype(bf16)
+            moved = pltpu.roll(wide, (2 * side + HALO - d) % (2 * side), 1)[:, :span]
+            taps[d * channels : (d + 1) * channels, r * span : (r + 1) * span] = moved.astype(bf16)
     summed = dot(choice[...], taps[...]) * scale
-    for r in range(lines):
-        result[pl.ds(r, channels, stride=lines), :] = summed[:, r * side : (r + 1) * side]
+    given = lines + 2 if wide_out else lines
+    for r in range(lines):
+        result[pl.ds(r, channels, stride=given), :] = summed[:, r * span : r * span + side]
+    if wide_out:
+        lane = lax.broadcasted_iota(jnp.int32, (channels, side), 1)
+        packed = jnp.zeros((channels, side), f32)
+        for r in range(lines):
+            part = summed[:, r * span + side : (r + 1) * span]
+            part = pltpu.roll(part, (HALO + 2 * HALO * r) % side, 1)
+            packed = jnp.where(lane // (2 * HALO) == r, part, packed)
+        result[pl.ds(lines, channels, stride=given), :] = packed
+        result[pl.ds(lines + 1, channels, stride=given), :] = jnp.zeros_like(packed)
     out[...] = result[...].astype(bf16)
 
 
-def shear_sum(source, choice, scale):
+def shear_sum(source, choice, scale, lines, wide_out):
     channels = choice.shape[0]
     side = source.shape[1]
-    lines = source.shape[0] // (2 * channels)
+    given = (lines + 2 if wide_out else lines) * channels
+    span = 2 * side if wide_out else side
     vmem = pl.BlockSpec(memory_space=pltpu.VMEM)
     return pl.pallas_call(
-        lambda *refs: shear_kernel(scale, lines, *refs),
-        out_shape=jax.ShapeDtypeStruct((lines * channels, side), bf16),
+        lambda *refs: shear_kernel(scale, lines, wide_out, *refs),
+        out_shape=jax.ShapeDtypeStruct((given, side), bf16),
         in_specs=[vmem] * 2,
         out_specs=vmem,
         scratch_shapes=[
-            pltpu.VMEM((2 * lines * channels, side), f32),
-            pltpu.VMEM((TAPS * channels, lines * side), bf16),
-            pltpu.VMEM((lines * channels, side), f32),
+            pltpu.VMEM(source.shape, f32),
+            pltpu.VMEM((TAPS * channels, lines * span), bf16),
+            pltpu.VMEM((given, side), f32),
         ],
         compiler_params=pltpu.CompilerParams(vmem_limit_bytes=32 * 1024 * 1024),
     )(source, choice)
@@ -178,25 +377,17 @@
     return lax.ppermute(value, "strip", pairs)
 
 
-def with_edges(value, before, after):
-    lane = lax.broadcasted_iota(jnp.int32, value.shape, value.ndim - 1)
-    return jnp.where(lane < value.shape[-1] // 2, after, before)
-
-
-def exchange(own, edge, groups):
-    side = own.shape[-1]
-    lines = own.size // (groups * side)
-    parcel = jnp.concatenate(
-        [own.reshape(groups, lines, side), edge.reshape(groups, lines, side)], axis=1
-    )
-    got = lax.all_to_all(parcel, "view", 0, 0, tiled=True)
-    return got.reshape(groups * 2 * lines, side)
-
-
-def give_back(value, groups):
+def strip_swap(value, begin):
+    pairs = []
+    for i in range(begin, lax.axis_size("strip") - 1, 2):
+        pairs += [(i, i + 1), (i + 1, i)]
+    return lax.ppermute(value, "strip", pairs)
+
+
+def regroup(value, groups):
     side = value.shape[-1]
-    parcel = value.reshape(groups, value.shape[0] // groups, side)
-    return lax.all_to_all(parcel, "view", 0, 0, tiled=True)
+    parcel = value.reshape(groups, value.shape[0] // (2 * groups), 2, side)
+    return lax.all_to_all(parcel, "view", 0, 0, tiled=True).reshape(value.shape)
 
 
 def per_device(slab, psi_start, dual, amplitudes, offsets, angles, probe):
@@ -209,7 +400,6 @@
     starts = offsets[0]
     root_scale = 1.0 / math.sqrt(slices)
     tables = dft_blocks(probe.shape[1])
-    step_size = 1.0 / starts.shape[0]
 
     depth = jnp.arange(slices, dtype=jnp.int32)
     tilt = angles - HALO
@@ -222,40 +412,33 @@
         (-shift.T[:, None, :] == tap[None, :, None]).astype(bf16).reshape(slices, TAPS * slices)
     )
 
-    slab_edge = with_edges(own_slab, strip_move(own_slab, 1), strip_move(own_slab, -1))
+    lines = shape[0] * shape[1] // slices
+    place = lax.axis_index("strip")
+    odd = place % 2
+    inside = (place < lax.axis_size("strip") - 1).astype(jnp.int32)
+    ends = jnp.stack([(place > 0).astype(jnp.int32), inside, odd])
     following = strip_move(psi, -1)
-    lined = exchange(own_slab, slab_edge, slices)
-    spread = gradient(starts, psi, following, measured, probe, tables)
-    spill = strip_move(spread[1], 1)
-    sums = shear_sum(lined, choice_project, root_scale)
-    projected = give_back(sums, slices).reshape(shape).astype(f32)
-    pull = projected - own_dual
-    psi = psi + step_size * (spread[0] + spill) + coupling * (pull - psi)
-
-    following = strip_move(psi, -1)
-    spread = gradient(starts, psi, following, measured, probe, tables)
-    part = psi + step_size * spread[0] + coupling * (pull - psi)
-    rest = (pull - part).astype(bf16)
-    outer = (spread[1] * step_size).astype(bf16)
-    up = strip_move(jnp.stack([rest, outer]), 1)
-    up_two = strip_move(outer, 2)
-    down = strip_move(rest, -1)
-    incoming = up[1].astype(f32)
-    psi = part + incoming
-    residual = (pull - psi).astype(bf16)
-    residual_edge = with_edges(
-        residual,
-        (up[0].astype(f32) - up_two.astype(f32)).astype(bf16),
-        (down.astype(f32) - outer.astype(f32)).astype(bf16),
-    )
-    last = lax.axis_index("strip") == lax.axis_size("strip") - 1
-    first = lax.axis_index("strip") == 0
-    lane = lax.broadcasted_iota(jnp.int32, shape, 2)
-    outside = (last & (lane < shape[2] // 2)) | (first & (lane >= shape[2] // 2))
-    residual_edge = jnp.where(outside, jnp.zeros_like(residual_edge), residual_edge)
-    lined = exchange(residual, residual_edge, slices)
-    sums = shear_sum(lined, choice_back, descent * root_scale)
-    backward = give_back(sums, slices).reshape(shape).astype(f32)
+    lined = regroup(own_slab.reshape(lines * slices, shape[2]), slices)
+    sums = shear_sum(lined, choice_project, root_scale, lines, True)
+    sums, following = lax.optimization_barrier((sums, following))
+    sums = regroup(sums, slices)
+    spread = first_gradient(starts, psi, following, measured, probe, tables)
+    base, pull, pair, beside, edges = between(ends[2:], sums, spread, psi, own_dual, lines)
+    two = strip_move(edges, -2)
+    beside = strip_swap(beside, 1)
+    pair = strip_swap(pair, 0)
+    part, want, send, rim = second_gradient(
+        starts, ends[1:], base, pull, spread, pair, beside, edges, two, measured, probe, tables,
+        lines,
+    )
+    two = strip_move(rim, 2)
+    beside = strip_swap(send, 1)
+    pair = strip_swap(send, 0)
+    psi, parcel = close(ends, part, want, pair, beside, two, rim, lines)
+    psi = psi.reshape(shape)
+    lined = regroup(parcel, slices)
+    sums = shear_sum(lined, choice_back, descent * root_scale, lines, False)
+    backward = regroup(sums, slices).reshape(shape).astype(f32)
     slab_new = (own_slab.astype(f32) - backward).astype(bf16)
     return (psi[None], slab_new[None])
 

time: 143 us -> 130 us (0.909)
  waiting for transfers between devices: 37 us -> 25.3 us
  blocking collectives: 44 us -> 41 us
  other arithmetic: 3.25 us -> 1.68 us
  Pallas kernels: 8.68 us -> 10.2 us
    ppermute x8 -> x3, starting transfers between devices: 25.9 us -> 8.02 us  [strip_move(): return lax.ppermute(value, 'strip', pairs)]
    ppermute x0 -> x4, starting transfers between devices: none -> 16.7 us  [strip_swap(): return lax.ppermute(value, 'strip', pairs)]
    ppermute x8 -> x3, waiting for transfers between devices: 17 us -> 3.88 us  [strip_move(): return lax.ppermute(value, 'strip', pairs)]
    all_to_all x2, blocking collectives: 44 us -> 41 us  [regroup(): return lax.all_to_all(parcel, 'view', 0, 0, tiled=True).reshape(value.shape)]
    all_to_all x2, starting transfers between devices: 21.6 us -> 23.6 us  [regroup(): return lax.all_to_all(parcel, 'view', 0, 0, tiled=True).reshape(value.shape)]
    pallas_call x4 -> x6, Pallas kernels: 8.68 us -> 10.2 us  [the longest x2 3.59 us: shear_sum(): pl.pallas_call(lambda *refs: shear_kernel(scale, lines, wide_out, *refs),...]
  transfers between devices with their start and end apart: 10 -> 9, of which waited for: 6 -> 4; matrix products, arithmetic and copies ran while one was open for 2% -> 1% of each run, Pallas kernels for 2% -> 3%
where the time goes in v4:
time: 130 us; the launch traced here: 128 us
  starting transfers between devices  48.4 us (37%)
  blocking collectives  41 us (32%)
  waiting for transfers between devices  25.3 us (19%)
  Pallas kernels  10.2 us (8%)
  other arithmetic  1.68 us (1%)
    all_to_all x2, blocking collectives, regroup(): return lax.all_to_all(parcel, 'view', 0, 0, tiled=True).reshape(value.shape)  41 us
    all_to_all x2, starting transfers between devices, regroup(): return lax.all_to_all(parcel, 'view', 0, 0, tiled=True).reshape(value.shape)  23.6 us
    all_to_all x2, waiting for transfers between devices, regroup(): return lax.all_to_all(parcel, 'view', 0, 0, tiled=True).reshape(value.shape)  21.4 us
    ppermute x4, starting transfers between devices, strip_swap(): return lax.ppermute(value, 'strip', pairs)  16.7 us
    ppermute x3, starting transfers between devices, strip_move(): return lax.ppermute(value, 'strip', pairs)  8.02 us
    ppermute x3, waiting for transfers between devices, strip_move(): return lax.ppermute(value, 'strip', pairs)  3.88 us
    pallas_call x2, Pallas kernels, shear_sum(): pl.pallas_call(lambda *refs: shear_kernel(scale, lines, wide_out, *refs),...  3.59 us
    pallas_call x1, Pallas kernels, second_gradient(): pl.pallas_call(lambda *refs: second_kernel(lines, *refs), out_shape=[jax....  2.73 us
  transfers between devices with their start and end apart: 9, of which 4 were waited for; matrix products, arithmetic and copies ran while one was open for 1% of the time, Pallas kernels for 3%

profile of v4, /device:TPU:25, one launch (start us, length us, event | category | flops | bytes accessed | tf_op | source)
XLA Modules:
  0.0 128.4 jit_solution(12609774055002478023)
XLA Ops:
  0.6 17.3 %all-to-all-start = ((bf16[64,2,2,128]{3,2,1,0:T(2,128)(2,1)}), bf16[64,2,2,128]{3,2,1,0:T(2,128)(2,1)S(1)}, u32[]{:S(2)}, u32[]{:S(2)}) async-start(bf16[64,2,2,128]{3,2,1,0:T(2,128)(2,1)} %bitcast.30), calls=%async_computation | async-start | bytes 131072 | tf_op jit(solution)/shard_map/all_to_all | solution.py:390
  17.9 4.5 %collective-permute-start = (f32[2,128,128]{2,1,0:T(8,128)}, f32[2,128,128]{2,1,0:T(8,128)S(1)}, u32[]{:S(2)}, u32[]{:S(2)}) collective-permute-start(f32[2,128,128]{2,1,0:T(8,128)} %bitcast.19), channel_id=1, source_target_pairs={{1,0},{2,1},{3,2},{4,3},{5,4},{6,5},{7,6},{9,8},{10,9},{11,10},{12... | collective-permute-start | bytes 393224 | tf_op jit(solution)/shard_map/ppermute | solution.py:377
  22.5 0.7 multiply_add_fusion
  23.1 0.1 fusion.3
  23.2 0.1 eq.42
  23.3 0.3 eq.43
  23.6 0.1 eq.48
  23.7 0.3 eq.49
  24.0 0.0 copy-start
  24.0 0.0 copy-start.1
  24.0 0.0 copy-start.2
  24.0 0.0 copy-start.3
  24.0 0.0 copy-start.5
  24.0 0.1 eq.44
  24.1 0.1 eq.45
  24.2 0.1 compare_convert_fusion
  24.3 0.0 copy-start.4
  24.3 8.2 %all-to-all-done = bf16[64,2,2,128]{3,2,1,0:T(2,128)(2,1)S(1)} async-done(((bf16[64,2,2,128]{3,2,1,0:T(2,128)(2,1)}), bf16[64,2,2,128]{3,2,1,0:T(2,128)(2,1)S(1)}, u32[]{:S(2)}, u32[]{:S(2)}) %all-to-all-start) | async-done | bytes 65568 | tf_op jit(solution)/shard_map/all_to_all | solution.py:390
  32.5 1.9 %shard_map.95 = bf16[384,128]{1,0:T(8,128)(2,1)} custom-call(bf16[256,128]{1,0:T(8,128)(2,1)S(1)} %bitcast.24, bf16[64,2112]{1,0:T(8,128)(2,1)S(1)} %get-tuple-element.29.refs_1_), custom_call_target="tpu_custom_call" | custom-call | tf_op jit(solution)/shard_map/pallas_call | solution.py:360
  34.3 0.0 collective-permute-done.following
  34.3 6.4 %all-to-all-start.1 = ((bf16[64,3,2,128]{3,2,1,0:T(2,128)(2,1)}), bf16[64,3,2,128]{3,2,1,0:T(2,128)(2,1)S(1)}, u32[]{:S(2)}, u32[]{:S(2)}) async-start(bf16[64,3,2,128]{3,2,1,0:T(2,128)(2,1)} %bitcast.7), calls=%async_computation.1 | async-start | bytes 196608 | tf_op jit(solution)/shard_map/all_to_all | solution.py:390
  40.8 0.0 copy-done
  40.8 0.0 copy-done.1
  40.8 0.0 copy-done.2
  40.8 0.0 copy-done.3
  40.8 0.0 copy-done.5
  40.8 2.5 %shard_map.96.refs_2_.refs_4_ = f32[2,2,128,128]{3,2,1,0:T(8,128)S(1)} custom-call(s32[4]{0:T(128)S(1)} %bitcast.28, f32[2,128,128]{2,1,0:T(8,128)S(1)} %bitcast.20, f32[2,128,128]{2,1,0:T(8,128)S(1)} %collective-permute-done.following, f32[4,128,128]{2,1,0:T(8,128)S(1)} %bitcast.17, f32[2,128,128]{2,1,0:T(8,128)S(1)} %copy-done.3, ...), custom_call_target="tpu_custom_call" | custom-call | tf_op jit(solution)/shard_map/pallas_call | solution.py:158
  43.4 13.2 %all-to-all-done.1 = bf16[64,3,2,128]{3,2,1,0:T(2,128)(2,1)S(1)} async-done(((bf16[64,3,2,128]{3,2,1,0:T(2,128)(2,1)}), bf16[64,3,2,128]{3,2,1,0:T(2,128)(2,1)S(1)}, u32[]{:S(2)}, u32[]{:S(2)}) %all-to-all-start.1) | async-done | bytes 98336 | tf_op jit(solution)/shard_map/all_to_all | solution.py:390
  56.6 0.0 copy-done.4
  56.6 0.1 shard_map.97
  56.7 2.5 %collective-permute-start.1 = (bf16[320,128]{1,0:T(8,128)(2,1)S(1)}, bf16[320,128]{1,0:T(8,128)(2,1)S(1)}, u32[]{:S(2)}, u32[]{:S(2)}) collective-permute-start(bf16[320,128]{1,0:T(8,128)(2,1)S(1)} %get-tuple-element.19), channel_id=1, source_target_pairs={{0,1},{1,0},{2,3},{3,2},{4,5},{5,4},{6,7},{7,6},{8,9},{9,8},{10,11... | collective-permute-start | bytes 245768 | tf_op jit(solution)/shard_map/ppermute | solution.py:384
  59.2 4.8 %collective-permute-start.2 = (bf16[320,128]{1,0:T(8,128)(2,1)S(1)}, bf16[320,128]{1,0:T(8,128)(2,1)S(1)}, u32[]{:S(2)}, u32[]{:S(2)}) collective-permute-start(bf16[320,128]{1,0:T(8,128)(2,1)S(1)} %get-tuple-element.20), channel_id=1, source_target_pairs={{1,2},{2,1},{3,4},{4,3},{5,6},{6,5},{9,10},{10,9},{11,12},{12,11},... | collective-permute-start | bytes 245768 | tf_op jit(solution)/shard_map/ppermute | solution.py:384
  64.0 2.2 %collective-permute-start.3 = (bf16[64,128]{1,0:T(8,128)(2,1)S(1)}, bf16[64,128]{1,0:T(8,128)(2,1)S(1)}, u32[]{:S(2)}, u32[]{:S(2)}) collective-permute-start(bf16[64,128]{1,0:T(8,128)(2,1)S(1)} %get-tuple-element.21.refs_7_), channel_id=1, source_target_pairs={{2,0},{3,1},{4,2},{5,3},{6,4},{7,5},{10,8},{11,9},{12,10},{13,11},... | collective-permute-start | bytes 49160 | tf_op jit(solution)/shard_map/ppermute | solution.py:377
  66.2 0.1 pad_add_fusion.1.refs_1_
  66.3 0.8 collective-permute-done.3.refs_8_
  67.1 0.0 collective-permute-done.1.refs_5_
  67.1 0.0 collective-permute-done.2.refs_6_
  67.1 0.0 copy-start.6
  67.1 2.7 %shard_map.98 = (f32[256,128]{1,0:T(8,128)S(1)}, f32[256,128]{1,0:T(8,128)S(1)}, bf16[320,128]{1,0:T(8,128)(2,1)S(1)}, bf16[64,128]{1,0:T(8,128)(2,1)S(1)}) custom-call(s32[4]{0:T(128)S(1)} %bitcast.29, s32[2]{0:T(128)S(1)} %pad_add_fusion.1.refs_1_, f32[256,128]{1,0:T(8,128)S(1)} %get-tuple-element.17.refs_2_, f32[256,128]{1,0:T(8,128)S(1)} %get-tuple-element.18.refs_3_, ...), custom_call_target="tpu_custom_call" | custom-call | tf_op jit(solution)/shard_map/pallas_call | solution.py:266
  69.8 2.9 %collective-permute-start.4 = (bf16[320,128]{1,0:T(8,128)(2,1)S(1)}, bf16[320,128]{1,0:T(8,128)(2,1)S(1)}, u32[]{:S(2)}, u32[]{:S(2)}) collective-permute-start(bf16[320,128]{1,0:T(8,128)(2,1)S(1)} %get-tuple-element.24), channel_id=1, source_target_pairs={{0,1},{1,0},{2,3},{3,2},{4,5},{5,4},{6,7},{7,6},{8,9},{9,8},{10,11... | collective-permute-start | bytes 245768 | tf_op jit(solution)/shard_map/ppermute | solution.py:384
  72.7 6.5 %collective-permute-start.5 = (bf16[320,128]{1,0:T(8,128)(2,1)S(1)}, bf16[320,128]{1,0:T(8,128)(2,1)S(1)}, u32[]{:S(2)}, u32[]{:S(2)}) collective-permute-start(bf16[320,128]{1,0:T(8,128)(2,1)S(1)} %get-tuple-element.24), channel_id=1, source_target_pairs={{1,2},{2,1},{3,4},{4,3},{5,6},{6,5},{9,10},{10,9},{11,12},{12,11},... | collective-permute-start | bytes 245768 | tf_op jit(solution)/shard_map/ppermute | solution.py:384
  79.3 1.3 %collective-permute-start.6 = (bf16[64,128]{1,0:T(8,128)(2,1)S(1)}, bf16[64,128]{1,0:T(8,128)(2,1)S(1)}, u32[]{:S(2)}, u32[]{:S(2)}) collective-permute-start(bf16[64,128]{1,0:T(8,128)(2,1)S(1)} %get-tuple-element.25.refs_6_), channel_id=1, source_target_pairs={{0,2},{1,3},{2,4},{3,5},{4,6},{5,7},{8,10},{9,11},{10,12},{11,13},... | collective-permute-start | bytes 49160 | tf_op jit(solution)/shard_map/ppermute | solution.py:377
  80.6 0.1 pad_add_fusion.refs_0_
  80.6 3.1 %collective-permute-done.6.refs_5_ = bf16[64,128]{1,0:T(8,128)(2,1)S(1)} collective-permute-done((bf16[64,128]{1,0:T(8,128)(2,1)S(1)}, bf16[64,128]{1,0:T(8,128)(2,1)S(1)}, u32[]{:S(2)}, u32[]{:S(2)}) %collective-permute-start.6) | collective-permute-done | bytes 16416 | tf_op jit(solution)/shard_map/ppermute | solution.py:377
  83.7 0.0 collective-permute-done.4.refs_3_
  83.7 0.0 collective-permute-done.5.refs_4_
  83.7 1.2 shard_map.99
  85.0 22.7 %all_to_all.20 = bf16[64,3,2,128]{3,2,1,0:T(2,128)(2,1)S(1)} all-to-all(bf16[64,3,2,128]{3,2,1,0:T(2,128)(2,1)S(1)} %bitcast.27), channel_id=1, replica_groups=mesh['view'=64,'strip'=8] {'view'}, dimensions={0} | all-to-all | bytes 196608 | tf_op jit(solution)/shard_map/all_to_all | solution.py:390
  107.7 1.7 %shard_map.100 = bf16[256,128]{1,0:T(8,128)(2,1)S(1)} custom-call(bf16[384,128]{1,0:T(8,128)(2,1)S(1)} %bitcast.22, bf16[64,2112]{1,0:T(8,128)(2,1)S(1)} %get-tuple-element.28.refs_1_), custom_call_target="tpu_custom_call" | custom-call | tf_op jit(solution)/shard_map/pallas_call | solution.py:360
  109.4 18.3 %all_to_all.21 = bf16[64,2,2,128]{3,2,1,0:T(2,128)(2,1)S(1)} all-to-all(bf16[64,2,2,128]{3,2,1,0:T(2,128)(2,1)S(1)} %bitcast.25), channel_id=1, replica_groups=mesh['view'=64,'strip'=8] {'view'}, dimensions={0} | all-to-all | bytes 131072 | tf_op jit(solution)/shard_map/all_to_all | solution.py:390
  127.7 0.0 copy-done.6
  127.7 0.7 fusion
  (1 shorter events, 0.0 us)
Async XLA Ops:
  0.6 31.9 %all-to-all-start = ((bf16[64,2,2,128]{3,2,1,0:T(2,128)(2,1)}), bf16[64,2,2,128]{3,2,1,0:T(2,128)(2,1)S(1)}, u32[]{:S(2)}, u32[]{:S(2)}) async-start(bf16[64,2,2,128]{3,2,1,0:T(2,128)(2,1)} %bitcast.30), calls=%async_computation | async-start | bytes 131072 | tf_op jit(solution)/shard_map/all_to_all | solution.py:390
  17.9 16.5 %collective-permute-start = (f32[2,128,128]{2,1,0:T(8,128)}, f32[2,128,128]{2,1,0:T(8,128)S(1)}, u32[]{:S(2)}, u32[]{:S(2)}) collective-permute-start(f32[2,128,128]{2,1,0:T(8,128)} %bitcast.19), channel_id=1, source_target_pairs={{1,0},{2,1},{3,2},{4,3},{5,4},{6,5},{7,6},{9,8},{10,9},{11,10},{12... | collective-permute-start | bytes 393224 | tf_op jit(solution)/shard_map/ppermute | solution.py:377
  24.0 16.8 %copy-start = (bf16[2,2,256,256]{3,2,1,0:T(8,128)(2,1)S(1)}, bf16[2,2,256,256]{3,2,1,0:T(8,128)(2,1)}, u32[]{:S(2)}) copy-start(bf16[2,2,256,256]{3,2,1,0:T(8,128)(2,1)} %constant.47.clone.tables.refs_11_) | copy-start | bytes 1572868
  24.0 16.8 %copy-start.1 = (f32[1,4,128,128]{3,2,1,0:T(8,128)S(1)}, f32[1,4,128,128]{3,2,1,0:T(8,128)}, u32[]{:S(2)}) copy-start(f32[1,4,128,128]{3,2,1,0:T(8,128)} %param.11) | copy-start | bytes 786436
  24.0 16.8 %copy-start.2 = (f32[1,2,128,128]{3,2,1,0:T(8,128)S(1)}, f32[1,2,128,128]{3,2,1,0:T(8,128)}, u32[]{:S(2)}) copy-start(f32[1,2,128,128]{3,2,1,0:T(8,128)} %param.9) | copy-start | bytes 393220
  24.0 16.8 %copy-start.3 = (f32[2,128,128]{2,1,0:T(8,128)S(1)}, f32[2,128,128]{2,1,0:T(8,128)}, u32[]{:S(2)}) copy-start(f32[2,128,128]{2,1,0:T(8,128)} %refs_10_.1) | copy-start | bytes 393220
  24.0 16.8 %copy-start.5 = (s32[1,4]{1,0:T(1,128)S(1)}, s32[1,4]{1,0:T(1,128)}, u32[]{:S(2)}) copy-start(s32[1,4]{1,0:T(1,128)} %param.12) | copy-start | bytes 52
  24.3 32.3 %copy-start.4 = (f32[1,2,128,128]{3,2,1,0:T(8,128)S(1)}, f32[1,2,128,128]{3,2,1,0:T(8,128)}, u32[]{:S(2)}) copy-start(f32[1,2,128,128]{3,2,1,0:T(8,128)} %param.10) | copy-start | bytes 393220
  34.3 22.2 %all-to-all-start.1 = ((bf16[64,3,2,128]{3,2,1,0:T(2,128)(2,1)}), bf16[64,3,2,128]{3,2,1,0:T(2,128)(2,1)S(1)}, u32[]{:S(2)}, u32[]{:S(2)}) async-start(bf16[64,3,2,128]{3,2,1,0:T(2,128)(2,1)} %bitcast.7), calls=%async_computation.1 | async-start | bytes 196608 | tf_op jit(solution)/shard_map/all_to_all | solution.py:390
  56.7 10.4 %collective-permute-start.1 = (bf16[320,128]{1,0:T(8,128)(2,1)S(1)}, bf16[320,128]{1,0:T(8,128)(2,1)S(1)}, u32[]{:S(2)}, u32[]{:S(2)}) collective-permute-start(bf16[320,128]{1,0:T(8,128)(2,1)S(1)} %get-tuple-element.19), channel_id=1, source_target_pairs={{0,1},{1,0},{2,3},{3,2},{4,5},{5,4},{6,7},{7,6},{8,9},{9,8},{10,11... | collective-permute-start | bytes 245768 | tf_op jit(solution)/shard_map/ppermute | solution.py:384
  59.2 7.9 %collective-permute-start.2 = (bf16[320,128]{1,0:T(8,128)(2,1)S(1)}, bf16[320,128]{1,0:T(8,128)(2,1)S(1)}, u32[]{:S(2)}, u32[]{:S(2)}) collective-permute-start(bf16[320,128]{1,0:T(8,128)(2,1)S(1)} %get-tuple-element.20), channel_id=1, source_target_pairs={{1,2},{2,1},{3,4},{4,3},{5,6},{6,5},{9,10},{10,9},{11,12},{12,11},... | collective-permute-start | bytes 245768 | tf_op jit(solution)/shard_map/ppermute | solution.py:384
  64.0 3.0 %collective-permute-start.3 = (bf16[64,128]{1,0:T(8,128)(2,1)S(1)}, bf16[64,128]{1,0:T(8,128)(2,1)S(1)}, u32[]{:S(2)}, u32[]{:S(2)}) collective-permute-start(bf16[64,128]{1,0:T(8,128)(2,1)S(1)} %get-tuple-element.21.refs_7_), channel_id=1, source_target_pairs={{2,0},{3,1},{4,2},{5,3},{6,4},{7,5},{10,8},{11,9},{12,10},{13,11},... | collective-permute-start | bytes 49160 | tf_op jit(solution)/shard_map/ppermute | solution.py:377
  67.1 60.6 %copy-start.6 = (bf16[1,2,128,128]{3,2,1,0:T(8,128)(2,1)S(1)}, bf16[1,2,128,128]{3,2,1,0:T(8,128)(2,1)}, u32[]{:S(2)}) copy-start(bf16[1,2,128,128]{3,2,1,0:T(8,128)(2,1)} %param.8) | copy-start | bytes 196612
  69.8 13.9 %collective-permute-start.4 = (bf16[320,128]{1,0:T(8,128)(2,1)S(1)}, bf16[320,128]{1,0:T(8,128)(2,1)S(1)}, u32[]{:S(2)}, u32[]{:S(2)}) collective-permute-start(bf16[320,128]{1,0:T(8,128)(2,1)S(1)} %get-tuple-element.24), channel_id=1, source_target_pairs={{0,1},{1,0},{2,3},{3,2},{4,5},{5,4},{6,7},{7,6},{8,9},{9,8},{10,11... | collective-permute-start | bytes 245768 | tf_op jit(solution)/shard_map/ppermute | solution.py:384
  72.7 11.0 %collective-permute-start.5 = (bf16[320,128]{1,0:T(8,128)(2,1)S(1)}, bf16[320,128]{1,0:T(8,128)(2,1)S(1)}, u32[]{:S(2)}, u32[]{:S(2)}) collective-permute-start(bf16[320,128]{1,0:T(8,128)(2,1)S(1)} %get-tuple-element.24), channel_id=1, source_target_pairs={{1,2},{2,1},{3,4},{4,3},{5,6},{6,5},{9,10},{10,9},{11,12},{12,11},... | collective-permute-start | bytes 245768 | tf_op jit(solution)/shard_map/ppermute | solution.py:384
  79.3 4.5 %collective-permute-start.6 = (bf16[64,128]{1,0:T(8,128)(2,1)S(1)}, bf16[64,128]{1,0:T(8,128)(2,1)S(1)}, u32[]{:S(2)}, u32[]{:S(2)}) collective-permute-start(bf16[64,128]{1,0:T(8,128)(2,1)S(1)} %get-tuple-element.25.refs_6_), channel_id=1, source_target_pairs={{0,2},{1,3},{2,4},{3,5},{4,6},{5,7},{8,10},{9,11},{10,12},{11,13},... | collective-permute-start | bytes 49160 | tf_op jit(solution)/shard_map/ppermute | solution.py:377

commit v5 on v4

--- a/solution.py
+++ b/solution.py
@@ -331,10 +331,10 @@
     for r in range(lines):
         near = plain[pl.ds(r, channels, stride=pieces), :]
         edge = open_edges(packed, r) if pieces > lines else jnp.zeros_like(near)
-        wide = jnp.concatenate([near, edge], axis=1)
+        wide = jnp.concatenate([near, edge], axis=1).astype(bf16)
         for d in range(TAPS):
             moved = pltpu.roll(wide, (2 * side + HALO - d) % (2 * side), 1)[:, :span]
-            taps[d * channels : (d + 1) * channels, r * span : (r + 1) * span] = moved.astype(bf16)
+            taps[d * channels : (d + 1) * channels, r * span : (r + 1) * span] = moved
     summed = dot(choice[...], taps[...]) * scale
     given = lines + 2 if wide_out else lines
     for r in range(lines):
@@ -369,6 +369,35 @@
         ],
         compiler_params=pltpu.CompilerParams(vmem_limit_bytes=32 * 1024 * 1024),
     )(source, choice)
+
+
+def back_kernel(scale, lines, source, choice, settled, out, psi, plain, taps, result, done):
+    copy = pltpu.make_async_copy(settled, psi, done)
+    copy.start()
+    shear_kernel(scale, lines, False, source, choice, out, plain, taps, result)
+    copy.wait()
+
+
+def back_sum(source, choice, settled, scale, lines):
+    channels = choice.shape[0]
+    side = source.shape[1]
+    vmem = pl.BlockSpec(memory_space=pltpu.VMEM)
+    return pl.pallas_call(
+        lambda *refs: back_kernel(scale, lines, *refs),
+        out_shape=[
+            jax.ShapeDtypeStruct((lines * channels, side), bf16),
+            jax.ShapeDtypeStruct(settled.shape, f32),
+        ],
+        in_specs=[vmem] * 3,
+        out_specs=[vmem, pl.BlockSpec(memory_space=pl.ANY)],
+        scratch_shapes=[
+            pltpu.VMEM(source.shape, f32),
+            pltpu.VMEM((TAPS * channels, lines * side), bf16),
+            pltpu.VMEM((lines * channels, side), f32),
+            pltpu.SemaphoreType.DMA,
+        ],
+        compiler_params=pltpu.CompilerParams(vmem_limit_bytes=32 * 1024 * 1024),
+    )(source, choice, settled)
 
 
 def strip_move(value, by):
@@ -435,9 +464,9 @@
     beside = strip_swap(send, 1)
     pair = strip_swap(send, 0)
     psi, parcel = close(ends, part, want, pair, beside, two, rim, lines)
+    lined = regroup(parcel, slices)
+    sums, psi = back_sum(lined, choice_back, psi, descent * root_scale, lines)
     psi = psi.reshape(shape)
-    lined = regroup(parcel, slices)
-    sums = shear_sum(lined, choice_back, descent * root_scale, lines, False)
     backward = regroup(sums, slices).reshape(shape).astype(f32)
     slab_new = (own_slab.astype(f32) - backward).astype(bf16)
     return (psi[None], slab_new[None])

time: 130 us -> 129 us (level)
    pallas_call x0 -> x1, Pallas kernels: none -> 2.09 us  [back_sum(): pl.pallas_call(lambda *refs: back_kernel(scale, lines, *refs), out_shape=...]
    pallas_call x2 -> x1, Pallas kernels: 3.59 us -> 1.72 us  [shear_sum(): pl.pallas_call(lambda *refs: shear_kernel(scale, lines, wide_out, *refs),...]
where the time goes in v5:
time: 129 us; the launch traced here: 128 us
  starting transfers between devices  48.6 us (38%)
  blocking collectives  41 us (32%)
  waiting for transfers between devices  25.3 us (20%)
  Pallas kernels  9.78 us (8%)
  other arithmetic  1.68 us (1%)
    all_to_all x2, blocking collectives, regroup(): return lax.all_to_all(parcel, 'view', 0, 0, tiled=True).reshape(value.shape)  41 us
    all_to_all x2, starting transfers between devices, regroup(): return lax.all_to_all(parcel, 'view', 0, 0, tiled=True).reshape(value.shape)  23.8 us
    all_to_all x2, waiting for transfers between devices, regroup(): return lax.all_to_all(parcel, 'view', 0, 0, tiled=True).reshape(value.shape)  21.4 us
    ppermute x4, starting transfers between devices, strip_swap(): return lax.ppermute(value, 'strip', pairs)  16.7 us
    ppermute x3, starting transfers between devices, strip_move(): return lax.ppermute(value, 'strip', pairs)  8.02 us
    ppermute x3, waiting for transfers between devices, strip_move(): return lax.ppermute(value, 'strip', pairs)  3.88 us
    pallas_call x1, Pallas kernels, second_gradient(): pl.pallas_call(lambda *refs: second_kernel(lines, *refs), out_shape=[jax....  2.73 us
  transfers between devices with their start and end apart: 9, of which 4 were waited for; matrix products, arithmetic and copies ran while one was open for 1% of the time, Pallas kernels for 3%

profile of v5, /device:TPU:25, one launch (start us, length us, event | category | flops | bytes accessed | tf_op | source)
XLA Modules:
  0.0 128.1 jit_solution(7522317093640307175)
XLA Ops:
  0.6 17.3 %all-to-all-start = ((bf16[64,2,2,128]{3,2,1,0:T(2,128)(2,1)}), bf16[64,2,2,128]{3,2,1,0:T(2,128)(2,1)S(1)}, u32[]{:S(2)}, u32[]{:S(2)}) async-start(bf16[64,2,2,128]{3,2,1,0:T(2,128)(2,1)} %bitcast.30), calls=%async_computation | async-start | bytes 131072 | tf_op jit(solution)/shard_map/all_to_all | solution.py:419
  17.9 4.5 %collective-permute-start = (f32[2,128,128]{2,1,0:T(8,128)}, f32[2,128,128]{2,1,0:T(8,128)S(1)}, u32[]{:S(2)}, u32[]{:S(2)}) collective-permute-start(f32[2,128,128]{2,1,0:T(8,128)} %bitcast.19), channel_id=1, source_target_pairs={{1,0},{2,1},{3,2},{4,3},{5,4},{6,5},{7,6},{9,8},{10,9},{11,10},{12... | collective-permute-start | bytes 393224 | tf_op jit(solution)/shard_map/ppermute | solution.py:406
  22.5 0.7 multiply_add_fusion
  23.1 0.1 fusion.3
  23.2 0.1 eq.42
  23.3 0.3 eq.43
  23.6 0.1 eq.48
  23.7 0.3 eq.49
  24.0 0.0 copy-start
  24.0 0.0 copy-start.1
  24.0 0.0 copy-start.2
  24.0 0.0 copy-start.3
  24.0 0.0 copy-start.5
  24.0 0.1 eq.44
  24.1 0.1 eq.45
  24.2 0.1 compare_convert_fusion
  24.3 0.0 copy-start.4
  24.3 8.2 %all-to-all-done = bf16[64,2,2,128]{3,2,1,0:T(2,128)(2,1)S(1)} async-done(((bf16[64,2,2,128]{3,2,1,0:T(2,128)(2,1)}), bf16[64,2,2,128]{3,2,1,0:T(2,128)(2,1)S(1)}, u32[]{:S(2)}, u32[]{:S(2)}) %all-to-all-start) | async-done | bytes 65568 | tf_op jit(solution)/shard_map/all_to_all | solution.py:419
  32.5 1.7 %shard_map.95 = bf16[384,128]{1,0:T(8,128)(2,1)} custom-call(bf16[256,128]{1,0:T(8,128)(2,1)S(1)} %bitcast.24, bf16[64,2112]{1,0:T(8,128)(2,1)S(1)} %get-tuple-element.33.refs_1_), custom_call_target="tpu_custom_call" | custom-call | tf_op jit(solution)/shard_map/pallas_call | solution.py:360
  34.2 0.0 collective-permute-done.following
  34.2 6.5 %all-to-all-start.1 = ((bf16[64,3,2,128]{3,2,1,0:T(2,128)(2,1)}), bf16[64,3,2,128]{3,2,1,0:T(2,128)(2,1)S(1)}, u32[]{:S(2)}, u32[]{:S(2)}) async-start(bf16[64,3,2,128]{3,2,1,0:T(2,128)(2,1)} %bitcast.7), calls=%async_computation.1 | async-start | bytes 196608 | tf_op jit(solution)/shard_map/all_to_all | solution.py:419
  40.8 0.0 copy-done
  40.8 0.0 copy-done.1
  40.8 0.0 copy-done.2
  40.8 0.0 copy-done.3
  40.8 0.0 copy-done.5
  40.8 2.5 %shard_map.96.refs_2_.refs_4_ = f32[2,2,128,128]{3,2,1,0:T(8,128)S(1)} custom-call(s32[4]{0:T(128)S(1)} %bitcast.28, f32[2,128,128]{2,1,0:T(8,128)S(1)} %bitcast.20, f32[2,128,128]{2,1,0:T(8,128)S(1)} %collective-permute-done.following, f32[4,128,128]{2,1,0:T(8,128)S(1)} %bitcast.17, f32[2,128,128]{2,1,0:T(8,128)S(1)} %copy-done.3, ...), custom_call_target="tpu_custom_call" | custom-call | tf_op jit(solution)/shard_map/pallas_call | solution.py:158
  43.4 13.2 %all-to-all-done.1 = bf16[64,3,2,128]{3,2,1,0:T(2,128)(2,1)S(1)} async-done(((bf16[64,3,2,128]{3,2,1,0:T(2,128)(2,1)}), bf16[64,3,2,128]{3,2,1,0:T(2,128)(2,1)S(1)}, u32[]{:S(2)}, u32[]{:S(2)}) %all-to-all-start.1) | async-done | bytes 98336 | tf_op jit(solution)/shard_map/all_to_all | solution.py:419
  56.6 0.0 copy-done.4
  56.6 0.1 shard_map.97
  56.7 2.4 %collective-permute-start.1 = (bf16[320,128]{1,0:T(8,128)(2,1)S(1)}, bf16[320,128]{1,0:T(8,128)(2,1)S(1)}, u32[]{:S(2)}, u32[]{:S(2)}) collective-permute-start(bf16[320,128]{1,0:T(8,128)(2,1)S(1)} %get-tuple-element.21), channel_id=1, source_target_pairs={{0,1},{1,0},{2,3},{3,2},{4,5},{5,4},{6,7},{7,6},{8,9},{9,8},{10,11... | collective-permute-start | bytes 245768 | tf_op jit(solution)/shard_map/ppermute | solution.py:413
  59.1 5.0 %collective-permute-start.2 = (bf16[320,128]{1,0:T(8,128)(2,1)S(1)}, bf16[320,128]{1,0:T(8,128)(2,1)S(1)}, u32[]{:S(2)}, u32[]{:S(2)}) collective-permute-start(bf16[320,128]{1,0:T(8,128)(2,1)S(1)} %get-tuple-element.22), channel_id=1, source_target_pairs={{1,2},{2,1},{3,4},{4,3},{5,6},{6,5},{9,10},{10,9},{11,12},{12,11},... | collective-permute-start | bytes 245768 | tf_op jit(solution)/shard_map/ppermute | solution.py:413
  64.0 2.2 %collective-permute-start.3 = (bf16[64,128]{1,0:T(8,128)(2,1)S(1)}, bf16[64,128]{1,0:T(8,128)(2,1)S(1)}, u32[]{:S(2)}, u32[]{:S(2)}) collective-permute-start(bf16[64,128]{1,0:T(8,128)(2,1)S(1)} %get-tuple-element.23.refs_7_), channel_id=1, source_target_pairs={{2,0},{3,1},{4,2},{5,3},{6,4},{7,5},{10,8},{11,9},{12,10},{13,11},... | collective-permute-start | bytes 49160 | tf_op jit(solution)/shard_map/ppermute | solution.py:406
  66.2 0.1 pad_add_fusion.1.refs_1_
  66.3 0.8 collective-permute-done.3.refs_8_
  67.1 0.0 collective-permute-done.1.refs_5_
  67.1 0.0 collective-permute-done.2.refs_6_
  67.1 0.0 copy-start.6
  67.1 2.7 %shard_map.98 = (f32[256,128]{1,0:T(8,128)S(1)}, f32[256,128]{1,0:T(8,128)S(1)}, bf16[320,128]{1,0:T(8,128)(2,1)S(1)}, bf16[64,128]{1,0:T(8,128)(2,1)S(1)}) custom-call(s32[4]{0:T(128)S(1)} %bitcast.29, s32[2]{0:T(128)S(1)} %pad_add_fusion.1.refs_1_, f32[256,128]{1,0:T(8,128)S(1)} %get-tuple-element.19.refs_2_, f32[256,128]{1,0:T(8,128)S(1)} %get-tuple-element.20.refs_3_, ...), custom_call_target="tpu_custom_call" | custom-call | tf_op jit(solution)/shard_map/pallas_call | solution.py:266
  69.8 2.7 %collective-permute-start.4 = (bf16[320,128]{1,0:T(8,128)(2,1)S(1)}, bf16[320,128]{1,0:T(8,128)(2,1)S(1)}, u32[]{:S(2)}, u32[]{:S(2)}) collective-permute-start(bf16[320,128]{1,0:T(8,128)(2,1)S(1)} %get-tuple-element.26), channel_id=1, source_target_pairs={{0,1},{1,0},{2,3},{3,2},{4,5},{5,4},{6,7},{7,6},{8,9},{9,8},{10,11... | collective-permute-start | bytes 245768 | tf_op jit(solution)/shard_map/ppermute | solution.py:413
  72.6 6.7 %collective-permute-start.5 = (bf16[320,128]{1,0:T(8,128)(2,1)S(1)}, bf16[320,128]{1,0:T(8,128)(2,1)S(1)}, u32[]{:S(2)}, u32[]{:S(2)}) collective-permute-start(bf16[320,128]{1,0:T(8,128)(2,1)S(1)} %get-tuple-element.26), channel_id=1, source_target_pairs={{1,2},{2,1},{3,4},{4,3},{5,6},{6,5},{9,10},{10,9},{11,12},{12,11},... | collective-permute-start | bytes 245768 | tf_op jit(solution)/shard_map/ppermute | solution.py:413
  79.3 1.3 %collective-permute-start.6 = (bf16[64,128]{1,0:T(8,128)(2,1)S(1)}, bf16[64,128]{1,0:T(8,128)(2,1)S(1)}, u32[]{:S(2)}, u32[]{:S(2)}) collective-permute-start(bf16[64,128]{1,0:T(8,128)(2,1)S(1)} %get-tuple-element.27.refs_6_), channel_id=1, source_target_pairs={{0,2},{1,3},{2,4},{3,5},{4,6},{5,7},{8,10},{9,11},{10,12},{11,13},... | collective-permute-start | bytes 49160 | tf_op jit(solution)/shard_map/ppermute | solution.py:406
  80.6 0.1 pad_add_fusion.refs_0_
  80.6 3.1 %collective-permute-done.6.refs_5_ = bf16[64,128]{1,0:T(8,128)(2,1)S(1)} collective-permute-done((bf16[64,128]{1,0:T(8,128)(2,1)S(1)}, bf16[64,128]{1,0:T(8,128)(2,1)S(1)}, u32[]{:S(2)}, u32[]{:S(2)}) %collective-permute-start.6) | collective-permute-done | bytes 16416 | tf_op jit(solution)/shard_map/ppermute | solution.py:406
  83.7 0.0 collective-permute-done.4.refs_3_
  83.7 0.0 collective-permute-done.5.refs_4_
  83.7 0.6 shard_map.99
  84.4 22.7 %all_to_all.20 = bf16[64,3,2,128]{3,2,1,0:T(2,128)(2,1)S(1)} all-to-all(bf16[64,3,2,128]{3,2,1,0:T(2,128)(2,1)S(1)} %bitcast.26), channel_id=1, replica_groups=mesh['view'=64,'strip'=8] {'view'}, dimensions={0} | all-to-all | bytes 196608 | tf_op jit(solution)/shard_map/all_to_all | solution.py:419
  107.1 2.1 %shard_map.100 = (bf16[256,128]{1,0:T(8,128)(2,1)S(1)}, f32[256,128]{1,0:T(8,128)}) custom-call(bf16[384,128]{1,0:T(8,128)(2,1)S(1)} %bitcast.23, bf16[64,2112]{1,0:T(8,128)(2,1)S(1)} %get-tuple-element.32.refs_1_, f32[256,128]{1,0:T(8,128)S(1)} %get-tuple-element.29.refs_2_), custom_call_target="tpu_custom_call" | custom-call | tf_op jit(solution)/shard_map/pallas_call | solution.py:385
  109.2 18.3 %all_to_all.21 = bf16[64,2,2,128]{3,2,1,0:T(2,128)(2,1)S(1)} all-to-all(bf16[64,2,2,128]{3,2,1,0:T(2,128)(2,1)S(1)} %bitcast.27), channel_id=1, replica_groups=mesh['view'=64,'strip'=8] {'view'}, dimensions={0} | all-to-all | bytes 131072 | tf_op jit(solution)/shard_map/all_to_all | solution.py:419
  127.5 0.0 copy-done.6
  127.5 0.7 fusion
  (1 shorter events, 0.0 us)
Async XLA Ops:
  0.6 31.9 %all-to-all-start = ((bf16[64,2,2,128]{3,2,1,0:T(2,128)(2,1)}), bf16[64,2,2,128]{3,2,1,0:T(2,128)(2,1)S(1)}, u32[]{:S(2)}, u32[]{:S(2)}) async-start(bf16[64,2,2,128]{3,2,1,0:T(2,128)(2,1)} %bitcast.30), calls=%async_computation | async-start | bytes 131072 | tf_op jit(solution)/shard_map/all_to_all | solution.py:419
  17.9 16.3 %collective-permute-start = (f32[2,128,128]{2,1,0:T(8,128)}, f32[2,128,128]{2,1,0:T(8,128)S(1)}, u32[]{:S(2)}, u32[]{:S(2)}) collective-permute-start(f32[2,128,128]{2,1,0:T(8,128)} %bitcast.19), channel_id=1, source_target_pairs={{1,0},{2,1},{3,2},{4,3},{5,4},{6,5},{7,6},{9,8},{10,9},{11,10},{12... | collective-permute-start | bytes 393224 | tf_op jit(solution)/shard_map/ppermute | solution.py:406
  24.0 16.8 %copy-start = (bf16[2,2,256,256]{3,2,1,0:T(8,128)(2,1)S(1)}, bf16[2,2,256,256]{3,2,1,0:T(8,128)(2,1)}, u32[]{:S(2)}) copy-start(bf16[2,2,256,256]{3,2,1,0:T(8,128)(2,1)} %constant.47.clone.tables.refs_11_) | copy-start | bytes 1572868
  24.0 16.8 %copy-start.1 = (f32[1,4,128,128]{3,2,1,0:T(8,128)S(1)}, f32[1,4,128,128]{3,2,1,0:T(8,128)}, u32[]{:S(2)}) copy-start(f32[1,4,128,128]{3,2,1,0:T(8,128)} %param.11) | copy-start | bytes 786436
  24.0 16.8 %copy-start.2 = (f32[1,2,128,128]{3,2,1,0:T(8,128)S(1)}, f32[1,2,128,128]{3,2,1,0:T(8,128)}, u32[]{:S(2)}) copy-start(f32[1,2,128,128]{3,2,1,0:T(8,128)} %param.9) | copy-start | bytes 393220
  24.0 16.8 %copy-start.3 = (f32[2,128,128]{2,1,0:T(8,128)S(1)}, f32[2,128,128]{2,1,0:T(8,128)}, u32[]{:S(2)}) copy-start(f32[2,128,128]{2,1,0:T(8,128)} %refs_10_.1) | copy-start | bytes 393220
  24.0 16.8 %copy-start.5 = (s32[1,4]{1,0:T(1,128)S(1)}, s32[1,4]{1,0:T(1,128)}, u32[]{:S(2)}) copy-start(s32[1,4]{1,0:T(1,128)} %param.12) | copy-start | bytes 52
  24.3 32.3 %copy-start.4 = (f32[1,2,128,128]{3,2,1,0:T(8,128)S(1)}, f32[1,2,128,128]{3,2,1,0:T(8,128)}, u32[]{:S(2)}) copy-start(f32[1,2,128,128]{3,2,1,0:T(8,128)} %param.10) | copy-start | bytes 393220
  34.2 22.4 %all-to-all-start.1 = ((bf16[64,3,2,128]{3,2,1,0:T(2,128)(2,1)}), bf16[64,3,2,128]{3,2,1,0:T(2,128)(2,1)S(1)}, u32[]{:S(2)}, u32[]{:S(2)}) async-start(bf16[64,3,2,128]{3,2,1,0:T(2,128)(2,1)} %bitcast.7), calls=%async_computation.1 | async-start | bytes 196608 | tf_op jit(solution)/shard_map/all_to_all | solution.py:419
  56.7 10.4 %collective-permute-start.1 = (bf16[320,128]{1,0:T(8,128)(2,1)S(1)}, bf16[320,128]{1,0:T(8,128)(2,1)S(1)}, u32[]{:S(2)}, u32[]{:S(2)}) collective-permute-start(bf16[320,128]{1,0:T(8,128)(2,1)S(1)} %get-tuple-element.21), channel_id=1, source_target_pairs={{0,1},{1,0},{2,3},{3,2},{4,5},{5,4},{6,7},{7,6},{8,9},{9,8},{10,11... | collective-permute-start | bytes 245768 | tf_op jit(solution)/shard_map/ppermute | solution.py:413
  59.1 8.0 %collective-permute-start.2 = (bf16[320,128]{1,0:T(8,128)(2,1)S(1)}, bf16[320,128]{1,0:T(8,128)(2,1)S(1)}, u32[]{:S(2)}, u32[]{:S(2)}) collective-permute-start(bf16[320,128]{1,0:T(8,128)(2,1)S(1)} %get-tuple-element.22), channel_id=1, source_target_pairs={{1,2},{2,1},{3,4},{4,3},{5,6},{6,5},{9,10},{10,9},{11,12},{12,11},... | collective-permute-start | bytes 245768 | tf_op jit(solution)/shard_map/ppermute | solution.py:413
  64.0 3.0 %collective-permute-start.3 = (bf16[64,128]{1,0:T(8,128)(2,1)S(1)}, bf16[64,128]{1,0:T(8,128)(2,1)S(1)}, u32[]{:S(2)}, u32[]{:S(2)}) collective-permute-start(bf16[64,128]{1,0:T(8,128)(2,1)S(1)} %get-tuple-element.23.refs_7_), channel_id=1, source_target_pairs={{2,0},{3,1},{4,2},{5,3},{6,4},{7,5},{10,8},{11,9},{12,10},{13,11},... | collective-permute-start | bytes 49160 | tf_op jit(solution)/shard_map/ppermute | solution.py:406
  67.1 60.4 %copy-start.6 = (bf16[1,2,128,128]{3,2,1,0:T(8,128)(2,1)S(1)}, bf16[1,2,128,128]{3,2,1,0:T(8,128)(2,1)}, u32[]{:S(2)}) copy-start(bf16[1,2,128,128]{3,2,1,0:T(8,128)(2,1)} %param.8) | copy-start | bytes 196612
  69.8 13.9 %collective-permute-start.4 = (bf16[320,128]{1,0:T(8,128)(2,1)S(1)}, bf16[320,128]{1,0:T(8,128)(2,1)S(1)}, u32[]{:S(2)}, u32[]{:S(2)}) collective-permute-start(bf16[320,128]{1,0:T(8,128)(2,1)S(1)} %get-tuple-element.26), channel_id=1, source_target_pairs={{0,1},{1,0},{2,3},{3,2},{4,5},{5,4},{6,7},{7,6},{8,9},{9,8},{10,11... | collective-permute-start | bytes 245768 | tf_op jit(solution)/shard_map/ppermute | solution.py:413
  72.6 11.2 %collective-permute-start.5 = (bf16[320,128]{1,0:T(8,128)(2,1)S(1)}, bf16[320,128]{1,0:T(8,128)(2,1)S(1)}, u32[]{:S(2)}, u32[]{:S(2)}) collective-permute-start(bf16[320,128]{1,0:T(8,128)(2,1)S(1)} %get-tuple-element.26), channel_id=1, source_target_pairs={{1,2},{2,1},{3,4},{4,3},{5,6},{6,5},{9,10},{10,9},{11,12},{12,11},... | collective-permute-start | bytes 245768 | tf_op jit(solution)/shard_map/ppermute | solution.py:413
  79.3 4.5 %collective-permute-start.6 = (bf16[64,128]{1,0:T(8,128)(2,1)S(1)}, bf16[64,128]{1,0:T(8,128)(2,1)S(1)}, u32[]{:S(2)}, u32[]{:S(2)}) collective-permute-start(bf16[64,128]{1,0:T(8,128)(2,1)S(1)} %get-tuple-element.27.refs_6_), channel_id=1, source_target_pairs={{0,2},{1,3},{2,4},{3,5},{4,6},{5,7},{8,10},{9,11},{10,12},{11,13},... | collective-permute-start | bytes 49160 | tf_op jit(solution)/shard_map/ppermute | solution.py:406

commit v6 on v5

--- a/solution.py
+++ b/solution.py
@@ -43,12 +43,14 @@
 
 def table_left(table, value):
     high, low = split(value)
-    return dot(table[0], high) + dot(table[0], low) + dot(table[1], high)
+    across = jnp.concatenate([table[0], table[0], table[1]], axis=1)
+    return dot(across, jnp.concatenate([high, low, high], axis=0))
 
 
 def table_right(value, table):
     high, low = split(value)
-    return dot(high, table[0]) + dot(low, table[0]) + dot(high, table[1])
+    along = jnp.concatenate([table[0], table[0], table[1]], axis=0)
+    return dot(jnp.concatenate([high, low, high], axis=1), along)
 
 
 def gradient_sums(starts, wide_real, wide_imag, measured, probe, tables):

time: 129 us -> 129 us (level)
  no operation moved by 1% of the time
where the time goes in v6:
time: 129 us; the launch traced here: 128 us
  starting transfers between devices  48.6 us (38%)
  blocking collectives  41 us (32%)
  waiting for transfers between devices  25.3 us (20%)
  Pallas kernels  9.75 us (8%)
  other arithmetic  1.68 us (1%)
    all_to_all x2, blocking collectives, regroup(): return lax.all_to_all(parcel, 'view', 0, 0, tiled=True).reshape(value.shape)  41 us
    all_to_all x2, starting transfers between devices, regroup(): return lax.all_to_all(parcel, 'view', 0, 0, tiled=True).reshape(value.shape)  23.8 us
    all_to_all x2, waiting for transfers between devices, regroup(): return lax.all_to_all(parcel, 'view', 0, 0, tiled=True).reshape(value.shape)  21.4 us
    ppermute x4, starting transfers between devices, strip_swap(): return lax.ppermute(value, 'strip', pairs)  16.7 us
    ppermute x3, starting transfers between devices, strip_move(): return lax.ppermute(value, 'strip', pairs)  8.02 us
    ppermute x3, waiting for transfers between devices, strip_move(): return lax.ppermute(value, 'strip', pairs)  3.88 us
    pallas_call x1, Pallas kernels, second_gradient(): pl.pallas_call(lambda *refs: second_kernel(lines, *refs), out_shape=[jax....  2.72 us
  transfers between devices with their start and end apart: 9, of which 4 were waited for; matrix products, arithmetic and copies ran while one was open for 1% of the time, Pallas kernels for 3%

profile of v6, /device:TPU:25, one launch (start us, length us, event | category | flops | bytes accessed | tf_op | source)
XLA Modules:
  0.0 128.1 jit_solution(10538220725351977203)
XLA Ops:
  0.6 17.3 %all-to-all-start = ((bf16[64,2,2,128]{3,2,1,0:T(2,128)(2,1)}), bf16[64,2,2,128]{3,2,1,0:T(2,128)(2,1)S(1)}, u32[]{:S(2)}, u32[]{:S(2)}) async-start(bf16[64,2,2,128]{3,2,1,0:T(2,128)(2,1)} %bitcast.30), calls=%async_computation | async-start | bytes 131072 | tf_op jit(solution)/shard_map/all_to_all | solution.py:421
  17.9 4.5 %collective-permute-start = (f32[2,128,128]{2,1,0:T(8,128)}, f32[2,128,128]{2,1,0:T(8,128)S(1)}, u32[]{:S(2)}, u32[]{:S(2)}) collective-permute-start(f32[2,128,128]{2,1,0:T(8,128)} %bitcast.19), channel_id=1, source_target_pairs={{1,0},{2,1},{3,2},{4,3},{5,4},{6,5},{7,6},{9,8},{10,9},{11,10},{12... | collective-permute-start | bytes 393224 | tf_op jit(solution)/shard_map/ppermute | solution.py:408
  22.5 0.7 multiply_add_fusion
  23.1 0.1 fusion.3
  23.2 0.1 eq.42
  23.3 0.3 eq.43
  23.6 0.1 eq.48
  23.7 0.3 eq.49
  24.0 0.0 copy-start
  24.0 0.0 copy-start.1
  24.0 0.0 copy-start.2
  24.0 0.0 copy-start.3
  24.0 0.0 copy-start.5
  24.0 0.1 eq.44
  24.1 0.1 eq.45
  24.2 0.1 compare_convert_fusion
  24.3 0.0 copy-start.4
  24.3 8.2 %all-to-all-done = bf16[64,2,2,128]{3,2,1,0:T(2,128)(2,1)S(1)} async-done(((bf16[64,2,2,128]{3,2,1,0:T(2,128)(2,1)}), bf16[64,2,2,128]{3,2,1,0:T(2,128)(2,1)S(1)}, u32[]{:S(2)}, u32[]{:S(2)}) %all-to-all-start) | async-done | bytes 65568 | tf_op jit(solution)/shard_map/all_to_all | solution.py:421
  32.5 1.7 %shard_map.95 = bf16[384,128]{1,0:T(8,128)(2,1)} custom-call(bf16[256,128]{1,0:T(8,128)(2,1)S(1)} %bitcast.24, bf16[64,2112]{1,0:T(8,128)(2,1)S(1)} %get-tuple-element.33.refs_1_), custom_call_target="tpu_custom_call" | custom-call | tf_op jit(solution)/shard_map/pallas_call | solution.py:362
  34.2 0.0 collective-permute-done.following
  34.2 6.5 %all-to-all-start.1 = ((bf16[64,3,2,128]{3,2,1,0:T(2,128)(2,1)}), bf16[64,3,2,128]{3,2,1,0:T(2,128)(2,1)S(1)}, u32[]{:S(2)}, u32[]{:S(2)}) async-start(bf16[64,3,2,128]{3,2,1,0:T(2,128)(2,1)} %bitcast.7), calls=%async_computation.1 | async-start | bytes 196608 | tf_op jit(solution)/shard_map/all_to_all | solution.py:421
  40.8 0.0 copy-done
  40.8 0.0 copy-done.1
  40.8 0.0 copy-done.2
  40.8 0.0 copy-done.3
  40.8 0.0 copy-done.5
  40.8 2.5 %shard_map.96.refs_2_.refs_4_ = f32[2,2,128,128]{3,2,1,0:T(8,128)S(1)} custom-call(s32[4]{0:T(128)S(1)} %bitcast.28, f32[2,128,128]{2,1,0:T(8,128)S(1)} %bitcast.20, f32[2,128,128]{2,1,0:T(8,128)S(1)} %collective-permute-done.following, f32[4,128,128]{2,1,0:T(8,128)S(1)} %bitcast.17, f32[2,128,128]{2,1,0:T(8,128)S(1)} %copy-done.3, ...), custom_call_target="tpu_custom_call" | custom-call | tf_op jit(solution)/shard_map/pallas_call | solution.py:160
  43.3 13.2 %all-to-all-done.1 = bf16[64,3,2,128]{3,2,1,0:T(2,128)(2,1)S(1)} async-done(((bf16[64,3,2,128]{3,2,1,0:T(2,128)(2,1)}), bf16[64,3,2,128]{3,2,1,0:T(2,128)(2,1)S(1)}, u32[]{:S(2)}, u32[]{:S(2)}) %all-to-all-start.1) | async-done | bytes 98336 | tf_op jit(solution)/shard_map/all_to_all | solution.py:421
  56.6 0.0 copy-done.4
  56.6 0.1 shard_map.97
  56.7 2.4 %collective-permute-start.1 = (bf16[320,128]{1,0:T(8,128)(2,1)S(1)}, bf16[320,128]{1,0:T(8,128)(2,1)S(1)}, u32[]{:S(2)}, u32[]{:S(2)}) collective-permute-start(bf16[320,128]{1,0:T(8,128)(2,1)S(1)} %get-tuple-element.21), channel_id=1, source_target_pairs={{0,1},{1,0},{2,3},{3,2},{4,5},{5,4},{6,7},{7,6},{8,9},{9,8},{10,11... | collective-permute-start | bytes 245768 | tf_op jit(solution)/shard_map/ppermute | solution.py:415
  59.1 5.0 %collective-permute-start.2 = (bf16[320,128]{1,0:T(8,128)(2,1)S(1)}, bf16[320,128]{1,0:T(8,128)(2,1)S(1)}, u32[]{:S(2)}, u32[]{:S(2)}) collective-permute-start(bf16[320,128]{1,0:T(8,128)(2,1)S(1)} %get-tuple-element.22), channel_id=1, source_target_pairs={{1,2},{2,1},{3,4},{4,3},{5,6},{6,5},{9,10},{10,9},{11,12},{12,11},... | collective-permute-start | bytes 245768 | tf_op jit(solution)/shard_map/ppermute | solution.py:415
  64.0 2.2 %collective-permute-start.3 = (bf16[64,128]{1,0:T(8,128)(2,1)S(1)}, bf16[64,128]{1,0:T(8,128)(2,1)S(1)}, u32[]{:S(2)}, u32[]{:S(2)}) collective-permute-start(bf16[64,128]{1,0:T(8,128)(2,1)S(1)} %get-tuple-element.23.refs_7_), channel_id=1, source_target_pairs={{2,0},{3,1},{4,2},{5,3},{6,4},{7,5},{10,8},{11,9},{12,10},{13,11},... | collective-permute-start | bytes 49160 | tf_op jit(solution)/shard_map/ppermute | solution.py:408
  66.2 0.1 pad_add_fusion.1.refs_1_
  66.3 0.8 collective-permute-done.3.refs_8_
  67.1 0.0 collective-permute-done.1.refs_5_
  67.1 0.0 collective-permute-done.2.refs_6_
  67.1 0.0 copy-start.6
  67.1 2.7 %shard_map.98 = (f32[256,128]{1,0:T(8,128)S(1)}, f32[256,128]{1,0:T(8,128)S(1)}, bf16[320,128]{1,0:T(8,128)(2,1)S(1)}, bf16[64,128]{1,0:T(8,128)(2,1)S(1)}) custom-call(s32[4]{0:T(128)S(1)} %bitcast.29, s32[2]{0:T(128)S(1)} %pad_add_fusion.1.refs_1_, f32[256,128]{1,0:T(8,128)S(1)} %get-tuple-element.19.refs_2_, f32[256,128]{1,0:T(8,128)S(1)} %get-tuple-element.20.refs_3_, ...), custom_call_target="tpu_custom_call" | custom-call | tf_op jit(solution)/shard_map/pallas_call | solution.py:268
  69.8 2.7 %collective-permute-start.4 = (bf16[320,128]{1,0:T(8,128)(2,1)S(1)}, bf16[320,128]{1,0:T(8,128)(2,1)S(1)}, u32[]{:S(2)}, u32[]{:S(2)}) collective-permute-start(bf16[320,128]{1,0:T(8,128)(2,1)S(1)} %get-tuple-element.26), channel_id=1, source_target_pairs={{0,1},{1,0},{2,3},{3,2},{4,5},{5,4},{6,7},{7,6},{8,9},{9,8},{10,11... | collective-permute-start | bytes 245768 | tf_op jit(solution)/shard_map/ppermute | solution.py:415
  72.6 6.7 %collective-permute-start.5 = (bf16[320,128]{1,0:T(8,128)(2,1)S(1)}, bf16[320,128]{1,0:T(8,128)(2,1)S(1)}, u32[]{:S(2)}, u32[]{:S(2)}) collective-permute-start(bf16[320,128]{1,0:T(8,128)(2,1)S(1)} %get-tuple-element.26), channel_id=1, source_target_pairs={{1,2},{2,1},{3,4},{4,3},{5,6},{6,5},{9,10},{10,9},{11,12},{12,11},... | collective-permute-start | bytes 245768 | tf_op jit(solution)/shard_map/ppermute | solution.py:415
  79.2 1.3 %collective-permute-start.6 = (bf16[64,128]{1,0:T(8,128)(2,1)S(1)}, bf16[64,128]{1,0:T(8,128)(2,1)S(1)}, u32[]{:S(2)}, u32[]{:S(2)}) collective-permute-start(bf16[64,128]{1,0:T(8,128)(2,1)S(1)} %get-tuple-element.27.refs_6_), channel_id=1, source_target_pairs={{0,2},{1,3},{2,4},{3,5},{4,6},{5,7},{8,10},{9,11},{10,12},{11,13},... | collective-permute-start | bytes 49160 | tf_op jit(solution)/shard_map/ppermute | solution.py:408
  80.5 0.1 pad_add_fusion.refs_0_
  80.6 3.1 %collective-permute-done.6.refs_5_ = bf16[64,128]{1,0:T(8,128)(2,1)S(1)} collective-permute-done((bf16[64,128]{1,0:T(8,128)(2,1)S(1)}, bf16[64,128]{1,0:T(8,128)(2,1)S(1)}, u32[]{:S(2)}, u32[]{:S(2)}) %collective-permute-start.6) | collective-permute-done | bytes 16416 | tf_op jit(solution)/shard_map/ppermute | solution.py:408
  83.7 0.0 collective-permute-done.4.refs_3_
  83.7 0.0 collective-permute-done.5.refs_4_
  83.7 0.6 shard_map.99
  84.3 22.7 %all_to_all.20 = bf16[64,3,2,128]{3,2,1,0:T(2,128)(2,1)S(1)} all-to-all(bf16[64,3,2,128]{3,2,1,0:T(2,128)(2,1)S(1)} %bitcast.26), channel_id=1, replica_groups=mesh['view'=64,'strip'=8] {'view'}, dimensions={0} | all-to-all | bytes 196608 | tf_op jit(solution)/shard_map/all_to_all | solution.py:421
  107.0 2.1 %shard_map.100 = (bf16[256,128]{1,0:T(8,128)(2,1)S(1)}, f32[256,128]{1,0:T(8,128)}) custom-call(bf16[384,128]{1,0:T(8,128)(2,1)S(1)} %bitcast.23, bf16[64,2112]{1,0:T(8,128)(2,1)S(1)} %get-tuple-element.32.refs_1_, f32[256,128]{1,0:T(8,128)S(1)} %get-tuple-element.29.refs_2_), custom_call_target="tpu_custom_call" | custom-call | tf_op jit(solution)/shard_map/pallas_call | solution.py:387
  109.1 18.3 %all_to_all.21 = bf16[64,2,2,128]{3,2,1,0:T(2,128)(2,1)S(1)} all-to-all(bf16[64,2,2,128]{3,2,1,0:T(2,128)(2,1)S(1)} %bitcast.27), channel_id=1, replica_groups=mesh['view'=64,'strip'=8] {'view'}, dimensions={0} | all-to-all | bytes 131072 | tf_op jit(solution)/shard_map/all_to_all | solution.py:421
  127.5 0.0 copy-done.6
  127.5 0.7 fusion
  (1 shorter events, 0.0 us)
Async XLA Ops:
  0.6 31.9 %all-to-all-start = ((bf16[64,2,2,128]{3,2,1,0:T(2,128)(2,1)}), bf16[64,2,2,128]{3,2,1,0:T(2,128)(2,1)S(1)}, u32[]{:S(2)}, u32[]{:S(2)}) async-start(bf16[64,2,2,128]{3,2,1,0:T(2,128)(2,1)} %bitcast.30), calls=%async_computation | async-start | bytes 131072 | tf_op jit(solution)/shard_map/all_to_all | solution.py:421
  17.9 16.3 %collective-permute-start = (f32[2,128,128]{2,1,0:T(8,128)}, f32[2,128,128]{2,1,0:T(8,128)S(1)}, u32[]{:S(2)}, u32[]{:S(2)}) collective-permute-start(f32[2,128,128]{2,1,0:T(8,128)} %bitcast.19), channel_id=1, source_target_pairs={{1,0},{2,1},{3,2},{4,3},{5,4},{6,5},{7,6},{9,8},{10,9},{11,10},{12... | collective-permute-start | bytes 393224 | tf_op jit(solution)/shard_map/ppermute | solution.py:408
  24.0 16.8 %copy-start = (bf16[2,2,256,256]{3,2,1,0:T(8,128)(2,1)S(1)}, bf16[2,2,256,256]{3,2,1,0:T(8,128)(2,1)}, u32[]{:S(2)}) copy-start(bf16[2,2,256,256]{3,2,1,0:T(8,128)(2,1)} %constant.47.clone.tables.refs_11_) | copy-start | bytes 1572868
  24.0 16.8 %copy-start.1 = (f32[1,4,128,128]{3,2,1,0:T(8,128)S(1)}, f32[1,4,128,128]{3,2,1,0:T(8,128)}, u32[]{:S(2)}) copy-start(f32[1,4,128,128]{3,2,1,0:T(8,128)} %param.11) | copy-start | bytes 786436
  24.0 16.8 %copy-start.2 = (f32[1,2,128,128]{3,2,1,0:T(8,128)S(1)}, f32[1,2,128,128]{3,2,1,0:T(8,128)}, u32[]{:S(2)}) copy-start(f32[1,2,128,128]{3,2,1,0:T(8,128)} %param.9) | copy-start | bytes 393220
  24.0 16.8 %copy-start.3 = (f32[2,128,128]{2,1,0:T(8,128)S(1)}, f32[2,128,128]{2,1,0:T(8,128)}, u32[]{:S(2)}) copy-start(f32[2,128,128]{2,1,0:T(8,128)} %refs_10_.1) | copy-start | bytes 393220
  24.0 16.8 %copy-start.5 = (s32[1,4]{1,0:T(1,128)S(1)}, s32[1,4]{1,0:T(1,128)}, u32[]{:S(2)}) copy-start(s32[1,4]{1,0:T(1,128)} %param.12) | copy-start | bytes 52
  24.3 32.3 %copy-start.4 = (f32[1,2,128,128]{3,2,1,0:T(8,128)S(1)}, f32[1,2,128,128]{3,2,1,0:T(8,128)}, u32[]{:S(2)}) copy-start(f32[1,2,128,128]{3,2,1,0:T(8,128)} %param.10) | copy-start | bytes 393220
  34.2 22.4 %all-to-all-start.1 = ((bf16[64,3,2,128]{3,2,1,0:T(2,128)(2,1)}), bf16[64,3,2,128]{3,2,1,0:T(2,128)(2,1)S(1)}, u32[]{:S(2)}, u32[]{:S(2)}) async-start(bf16[64,3,2,128]{3,2,1,0:T(2,128)(2,1)} %bitcast.7), calls=%async_computation.1 | async-start | bytes 196608 | tf_op jit(solution)/shard_map/all_to_all | solution.py:421
  56.7 10.4 %collective-permute-start.1 = (bf16[320,128]{1,0:T(8,128)(2,1)S(1)}, bf16[320,128]{1,0:T(8,128)(2,1)S(1)}, u32[]{:S(2)}, u32[]{:S(2)}) collective-permute-start(bf16[320,128]{1,0:T(8,128)(2,1)S(1)} %get-tuple-element.21), channel_id=1, source_target_pairs={{0,1},{1,0},{2,3},{3,2},{4,5},{5,4},{6,7},{7,6},{8,9},{9,8},{10,11... | collective-permute-start | bytes 245768 | tf_op jit(solution)/shard_map/ppermute | solution.py:415
  59.1 8.0 %collective-permute-start.2 = (bf16[320,128]{1,0:T(8,128)(2,1)S(1)}, bf16[320,128]{1,0:T(8,128)(2,1)S(1)}, u32[]{:S(2)}, u32[]{:S(2)}) collective-permute-start(bf16[320,128]{1,0:T(8,128)(2,1)S(1)} %get-tuple-element.22), channel_id=1, source_target_pairs={{1,2},{2,1},{3,4},{4,3},{5,6},{6,5},{9,10},{10,9},{11,12},{12,11},... | collective-permute-start | bytes 245768 | tf_op jit(solution)/shard_map/ppermute | solution.py:415
  64.0 3.0 %collective-permute-start.3 = (bf16[64,128]{1,0:T(8,128)(2,1)S(1)}, bf16[64,128]{1,0:T(8,128)(2,1)S(1)}, u32[]{:S(2)}, u32[]{:S(2)}) collective-permute-start(bf16[64,128]{1,0:T(8,128)(2,1)S(1)} %get-tuple-element.23.refs_7_), channel_id=1, source_target_pairs={{2,0},{3,1},{4,2},{5,3},{6,4},{7,5},{10,8},{11,9},{12,10},{13,11},... | collective-permute-start | bytes 49160 | tf_op jit(solution)/shard_map/ppermute | solution.py:408
  67.1 60.4 %copy-start.6 = (bf16[1,2,128,128]{3,2,1,0:T(8,128)(2,1)S(1)}, bf16[1,2,128,128]{3,2,1,0:T(8,128)(2,1)}, u32[]{:S(2)}) copy-start(bf16[1,2,128,128]{3,2,1,0:T(8,128)(2,1)} %param.8) | copy-start | bytes 196612
  69.8 13.9 %collective-permute-start.4 = (bf16[320,128]{1,0:T(8,128)(2,1)S(1)}, bf16[320,128]{1,0:T(8,128)(2,1)S(1)}, u32[]{:S(2)}, u32[]{:S(2)}) collective-permute-start(bf16[320,128]{1,0:T(8,128)(2,1)S(1)} %get-tuple-element.26), channel_id=1, source_target_pairs={{0,1},{1,0},{2,3},{3,2},{4,5},{5,4},{6,7},{7,6},{8,9},{9,8},{10,11... | collective-permute-start | bytes 245768 | tf_op jit(solution)/shard_map/ppermute | solution.py:415
  72.6 11.2 %collective-permute-start.5 = (bf16[320,128]{1,0:T(8,128)(2,1)S(1)}, bf16[320,128]{1,0:T(8,128)(2,1)S(1)}, u32[]{:S(2)}, u32[]{:S(2)}) collective-permute-start(bf16[320,128]{1,0:T(8,128)(2,1)S(1)} %get-tuple-element.26), channel_id=1, source_target_pairs={{1,2},{2,1},{3,4},{4,3},{5,6},{6,5},{9,10},{10,9},{11,12},{12,11},... | collective-permute-start | bytes 245768 | tf_op jit(solution)/shard_map/ppermute | solution.py:415
  79.2 4.5 %collective-permute-start.6 = (bf16[64,128]{1,0:T(8,128)(2,1)S(1)}, bf16[64,128]{1,0:T(8,128)(2,1)S(1)}, u32[]{:S(2)}, u32[]{:S(2)}) collective-permute-start(bf16[64,128]{1,0:T(8,128)(2,1)S(1)} %get-tuple-element.27.refs_6_), channel_id=1, source_target_pairs={{0,2},{1,3},{2,4},{3,5},{4,6},{5,7},{8,10},{9,11},{10,12},{11,13},... | collective-permute-start | bytes 49160 | tf_op jit(solution)/shard_map/ppermute | solution.py:408
